TPU v7x, 32 devices: a whole 2x2x4 slice. The times are simulated.
32 devices in a mesh: dp: 8 (over y, x, core), space: 4 (over z).
Axes of the slice: x: 2, y: 2, z: 4, core: 2. Of those that a mesh axis runs over, the one named last changes fastest.
Arguments:
- scenes: bfloat16 [16, 56, 8, 768], P('dp', 'space'), may hold values from -8 to 8
- kernel: bfloat16 [7, 7, 768], replicated, may hold values from -0.875 to 0.875
- weight_in: bfloat16 [768, 1536], replicated, may hold values from -0.21875 to 0.21875
- weight_out: bfloat16 [1536, 768], replicated, may hold values from -0.15625 to 0.15625
- captions: bfloat16 [16, 768], P('dp'), may hold values from -0.21972656 to 0.21972656
- positives: int32 [16], P('dp'), may hold values from 0 to 15, each once
Outputs:
- loss: float32 [], replicated
- text_grad: float32 [16, 768], P('dp')
- kernel_grad: float32 [7, 7, 768], replicated
Inputs may be any that keep to these rules, and one draw needn't show every extreme that they name: `positives`: every caption index appears exactly once.
All inputs are finite; a program needn't handle non-finite values.
Results may differ from a plain program's by a relative error of at most 0.0054.
Values may be sent and summed in bfloat16 or wider, within the bound.
No kernel may reach another device: no remote copies, remote signals or barrier semaphores. Data moves between devices by JAX's collectives and lax.ppermute only.
A program may use at most 64 MiB of HBM per device.

v0:
```python
import jax
import jax.numpy as jnp
from jax import lax
from jax.sharding import PartitionSpec as P

EPS = 1e-06
LOGIT_SCALE = 10.0
LOGIT_BIAS = -1.0
GELU_C = 0.7978845608028654


def with_halo(array, sides, width):
    for axis, dim in sides:
        count, length = (lax.axis_size(axis), array.shape[dim])
        up = [(i, (i + 1) % count) for i in range(count - 1)]
        down = [(j, i) for i, j in up]
        last = lax.slice_in_dim(array, length - width, length, axis=dim)
        first = lax.slice_in_dim(array, 0, width, axis=dim)
        before = lax.ppermute(last, axis, up)
        after = lax.ppermute(first, axis, down)
        array = jnp.concatenate([before, array, after], axis=dim)
    return array


def gelu_tanh(values):
    return 0.5 * values * (1.0 + jnp.tanh(GELU_C * (values + 0.044715 * values * values * values)))


def gelu_slope(values):
    tangent = jnp.tanh(GELU_C * (values + 0.044715 * values * values * values))
    return 0.5 * (1.0 + tangent) + 0.5 * values * (1.0 - tangent * tangent) * GELU_C * (
        1.0 + 3.0 * 0.044715 * values * values
    )


def depthwise(padded, kernel, tile_rows, tile_cols):
    total = jnp.zeros(padded.shape[:-3] + (tile_rows, tile_cols, padded.shape[-1]), jnp.float32)
    for row_shift in range(7):
        for col_shift in range(7):
            total = (
                total
                + kernel[row_shift, col_shift].astype(jnp.float32)
                * padded[
                    ..., row_shift : row_shift + tile_rows, col_shift : col_shift + tile_cols, :
                ]
            )
    return total


def kernel_terms(padded, conv_grad, tile_rows, tile_cols):
    summed_axes = tuple(range(conv_grad.ndim - 1))
    listed = []
    for row_shift in range(7):
        for col_shift in range(7):
            window = padded[
                ..., row_shift : row_shift + tile_rows, col_shift : col_shift + tile_cols, :
            ]
            listed.append(jnp.sum(window * conv_grad, axis=summed_axes))
    return jnp.stack(listed).reshape(7, 7, conv_grad.shape[-1])


def normalize_rows(conv_out):
    center = conv_out - jnp.mean(conv_out, axis=-1, keepdims=True)
    inv_scale = lax.rsqrt(jnp.mean(center * center, axis=-1, keepdims=True) + EPS)
    return (center * inv_scale, inv_scale)


def unit_rows(values):
    norms = jnp.sqrt(jnp.sum(values * values, axis=-1, keepdims=True) + EPS)
    return (values / norms, norms)


def pair_weights(labels, logits):
    return (-labels * jax.nn.sigmoid(-labels * logits)).astype(jnp.bfloat16)


def per_device(scenes, kernel, weight_in, weight_out, captions, positives):
    images, tile_rows, tile_cols, channels = scenes.shape
    hidden_units = weight_in.shape[1]
    space_count = lax.axis_size("space")
    pixels = tile_rows * space_count * tile_cols
    row_padded = with_halo(scenes, (("space", 1),), 3)
    padded = jnp.pad(row_padded.astype(jnp.float32), ((0, 0), (0, 0), (3, 3), (0, 0)))
    conv_out = depthwise(padded, kernel, tile_rows, tile_cols)
    normed, inv_scale = normalize_rows(conv_out)
    flat_rows = normed.reshape(-1, channels).astype(jnp.bfloat16)
    hidden = jnp.dot(flat_rows, weight_in, preferred_element_type=jnp.float32)
    activated = gelu_tanh(hidden).astype(jnp.bfloat16)
    mixed_out = jnp.dot(activated, weight_out, preferred_element_type=jnp.float32)
    block_out = scenes.reshape(-1, channels).astype(jnp.float32) + mixed_out
    tile_sums = jnp.sum(block_out.reshape(images, -1, channels), axis=1)
    pooled = lax.psum(tile_sums, "space") / pixels
    image_unit, pooled_norm = unit_rows(pooled)
    text_unit, text_norm = unit_rows(captions.astype(jnp.float32))
    image_cast = image_unit.astype(jnp.bfloat16)
    gathered = lax.all_gather(captions, "dp", axis=0, tiled=True)
    all_unit, all_norm = unit_rows(gathered.astype(jnp.float32))
    all_cast = all_unit.astype(jnp.bfloat16)
    total_rows = gathered.shape[0]
    logits = (
        LOGIT_SCALE * jnp.dot(image_cast, all_cast.T, preferred_element_type=jnp.float32)
        + LOGIT_BIAS
    )
    labels = jnp.where(
        positives[:, None] == jnp.arange(total_rows, dtype=jnp.int32)[None, :], 1.0, -1.0
    ).astype(jnp.float32)
    loss_part = jnp.sum(jax.nn.softplus(-labels * logits))
    pair_grad = pair_weights(labels, logits)
    image_side = LOGIT_SCALE * jnp.dot(pair_grad, all_cast, preferred_element_type=jnp.float32)
    caption_side = lax.psum_scatter(
        LOGIT_SCALE * jnp.dot(pair_grad.T, image_cast, preferred_element_type=jnp.float32),
        "dp",
        scatter_dimension=0,
        tiled=True,
    )
    text_grad = (
        caption_side - text_unit * jnp.sum(text_unit * caption_side, axis=-1, keepdims=True)
    ) / text_norm
    pooled_grad = (
        image_side - image_unit * jnp.sum(image_unit * image_side, axis=-1, keepdims=True)
    ) / pooled_norm
    slope = (pooled_grad / pixels).astype(jnp.bfloat16)
    act_grad = jnp.dot(slope, weight_out.T, preferred_element_type=jnp.float32)
    hidden_grad = (
        act_grad[:, None, :] * gelu_slope(hidden.reshape(images, -1, hidden_units))
    ).astype(jnp.bfloat16)
    normed_grad = jnp.dot(
        hidden_grad.reshape(-1, hidden_units), weight_in.T, preferred_element_type=jnp.float32
    )
    normed_grad = normed_grad.reshape(images, tile_rows, tile_cols, channels)
    conv_grad = inv_scale * (
        normed_grad
        - jnp.mean(normed_grad, axis=-1, keepdims=True)
        - normed * jnp.mean(normed_grad * normed, axis=-1, keepdims=True)
    )
    kernel_part = kernel_terms(padded, conv_grad, tile_rows, tile_cols)
    loss_share = jnp.where(lax.axis_index("space") == 0, loss_part, jnp.zeros((), jnp.float32))
    kernel_grad, loss_total = lax.psum((kernel_part, loss_share), ("dp", "space"))
    loss = loss_total / (images * lax.axis_size("dp"))
    return (loss, text_grad, kernel_grad)


def solution(mesh):
    return jax.shard_map(
        per_device,
        mesh=mesh,
        in_specs=(P("dp", "space", None, None), P(), P(), P(), P("dp", None), P("dp")),
        out_specs=(P(), P("dp", None), P()),
        check_vma=False,
    )
```

profile of v0, /device:TPU:0, one launch (start us, length us, event | category | flops | bytes accessed | tf_op | source)
XLA Modules:
  0.0 199.3 jit_solution(8548832725383272184)
XLA Ops:
  7.2 0.0 copy-start
  7.2 0.0 all-reduce.4.cloned.1.call-start
  7.2 1.1 fusion.35
  8.3 4.9 %collective-permute-start = (bf16[2,3,8,768]{3,2,1,0:T(8,128)(2,1)S(1)}, bf16[2,3,8,768]{3,2,1,0:T(8,128)(2,1)S(1)}, u32[]{:S(2)}, u32[]{:S(2)}) collective-permute-start(bf16[2,3,8,768]{3,2,1,0:T(8,128)(2,1)S(1)} %get-tuple-element.108), channel_id=1, source_target_pairs={{0,1},{1,2},{2,3},{4,5},{5,6},{6,7},{8,9},{9,10},{10,11},{12,13},{... | collective-permute-start | bytes 221192 | tf_op jit(solution)/shard_map/ppermute | solution.py:19
  13.3 1.3 collective-permute-start.1
  14.6 1.9 convert_reduce_fusion.48
  16.5 2.0 %convert_reduce_fusion.47 = (f32[768]{0:T(1024)}, f32[768]{0:T(1024)}, f32[768]{0:T(1024)}, f32[768]{0:T(1024)}, f32[768]{0:T(1024)}, /*index=5*/f32[768]{0:T(10...) fusion(bf16[7,7,768]{2,1,0:T(8,128)(2,1)} %param.7), kind=kLoop, calls=%fused_computation.186 | loop fusion | flops 14592 | bytes 87552 | tf_op jit(solution)/shard_map/convert_element_type | solution.py:42
  18.5 0.8 fusion.16
  19.3 9.2 %all-gather = bf16[8,2,768]{2,1,0:T(2,128)(2,1)S(1)} all-gather(bf16[1,2,768]{2,1,0:T(2,128)(2,1)} %bitcast.27), channel_id=1, replica_groups=mesh['dp'=8,'space'=4] {'dp'}, dimensions={0}, use_global_device_ids=true | all-gather | bytes 27648 | tf_op jit(solution)/shard_map/all_gather | solution.py:96
  28.5 0.1 multiply_reduce_fusion.51
  28.6 0.1 divide_convert_fusion
  28.7 0.6 add_sqrt_fusion
  29.3 1.2 dynamic-slice
  31.2 1.0 convert_reduce_fusion.46
  32.2 0.0 collective-permute-done
  32.2 0.0 collective-permute-done.1
  32.2 1.1 maximum_convert_fusion
  33.3 6.4 %fusion.34 = (f32[2,14,8]{2,1,0:T(8,128)S(1)}, f32[2,14,8,768]{3,2,1,0:T(8,128)S(1)}) fusion(f32[768]{0:T(1024)S(1)} %get-tuple-element.101, f32[768]{0:T(1024)S(1)} %get-tuple-element.102, f32[768]{0:T(1024)S(1)} %get-tuple-element.55, f32[2,20,8,768]{3,2,1,0:T(8,128)S(1)} %maximum_convert_fusion, f32[768]{0:T(1024)S(1)} %get-tuple-element.56, ...), kind=kLoop, calls=%fused_computation.205 | loop fusion | flops 16858912 | bytes 6660992 | tf_op jit(solution)/shard_map/reduce_sum | solution.py:63
  39.7 0.0 copy-start.1
  39.8 0.2 multiply_reduce_fusion.50
  40.0 0.1 fusion.15
  40.1 0.0 copy-done
  40.1 0.0 copy-start.5
  40.2 0.0 copy-start.6
  40.2 0.7 fusion.36
  40.9 0.0 copy-done.1
  40.9 0.0 copy-start.3
  40.9 0.9 copy-done.5
  41.8 0.2 copy-done.6
  42.0 0.0 copy-start.9
  42.0 1.8 convolution_add_fusion
  43.8 0.0 copy-done.3
  43.8 1.2 reduce_sum.542
  45.0 13.1 %psum.21 = f32[2,768]{1,0:T(2,128)S(1)} all-reduce(f32[2,768]{1,0:T(2,128)S(1)} %reduce_sum.542), channel_id=1, replica_groups=mesh['dp'=8,'space'=4] {'space'}, use_global_device_ids=true, to_apply=%region_3.4 | all-reduce | flops 1536 | bytes 12288 | tf_op jit(solution)/shard_map/psum | solution.py:92
  58.1 0.0 copy-start.4
  58.1 0.1 multiply_reduce_fusion.54
  58.3 0.0 copy-done.9
  58.3 0.8 fusion.24
  59.1 0.3 multiply_reduce_fusion.52
  59.4 0.0 copy-start.2
  59.4 2.4 %fusion.17 = f32[2,1536]{1,0:T(2,128)S(1)} fusion(bf16[1536,768]{1,0:T(8,128)(2,1)} %param.9, f32[2,768]{1,0:T(2,128)S(1)} %get-tuple-element.113, f32[2]{0:T(128)S(1)} %get-tuple-element.112, f32[2]{0:T(128)S(1)} %add_sqrt_fusion.2, f32[2,768]{1,0:T(2,128)S(1)} %psum.21), kind=kOutput, calls=%fused_computation.136 | convolution fusion | flops 4729344 | bytes 2383888 | tf_op jit(solution)/shard_map/dot_general | solution.py:123
  61.8 0.0 copy-done.4
  61.8 0.9 fusion.8
  62.7 0.0 copy-done.2
  62.7 1.0 fusion.33
  63.8 2.0 multiply_reduce_fusion
  65.7 1.7 multiply_reduce_fusion.18
  67.4 0.0 copy-start.7
  67.4 0.0 copy-start.8
  67.4 1.2 multiply_reduce_fusion.36
  68.6 0.3 convolution_multiply_fusion
  69.5 0.3 stack.199
  69.8 0.7 reshape.408
  70.5 0.0 all-reduce.4.cloned.1.call-update
  70.5 22.8 %all-reduce.1 = f32[16,768]{1,0:T(8,128)S(1)} all-reduce(f32[16,768]{1,0:T(8,128)S(1)} %convolution_multiply_fusion), channel_id=2, replica_groups=mesh['dp'=8,'space'=4] {'dp'}, use_global_device_ids=true, to_apply=%region_8.9.clone | all-reduce | flops 12288 | bytes 98304
  93.9 0.0 copy-done.7
  93.9 0.0 copy-done.8
  93.9 0.2 multiply_reduce_fusion.53
  94.1 0.7 subtract_divide_fusion
  94.8 36.9 %psum.22 = f32[]{:T(128)} all-reduce(f32[]{:T(128)S(6)} %select_n.14), channel_id=1, replica_groups=mesh['dp'=8,'space'=4] {'dp','space'}, use_global_device_ids=true, to_apply=%region_7.8 | all-reduce | flops 1 | bytes 8 | tf_op jit(solution)/shard_map/psum | solution.py:138
  132.3 57.4 %all-reduce.4.cloned.1.call-done = f32[7,7,768]{2,1,0:T(8,128)} async-done(((f32[7,7,768]{2,1,0:T(8,128)}), f32[7,7,768]{2,1,0:T(8,128)}) %all-reduce.4.cloned.1.call-update) | async-done | bytes 150544 | tf_op jit(solution)/shard_map/psum | solution.py:138
  189.7 1.6 copy.11
  (55 shorter events, 0.3 us)
Async XLA Ops:
  7.2 33.0 %copy-start = (bf16[768,1536]{1,0:T(8,128)(2,1)S(1)}, bf16[768,1536]{1,0:T(8,128)(2,1)}, u32[]{:S(2)}) copy-start(bf16[768,1536]{1,0:T(8,128)(2,1)} %param.8) | copy-start | bytes 7077892
  7.2 182.5 %all-reduce.4.cloned.1.call-start = ((), (), s32[]{:S(2)}) async-start(), calls=%async_computation | async-start | bytes 344064 | tf_op jit(solution)/shard_map/psum | solution.py:138
  8.3 23.9 %collective-permute-start = (bf16[2,3,8,768]{3,2,1,0:T(8,128)(2,1)S(1)}, bf16[2,3,8,768]{3,2,1,0:T(8,128)(2,1)S(1)}, u32[]{:S(2)}, u32[]{:S(2)}) collective-permute-start(bf16[2,3,8,768]{3,2,1,0:T(8,128)(2,1)S(1)} %get-tuple-element.108), channel_id=1, source_target_pairs={{0,1},{1,2},{2,3},{4,5},{5,6},{6,7},{8,9},{9,10},{10,11},{12,13},{... | collective-permute-start | bytes 221192 | tf_op jit(solution)/shard_map/ppermute | solution.py:19
  13.3 19.0 %collective-permute-start.1 = (bf16[2,3,8,768]{3,2,1,0:T(8,128)(2,1)S(1)}, bf16[2,3,8,768]{3,2,1,0:T(8,128)(2,1)S(1)}, u32[]{:S(2)}, u32[]{:S(2)}) collective-permute-start(bf16[2,3,8,768]{3,2,1,0:T(8,128)(2,1)S(1)} %get-tuple-element.109), channel_id=1, source_target_pairs={{1,0},{2,1},{3,2},{5,4},{6,5},{7,6},{9,8},{10,9},{11,10},{13,12},{... | collective-permute-start | bytes 221192 | tf_op jit(solution)/shard_map/ppermute | solution.py:20
  39.7 1.1 copy-start.1
  40.1 1.7 copy-start.5
  40.2 1.8 copy-start.6
  40.9 2.9 %copy-start.3 = (f32[224,1536]{1,0:T(8,128)}, f32[224,1536]{1,0:T(8,128)S(1)}, u32[]{:S(2)}) copy-start(f32[224,1536]{1,0:T(8,128)S(1)} %fusion.36) | copy-start | bytes 4128772
  42.0 16.3 %copy-start.9 = (s32[2]{0:T(128)S(1)}, s32[2]{0:T(128)}, u32[]{:S(2)}) copy-start(s32[2]{0:T(128)} %param.11) | copy-start | bytes 28
  58.1 3.7 %copy-start.4 = (f32[224,1536]{1,0:T(8,128)S(1)}, f32[224,1536]{1,0:T(8,128)}, u32[]{:S(2)}) copy-start(f32[224,1536]{1,0:T(8,128)} %copy-done.3) | copy-start | bytes 4128772
  59.4 3.4 %copy-start.2 = (f32[2,14,8,768]{3,2,1,0:T(8,128)S(1)}, f32[2,14,8,768]{3,2,1,0:T(8,128)}, u32[]{:S(2)}) copy-start(f32[2,14,8,768]{3,2,1,0:T(8,128)} %copy-done.1) | copy-start | bytes 2064388
  67.4 26.5 %copy-start.7 = (bf16[2,768]{1,0:T(2,128)(2,1)S(1)}, bf16[2,768]{1,0:T(2,128)(2,1)}, u32[]{:S(2)}) copy-start(bf16[2,768]{1,0:T(2,128)(2,1)} %param.10) | copy-start | bytes 9220
  67.4 26.5 %copy-start.8 = (f32[2]{0:T(128)S(1)}, f32[2]{0:T(128)}, u32[]{:S(2)}) copy-start(f32[2]{0:T(128)} %add_sqrt_fusion) | copy-start | bytes 28
Sparse Core Ops, SparseCore 0:
  70.6 119.0 all-reduce.3
where the time goes:
time: 201 us; the launch traced here: 199 us
  blocking collectives  81.9 us (41%)
  waiting for transfers between devices  57.4 us (29%)
  other arithmetic  22.3 us (11%)
  between operations  17.8 us (9%)
  matrix products  7.31 us (4%)
  local copies, waits for them, and re-layouts  6.3 us (3%)
  starting transfers between devices  6.26 us (3%)
    psum x1, waiting for transfers between devices, per_device(): lax.psum((kernel_part, loss_share), ('dp', 'space'))  57.4 us
    psum x1, blocking collectives, per_device(): lax.psum((kernel_part, loss_share), ('dp', 'space'))  36.9 us
    unnamed x1, blocking collectives  22.8 us
    psum x1, blocking collectives, per_device(): pooled = lax.psum(tile_sums, 'space') / pixels  13.1 us
    all_gather x1, blocking collectives, per_device(): gathered = lax.all_gather(captions, 'dp', axis=0, tiled=True)  9.18 us
    reduce_sum x1, other arithmetic, normalize_rows(): center = conv_out - jnp.mean(conv_out, axis=-1, keepdims=True)  6.42 us
    convert_element_type x3, other arithmetic, depthwise(): kernel[row_shift, col_shift].astype(jnp.float32)  4.97 us
    ppermute x1, starting transfers between devices, with_halo(): before = lax.ppermute(last, axis, up)  4.93 us
  transfers between devices with their start and end apart: 3, of which 1 were waited for; matrix products, arithmetic and copies ran while one was open for 4% of the time, Pallas kernels for 0%

commit v1 on v0

v1 whole, which is shorter than its diff:
```python
import functools

import jax
import jax.numpy as jnp
from jax import lax
from jax.experimental import pallas as pl
from jax.experimental.pallas import tpu as pltpu
from jax.sharding import PartitionSpec as P

EPS = 1e-06
LOGIT_SCALE = 10.0
LOGIT_BIAS = -1.0
GELU_C = 0.7978845608028654
TAPS = 7
SIDE = 3
LANES = 128
BF = jnp.bfloat16
F32 = jnp.float32


def in_vmem(array):
    return pltpu.with_memory_space_constraint(array, pltpu.VMEM)


def vmem_out(shape, dtype):
    return pltpu.VMEM(shape, dtype)


def call(body, outs, args, scratch=(), smem=(), limit=40, flops=0):
    specs = [
        pl.BlockSpec(memory_space=pltpu.SMEM if k in smem else pltpu.VMEM)
        for k in range(len(args))
    ]
    args = [a if k in smem else in_vmem(a) for k, a in enumerate(args)]
    return pl.pallas_call(
        body,
        out_shape=[vmem_out(shape, dtype) for shape, dtype in outs],
        in_specs=specs,
        out_specs=[pl.BlockSpec(memory_space=pltpu.VMEM) for _ in outs],
        scratch_shapes=list(scratch),
        compiler_params=pltpu.CompilerParams(vmem_limit_bytes=limit * 1024 * 1024),
        cost_estimate=pl.CostEstimate(flops=flops, bytes_accessed=0, transcendentals=0),
    )(*args)


def column_masks(cols, lanes=LANES):
    at = lax.broadcasted_iota(jnp.int32, (cols, lanes), 0)
    return [
        (at - (j - SIDE) >= 0) & (at - (j - SIDE) < cols) for j in range(TAPS)
    ]


def tile_at(t):
    return pl.ds(pl.multiple_of(t * LANES, LANES), LANES)


def conv_body(x_ref, k_ref, part_ref, kw_ref):
    images, rows, cols, channels = x_ref.shape
    masks = column_masks(cols, channels)
    for i in range(TAPS):
        taps = k_ref[i].astype(F32)
        for j in range(TAPS):
            spread = jnp.broadcast_to(taps[j : j + 1], (cols, channels))
            kw_ref[i * TAPS + j] = jnp.where(masks[j], spread, 0.0)

    def tile(t, carry):
        at = tile_at(t)
        for b in range(images):
            xs = [x_ref[b, r, :, at].astype(F32) for r in range(rows)]
            outs = [None] * rows
            for j in range(TAPS):
                ws = [kw_ref[i * TAPS + j, :, at] for i in range(TAPS)]
                for r in range(rows):
                    total = None
                    for i in range(TAPS):
                        if 0 <= r + i - SIDE < rows:
                            term = ws[i] * xs[r + i - SIDE]
                            total = term if total is None else total + term
                    if j != SIDE:
                        total = pltpu.roll(total, (SIDE - j) % cols, 0)
                    outs[r] = total if outs[r] is None else outs[r] + total
            for r in range(rows):
                part_ref[b, r, :, at] = outs[r]
        return carry

    lax.fori_loop(0, channels // LANES, tile, 0)


def gelu_tanh(values):
    return 0.5 * values * (1.0 + jnp.tanh(GELU_C * (values + 0.044715 * values * values * values)))


def gelu_slope(values):
    tangent = jnp.tanh(GELU_C * (values + 0.044715 * values * values * values))
    return 0.5 * (1.0 + tangent) + 0.5 * values * (1.0 - tangent * tangent) * GELU_C * (
        1.0 + 3.0 * 0.044715 * values * values
    )


def three_terms(value):
    high = value.astype(BF).astype(F32)
    rest = value - high
    mid = rest.astype(BF).astype(F32)
    return high, mid, rest - mid


def forward_body(
    part_ref, before_ref, after_ref, kw_ref, x_ref, win_ref, wout_ref,
    sums_ref, normed_ref, inv_ref, hid_ref, conv_ref, cast_ref,
):
    images, rows, cols, channels = x_ref.shape
    hidden_units = win_ref.shape[1]
    pixels = rows * cols

    def tile(t, carry):
        at = tile_at(t)
        for b in range(images):
            heads = [before_ref[b, q, :, at].astype(F32) for q in range(SIDE)]
            tails = [after_ref[b, q, :, at].astype(F32) for q in range(SIDE)]
            outs = [part_ref[b, r, :, at] for r in range(rows)]
            for j in range(TAPS):
                ws = [kw_ref[i * TAPS + j, :, at] for i in range(TAPS)]
                for r in list(range(SIDE)) + list(range(rows - SIDE, rows)):
                    total = None
                    for i in range(TAPS):
                        q = r + i
                        if q < SIDE:
                            term = ws[i] * heads[q]
                        elif q >= rows + SIDE:
                            term = ws[i] * tails[q - rows - SIDE]
                        else:
                            continue
                        total = term if total is None else total + term
                    if j != SIDE:
                        total = pltpu.roll(total, (SIDE - j) % cols, 0)
                    outs[r] = outs[r] + total
            for r in range(rows):
                conv_ref[pl.ds((b * rows + r) * cols, cols), at] = outs[r]
        return carry

    lax.fori_loop(0, channels // LANES, tile, 0)

    for start in range(0, images * pixels, 32):
        some = pl.ds(start, 32)
        conv_out = conv_ref[some, :]
        center = conv_out - jnp.mean(conv_out, axis=-1, keepdims=True)
        inv = lax.rsqrt(jnp.mean(center * center, axis=-1, keepdims=True) + EPS)
        normed = center * inv
        normed_ref[some, :] = normed
        inv_ref[some, :] = jnp.broadcast_to(inv, (32, LANES))
        cast_ref[some, :] = normed.astype(BF)

    width = 256
    mixed = jnp.zeros((8, channels), F32)
    for start in range(0, hidden_units, width):
        some = pl.ds(start, width)
        hidden = jnp.dot(cast_ref[...], win_ref[:, some], preferred_element_type=F32)
        hid_ref[:, some] = hidden
        activated = gelu_tanh(hidden).astype(BF).astype(F32)
        listed = []
        for b in range(images):
            total = jnp.sum(activated[b * pixels : (b + 1) * pixels], axis=0, keepdims=True)
            listed.extend(three_terms(total))
        listed.append(jnp.zeros((8 - 3 * images, width), F32))
        terms = jnp.concatenate(listed, axis=0).astype(BF)
        mixed = mixed + jnp.dot(terms, wout_ref[some, :], preferred_element_type=F32)
    for b in range(images):
        own = x_ref[b, 0].astype(F32)
        for r in range(1, rows):
            own = own + x_ref[b, r].astype(F32)
        sums_ref[b : b + 1, :] = jnp.sum(own, axis=0, keepdims=True) + jnp.sum(
            mixed[3 * b : 3 * b + 3], axis=0, keepdims=True
        )


def slope_body(hid_ref, slope_ref):
    for start in range(0, hid_ref.shape[1], 256):
        some = pl.ds(start, 256)
        slope_ref[:, some] = gelu_slope(hid_ref[:, some])


def unit_rows(values):
    norms = jnp.sqrt(jnp.sum(values * values, axis=-1, keepdims=True) + EPS)
    return (values / norms, norms)


def kernel_sums(grad_ref, x_ref, before_ref, after_ref, list_ref, half):
    images, rows, cols, channels = x_ref.shape
    masks = column_masks(cols)
    tiles = channels // LANES // 2

    def tile(t, carry):
        at = tile_at(half * tiles + t)
        for j in range(TAPS):
            sums = [None] * TAPS
            for b in range(images):
                grads = []
                for r in range(rows):
                    grad = grad_ref[pl.ds((b * rows + r) * cols, cols), at]
                    grads.append(grad if j == SIDE else pltpu.roll(grad, (j - SIDE) % cols, 0))
                for q in range(rows + 2 * SIDE):
                    if q < SIDE:
                        here = before_ref[b, q, :, at]
                    elif q < rows + SIDE:
                        here = x_ref[b, q - SIDE, :, at]
                    else:
                        here = after_ref[b, q - rows - SIDE, :, at]
                    here = here.astype(F32)
                    for i in range(TAPS):
                        if 0 <= q - i < rows:
                            term = here * grads[q - i]
                            sums[i] = term if sums[i] is None else sums[i] + term
            for i in range(TAPS):
                kept = jnp.where(masks[j], sums[i], 0.0)
                list_ref[pl.ds(t * TAPS * TAPS + i * TAPS + j, 1), :] = jnp.sum(
                    kept, axis=0, keepdims=True
                )
        return carry

    list_ref[...] = jnp.zeros_like(list_ref)
    lax.fori_loop(0, tiles, tile, 0)


def backward_body(
    scene_pixels, total_ref, caps_ref, pos_ref, slope_ref, normed_ref, inv_ref, win_ref, wout_ref,
    x_ref, before_ref, after_ref,
    grad_ref, pay_ref, list_ref, hg_ref, row_ref,
):
    images, rows, cols, channels = x_ref.shape
    pixels = rows * cols
    count = caps_ref.shape[0]
    pooled = total_ref[...] / scene_pixels
    image_unit, pooled_norm = unit_rows(pooled)
    image_cast = image_unit.astype(BF)
    text_unit, _ = unit_rows(caps_ref[...].astype(F32))
    text_cast = text_unit.astype(BF)
    logits = (
        LOGIT_SCALE
        * lax.dot_general(
            image_cast, text_cast, (((1,), (1,)), ((), ())), preferred_element_type=F32
        )
        + LOGIT_BIAS
    )
    row_at = lax.broadcasted_iota(jnp.int32, (images, count), 0)
    positive = jnp.zeros((images, count), jnp.int32)
    for b in range(images):
        positive = jnp.where(row_at == b, pos_ref[b], positive)
    labels = jnp.where(
        positive == lax.broadcasted_iota(jnp.int32, (images, count), 1), 1.0, -1.0
    ).astype(F32)
    margin = -labels * logits
    losses = jnp.maximum(margin, 0.0) + jnp.log(1.0 + jnp.exp(-jnp.abs(margin)))
    loss_part = jnp.sum(jnp.sum(losses, axis=1, keepdims=True), axis=0, keepdims=True)
    pair_grad = (-labels / (1.0 + jnp.exp(-margin))).astype(BF)
    image_side = LOGIT_SCALE * jnp.dot(pair_grad, text_cast, preferred_element_type=F32)
    pooled_grad = (
        image_side - image_unit * jnp.sum(image_unit * image_side, axis=-1, keepdims=True)
    ) / pooled_norm
    slope = (pooled_grad / scene_pixels).astype(BF)
    act_grad = lax.dot_general(
        slope, wout_ref[...], (((1,), (1,)), ((), ())), preferred_element_type=F32
    )
    for b in range(images):
        some = pl.ds(b * pixels, pixels)
        hg_ref[some, :] = (act_grad[b : b + 1] * slope_ref[some, :]).astype(BF)
    normed_grad = lax.dot_general(
        hg_ref[...], win_ref[...], (((1,), (1,)), ((), ())), preferred_element_type=F32
    )
    normed = normed_ref[...]
    grad_ref[...] = inv_ref[:, 0:1] * (
        normed_grad
        - jnp.mean(normed_grad, axis=-1, keepdims=True)
        - normed * jnp.mean(normed_grad * normed, axis=-1, keepdims=True)
    )
    half = 1 - lax.rem(lax.axis_index("dp"), 2)
    kernel_sums(grad_ref, x_ref, before_ref, after_ref, list_ref, half)
    listed = list_ref.shape[0]
    pay_ref[0:listed, :] = list_ref[...].astype(BF)

    row_ref[...] = jnp.zeros_like(row_ref)
    chunks = channels // LANES
    high, mid, low = three_terms(loss_part)
    lane = lax.broadcasted_iota(jnp.int32, (1, LANES), 1)
    for b in range(images):
        for c in range(chunks):
            row_ref[b * (chunks + 1) + c : b * (chunks + 1) + c + 1, :] = image_cast[
                b : b + 1, c * LANES : (c + 1) * LANES
            ].astype(F32)
        at = b * (chunks + 1) + chunks
        row_ref[at : at + 1, 0:count] = pair_grad[b : b + 1, :].astype(F32)
        if b == 0:
            known = row_ref[at : at + 1, :]
            known = jnp.where(lane == LANES - 3, high, known)
            known = jnp.where(lane == LANES - 2, mid, known)
            known = jnp.where(lane == LANES - 1, low, known)
            row_ref[at : at + 1, :] = known
    pay_ref[listed:, :] = row_ref[...].astype(BF)


def own_half_body(grad_ref, x_ref, before_ref, after_ref, list_ref):
    half = lax.rem(lax.axis_index("dp"), 2)
    kernel_sums(grad_ref, x_ref, before_ref, after_ref, list_ref, half)


def text_body(rows_ref, caps_ref, text_ref, loss_ref, wide_ref):
    images, channels = caps_ref.shape
    chunks = channels // LANES
    stride = wide_ref.shape[0] // lax.axis_size("dp")
    groups = lax.axis_size("dp")
    wide_ref[...] = rows_ref[...].astype(F32)
    lane = lax.broadcasted_iota(jnp.int32, (groups, LANES), 1)
    first = lax.axis_index("dp") * images
    caption_side = [[jnp.zeros((1, LANES), F32) for _ in range(chunks)] for _ in range(images)]
    loss = jnp.zeros((1, 1), F32)
    for b in range(images):
        base = b * (chunks + 1)
        pairs = wide_ref[pl.ds(base + chunks, groups, stride=stride), :]
        if b == 0:
            terms = jnp.where(lane >= LANES - 3, pairs, 0.0)
            loss = jnp.sum(jnp.sum(terms, axis=1, keepdims=True), axis=0, keepdims=True)
        weights = [
            jnp.sum(jnp.where(lane == first + k, pairs, 0.0), axis=1, keepdims=True)
            for k in range(images)
        ]
        for c in range(chunks):
            unit = wide_ref[pl.ds(base + c, groups, stride=stride), :]
            for k in range(images):
                caption_side[k][c] = caption_side[k][c] + jnp.sum(
                    weights[k] * unit, axis=0, keepdims=True
                )
    loss_ref[...] = loss / (groups * images)
    text_unit, text_norm = unit_rows(caps_ref[...].astype(F32))
    for k in range(images):
        side = LOGIT_SCALE * jnp.concatenate(caption_side[k], axis=1)
        unit = text_unit[k : k + 1]
        text_ref[k : k + 1, :] = (
            side - unit * jnp.sum(unit * side, axis=-1, keepdims=True)
        ) / text_norm[k : k + 1]


def merge_body(own_ref, other_ref, out_ref, wide_ref):
    tiles = out_ref.shape[2] // LANES // 2
    half = lax.rem(lax.axis_index("dp"), 2)
    for source, side in ((own_ref, half), (other_ref, 1 - half)):
        wide_ref[...] = source[...].astype(F32)
        for t in range(tiles):
            at = tile_at(side * tiles + t)
            for i in range(TAPS):
                out_ref[i, :, at] = wide_ref[pl.ds((t * TAPS + i) * TAPS, TAPS), :]


def flip(array, axis, bit):
    return lax.ppermute(array, axis, [(i, i ^ bit) for i in range(lax.axis_size(axis))])


def bits(axis):
    size = lax.axis_size(axis)
    return [1 << k for k in range(size.bit_length() - 1)]


def join(mine, theirs, axis, bit):
    upper = lax.rem(lax.axis_index(axis) // bit, 2) == 1
    return jnp.where(
        upper,
        jnp.concatenate([theirs, mine], axis=0),
        jnp.concatenate([mine, theirs], axis=0),
    )


def rounded(values):
    return lax.reduce_precision(values, 8, 7).astype(BF)


def per_device(scenes, kernel, weight_in, weight_out, captions, positives):
    images, rows, cols, channels = scenes.shape
    hidden_units = weight_in.shape[1]
    space_count = lax.axis_size("space")
    pixels = images * rows * cols
    scene_pixels = rows * space_count * cols

    up = [(i, i + 1) for i in range(space_count - 1)]
    down = [(j, i) for i, j in up]
    before = lax.ppermute(scenes[:, rows - SIDE :], "space", up)
    after = lax.ppermute(scenes[:, :SIDE], "space", down)
    macs = 2 * TAPS * TAPS * pixels * channels
    part, spread = call(
        conv_body,
        [((images, rows, cols, channels), F32), ((TAPS * TAPS, cols, channels), F32)],
        [scenes, kernel],
        flops=macs,
    )
    gathered = captions
    for bit in bits("dp"):
        gathered = join(gathered, flip(gathered, "dp", bit), "dp", bit)

    sums, normed, inv, hidden = call(
        forward_body,
        [
            ((images, channels), F32),
            ((pixels, channels), F32),
            ((pixels, LANES), F32),
            ((pixels, hidden_units), F32),
        ],
        [part, before, after, spread, scenes, weight_in, weight_out],
        scratch=[pltpu.VMEM((pixels, channels), F32), pltpu.VMEM((pixels, channels), BF)],
        flops=2 * pixels * channels * hidden_units,
    )
    for bit in bits("space"):
        sums = sums + flip(sums, "space", bit)
    (slope,) = call(slope_body, [((pixels, hidden_units), F32)], [hidden], flops=1000000)

    listed = channels // LANES // 2 * TAPS * TAPS
    listed += -listed % 16
    own_rows = images * (channels // LANES + 1)
    own_rows += -own_rows % 16
    grad, pay = call(
        functools.partial(backward_body, scene_pixels),
        [((pixels, channels), F32), ((listed + own_rows, LANES), BF)],
        [sums, gathered, positives, slope, normed, inv, weight_in, weight_out, scenes, before, after],
        scratch=[
            pltpu.VMEM((listed, LANES), F32),
            pltpu.VMEM((pixels, hidden_units), BF),
            pltpu.VMEM((own_rows, LANES), F32),
        ],
        smem=(2,),
        flops=macs,
    )
    other = flip(pay, "dp", 1)
    (own,) = call(
        own_half_body, [((listed, LANES), F32)], [grad, scenes, before, after], flops=macs // 2
    )
    total = own + other[:listed].astype(F32)
    units = join(pay[listed:], other[listed:], "dp", 1)
    for bit in bits("dp")[1:]:
        mine = rounded(total)
        other = flip(jnp.concatenate([mine, units], axis=0), "dp", bit)
        total = mine.astype(F32) + other[:listed].astype(F32)
        units = join(units, other[listed:], "dp", bit)
    text_grad, loss = call(
        text_body,
        [((images, channels), F32), ((1, 1), F32)],
        [units, captions],
        scratch=[pltpu.VMEM(units.shape, F32)],
    )
    for bit in bits("space"):
        mine = rounded(total)
        total = mine.astype(F32) + flip(mine, "space", bit).astype(F32)
    mine = rounded(total)
    other = flip(mine, "dp", 1)
    (kernel_grad,) = call(
        merge_body,
        [((TAPS, TAPS, channels), F32)],
        [mine, other],
        scratch=[pltpu.VMEM((listed, LANES), F32)],
    )
    return (loss.reshape(()), text_grad, kernel_grad)


def solution(mesh):
    return jax.shard_map(
        per_device,
        mesh=mesh,
        in_specs=(P("dp", "space", None, None), P(), P(), P(), P("dp", None), P("dp")),
        out_specs=(P(), P("dp", None), P()),
        check_vma=False,
    )
```

time: 201 us -> 61.9 us (0.31)
  blocking collectives: 81.9 us -> 0 us
  waiting for transfers between devices: 57.4 us -> 16 us
  other arithmetic: 22.3 us -> 0.93 us
  between operations: 17.8 us -> 2.06 us
  starting transfers between devices: 6.26 us -> 20 us
  Pallas kernels: 0 us -> 11.7 us
  matrix products: 7.31 us -> 0 us
  local copies, waits for them, and re-layouts: 6.3 us -> 10.7 us
    psum x1 -> x0, waiting for transfers between devices: 57.4 us -> none  [per_device(): lax.psum((kernel_part, loss_share), ('dp', 'space'))]
    psum x2 -> x0, blocking collectives: 50 us -> none  [the longest x1 36.9 us: per_device(): lax.psum((kernel_part, loss_share), ('dp', 'space'))]
    unnamed x1 -> x0, blocking collectives: 22.8 us -> none
    ppermute x2 -> x13, waiting for transfers between devices: 0.01 us -> 16 us  [the longest x11 16 us: flip(): lax.ppermute(array, axis, [(i, i ^ bit) for i in range(lax.axis_size(axis...]
    reduce_sum x10 -> x0, other arithmetic: 13.8 us -> none  [the longest x1 6.42 us: normalize_rows(): center = conv_out - jnp.mean(conv_out, axis=-1, keepdims=True)]
    ppermute x2 -> x13, starting transfers between devices: 6.22 us -> 20 us  [the longest x11 15.2 us: flip(): lax.ppermute(array, axis, [(i, i ^ bit) for i in range(lax.axis_size(axis...]
    pallas_call x0 -> x7, Pallas kernels: none -> 11.7 us  [call(): pl.pallas_call(body, out_shape=[vmem_out(shape, dtype) for shape, dtype i...]
    all_gather x1 -> x0, blocking collectives: 9.18 us -> none  [per_device(): gathered = lax.all_gather(captions, 'dp', axis=0, tiled=True)]
  transfers between devices with their start and end apart: 3 -> 13, of which waited for: 1 -> 7; matrix products, arithmetic and copies ran while one was open for 4% -> 3% of each run, Pallas kernels for 0% -> 12%
where the time goes in v1:
time: 61.9 us; the launch traced here: 61.5 us
  starting transfers between devices  20 us (32%)
  waiting for transfers between devices  16 us (26%)
  Pallas kernels  11.7 us (19%)
  local copies, waits for them, and re-layouts  10.7 us (17%)
  between operations  2.06 us (3%)
  other arithmetic  0.93 us (2%)
    ppermute x11, waiting for transfers between devices, flip(): lax.ppermute(array, axis, [(i, i ^ bit) for i in range(lax.axis_size(axis...  16 us
    ppermute x11, starting transfers between devices, flip(): lax.ppermute(array, axis, [(i, i ^ bit) for i in range(lax.axis_size(axis...  15.2 us
    pallas_call x7, Pallas kernels, call(): pl.pallas_call(body, out_shape=[vmem_out(shape, dtype) for shape, dtype i...  11.7 us
    unnamed x24, local copies, waits for them, and re-layouts  9.75 us
    ppermute x1, starting transfers between devices, per_device(): before = lax.ppermute(scenes[:, rows - SIDE:], 'space', up)  3.48 us
    ppermute x1, starting transfers between devices, per_device(): after = lax.ppermute(scenes[:, :SIDE], 'space', down)  1.29 us
  transfers between devices with their start and end apart: 13, of which 7 were waited for; matrix products, arithmetic and copies ran while one was open for 3% of the time, Pallas kernels for 12%

profile of v1, /device:TPU:0, one launch (start us, length us, event | category | flops | bytes accessed | tf_op | source)
XLA Modules:
  0.0 61.5 jit_solution(5581383980056183326)
XLA Ops:
  0.6 0.5 collective-permute-start.4
  1.1 1.0 %collective-permute-done.4 = bf16[2,768]{1,0:T(2,128)(2,1)S(1)} collective-permute-done((bf16[2,768]{1,0:T(2,128)(2,1)}, bf16[2,768]{1,0:T(2,128)(2,1)S(1)}, u32[]{:S(2)}, u32[]{:S(2)}) %collective-permute-start.4) | collective-permute-done | bytes 3104 | tf_op jit(solution)/shard_map/ppermute | solution.py:353
  2.2 0.8 %maximum_select_fusion.5 = bf16[4,768]{1,0:T(4,128)(2,1)S(1)} fusion(bf16[2,768]{1,0:T(2,128)(2,1)} %caps_ref.1, bf16[2,768]{1,0:T(2,128)(2,1)S(1)} %collective-permute-done.4, pred[]{:T(512)S(6)} %eq.14), kind=kLoop, calls=%fused_computation.12 | loop fusion | flops 27648 | bytes 12289 | tf_op jit(solution)/shard_map/jit(_where)/select_n | solution.py:363
  3.0 2.9 %collective-permute-start.5 = (bf16[4,768]{1,0:T(4,128)(2,1)S(1)}, bf16[4,768]{1,0:T(4,128)(2,1)S(1)}, u32[]{:S(2)}, u32[]{:S(2)}) collective-permute-start(bf16[4,768]{1,0:T(4,128)(2,1)S(1)} %maximum_select_fusion.5), channel_id=1, source_target_pairs={{0,8},{4,12},{8,0},{12,4},{16,24},{20,28},{24,16},{28,20},{1,9},{5... | collective-permute-start | bytes 18440 | tf_op jit(solution)/shard_map/ppermute | solution.py:353
  5.9 0.9 %fusion = (bf16[2,3,8,768]{3,2,1,0:T(8,128)(2,1)S(1)}, bf16[2,3,8,768]{3,2,1,0:T(8,128)(2,1)S(1)}) fusion(bf16[2,14,8,768]{3,2,1,0:T(8,128)(2,1)} %x_ref.7), kind=kLoop, calls=%fused_computation.13 | loop fusion | bytes 294912 | tf_op jit(solution)/shard_map/slice | solution.py:384
  6.8 3.5 %collective-permute-start = (bf16[2,3,8,768]{3,2,1,0:T(8,128)(2,1)S(1)}, bf16[2,3,8,768]{3,2,1,0:T(8,128)(2,1)S(1)}, u32[]{:S(2)}, u32[]{:S(2)}) collective-permute-start(bf16[2,3,8,768]{3,2,1,0:T(8,128)(2,1)S(1)} %get-tuple-element.24), channel_id=1, source_target_pairs={{0,1},{1,2},{2,3},{4,5},{5,6},{6,7},{8,9},{9,10},{10,11},{12,13},{... | collective-permute-start | bytes 221192 | tf_op jit(solution)/shard_map/ppermute | solution.py:383
  10.3 1.3 %collective-permute-start.1 = (bf16[2,3,8,768]{3,2,1,0:T(8,128)(2,1)S(1)}, bf16[2,3,8,768]{3,2,1,0:T(8,128)(2,1)S(1)}, u32[]{:S(2)}, u32[]{:S(2)}) collective-permute-start(bf16[2,3,8,768]{3,2,1,0:T(8,128)(2,1)S(1)} %get-tuple-element.23), channel_id=1, source_target_pairs={{1,0},{2,1},{3,2},{5,4},{6,5},{7,6},{9,8},{10,9},{11,10},{13,12},{... | collective-permute-start | bytes 221192 | tf_op jit(solution)/shard_map/ppermute | solution.py:384
  11.6 0.0 copy-start.4
  11.6 1.0 %copy-done.4 = bf16[2,14,8,768]{3,2,1,0:T(8,128)(2,1)S(1)} copy-done((bf16[2,14,8,768]{3,2,1,0:T(8,128)(2,1)S(1)}, bf16[2,14,8,768]{3,2,1,0:T(8,128)(2,1)}, u32[]{:S(2)}) %copy-start.4) | copy-done | bytes 344088
  12.6 0.0 copy-start.8
  12.6 0.9 %copy-done.8 = bf16[7,7,768]{2,1,0:T(8,128)(2,1)S(1)} copy-done((bf16[7,7,768]{2,1,0:T(8,128)(2,1)S(1)}, bf16[7,7,768]{2,1,0:T(8,128)(2,1)}, u32[]{:S(2)}) %copy-start.8) | copy-done | bytes 75288
  13.5 2.2 %shard_map.85 = (f32[2,14,8,768]{3,2,1,0:T(8,128)S(1)}, f32[49,8,768]{2,1,0:T(8,128)S(1)}) custom-call(bf16[2,14,8,768]{3,2,1,0:T(8,128)(2,1)S(1)} %copy-done.4, bf16[7,7,768]{2,1,0:T(8,128)(2,1)S(1)} %copy-done.8), custom_call_target="tpu_custom_call" | custom-call | flops 16859136 | tf_op jit(solution)/shard_map/pallas_call | solution.py:35
  15.7 0.0 collective-permute-done.5
  15.7 1.6 %collective-permute-start.6 = (bf16[8,768]{1,0:T(8,128)(2,1)S(1)}, bf16[8,768]{1,0:T(8,128)(2,1)S(1)}, u32[]{:S(2)}, u32[]{:S(2)}) collective-permute-start(bf16[8,768]{1,0:T(8,128)(2,1)S(1)} %maximum_select_fusion.3), channel_id=1, source_target_pairs={{0,16},{4,20},{8,24},{12,28},{16,0},{20,4},{24,8},{28,12},{1,17},{... | collective-permute-start | bytes 36872 | tf_op jit(solution)/shard_map/ppermute | solution.py:353
  17.3 0.0 collective-permute-done.before_ref
  17.3 0.0 collective-permute-done.1.after_ref
  17.3 0.0 copy-start
  17.3 1.7 %copy-done = bf16[768,1536]{1,0:T(8,128)(2,1)S(1)} copy-done((bf16[768,1536]{1,0:T(8,128)(2,1)S(1)}, bf16[768,1536]{1,0:T(8,128)(2,1)}, u32[]{:S(2)}) %copy-start) | copy-done | bytes 2359320
  19.0 0.0 copy-start.2
  19.0 1.7 %copy-done.2 = bf16[1536,768]{1,0:T(8,128)(2,1)S(1)} copy-done((bf16[1536,768]{1,0:T(8,128)(2,1)S(1)}, bf16[1536,768]{1,0:T(8,128)(2,1)}, u32[]{:S(2)}) %copy-start.2) | copy-done | bytes 2359320
  20.6 0.0 copy-start.3
  20.6 2.9 %shard_map.86 = (f32[2,768]{1,0:T(2,128)S(1)}, f32[224,768]{1,0:T(8,128)S(1)}, f32[224,128]{1,0:T(8,128)S(1)}, f32[224,1536]{1,0:T(8,128)S(1)}) custom-call(f32[2,14,8,768]{3,2,1,0:T(8,128)S(1)} %get-tuple-element.13.part_ref, bf16[2,3,8,768]{3,2,1,0:T(8,128)(2,1)S(1)} %collective-permute-done.before_ref, ...), custom_call_target="tpu_custom_call" | custom-call | flops 528482304 | tf_op jit(solution)/shard_map/pallas_call | solution.py:35
  23.5 0.0 copy-start.6
  23.5 1.1 %copy-done.6 = f32[224,1536]{1,0:T(8,128)} copy-done((f32[224,1536]{1,0:T(8,128)}, f32[224,1536]{1,0:T(8,128)S(1)}, u32[]{:S(2)}) %copy-start.6) | copy-done | bytes 1376280
  24.6 2.7 %collective-permute-start.2 = (f32[2,768]{1,0:T(2,128)S(1)}, f32[2,768]{1,0:T(2,128)S(1)}, u32[]{:S(2)}, u32[]{:S(2)}) collective-permute-start(f32[2,768]{1,0:T(2,128)S(1)} %get-tuple-element.15), channel_id=1, source_target_pairs={{0,1},{1,0},{2,3},{3,2},{4,5},{5,4},{6,7},{7,6},{8,9},{9,8},{10,11... | collective-permute-start | bytes 18440 | tf_op jit(solution)/shard_map/ppermute | solution.py:353
  27.3 1.6 %collective-permute-done.2 = f32[2,768]{1,0:T(2,128)S(1)} collective-permute-done((f32[2,768]{1,0:T(2,128)S(1)}, f32[2,768]{1,0:T(2,128)S(1)}, u32[]{:S(2)}, u32[]{:S(2)}) %collective-permute-start.2) | collective-permute-done | bytes 6176 | tf_op jit(solution)/shard_map/ppermute | solution.py:353
  28.9 3.0 %collective-permute-start.3 = (f32[2,768]{1,0:T(2,128)S(1)}, f32[2,768]{1,0:T(2,128)S(1)}, u32[]{:S(2)}, u32[]{:S(2)}) collective-permute-start(f32[2,768]{1,0:T(2,128)S(1)} %add.24), channel_id=1, source_target_pairs={{0,2},{1,3},{2,0},{3,1},{4,6},{5,7},{6,4},{7,5},{8,10},{9,11},{10,... | collective-permute-start | bytes 18440 | tf_op jit(solution)/shard_map/ppermute | solution.py:353
  31.9 0.0 collective-permute-done.6
  31.9 0.0 copy-start.7
  31.9 1.3 %copy-done.7 = f32[224,1536]{1,0:T(8,128)S(1)} copy-done((f32[224,1536]{1,0:T(8,128)S(1)}, f32[224,1536]{1,0:T(8,128)}, u32[]{:S(2)}) %copy-start.7) | copy-done | bytes 1376280
  33.3 0.0 copy-start.1
  33.3 0.0 copy-start.5
  33.3 0.0 copy-start.10
  33.3 0.8 %shard_map.87.slope_ref = f32[224,1536]{1,0:T(8,128)S(1)} custom-call(f32[224,1536]{1,0:T(8,128)S(1)} %copy-done.7), custom_call_target="tpu_custom_call" | custom-call | flops 1000000 | tf_op jit(solution)/shard_map/pallas_call | solution.py:35
  34.1 0.0 collective-permute-done.3
  34.1 0.0 copy-done.3
  34.1 0.8 %copy-done.1 = bf16[768,1536]{1,0:T(8,128)(2,1)S(1)} copy-done((bf16[768,1536]{1,0:T(8,128)(2,1)S(1)}, bf16[768,1536]{1,0:T(8,128)(2,1)}, u32[]{:S(2)}) %copy-start.1) | copy-done | bytes 2359320
  34.9 0.0 copy-done.5
  35.0 0.0 copy-done.10
  35.0 4.1 %shard_map.88 = (f32[224,768]{1,0:T(8,128)S(1)}, bf16[176,128]{1,0:T(8,128)(2,1)S(1)}) custom-call(f32[2,768]{1,0:T(2,128)S(1)} %add.25.total_ref, bf16[16,768]{1,0:T(8,128)(2,1)S(1)} %maximum_select_fusion.1.caps_ref, s32[2]{0:T(128)S(1)} %copy-done.10, f32[224,1536]{1,0:T(8,128)S(1)} %shard_map.87.slope_ref, f32[224,768]{1,0:T(8,128)S(1)} %get-tuple-element.17.normed_ref, ...), custom_call_target="tpu_custom_call" | custom-call | flops 16859136 | tf_op jit(solution)/shard_map/pallas_call | solution.py:35
  39.1 0.0 copy-start.9
  39.1 0.1 collective-permute-start.7
  39.2 1.5 %shard_map.89 = f32[160,128]{1,0:T(8,128)S(1)} custom-call(f32[224,768]{1,0:T(8,128)S(1)} %get-tuple-element.19.grad_ref, bf16[2,14,8,768]{3,2,1,0:T(8,128)(2,1)S(1)} %copy-done.5, bf16[2,3,8,768]{3,2,1,0:T(8,128)(2,1)S(1)} %collective-permute-done.before_ref, bf16[2,3,8,768]{3,2,1,0:T(8,128)(2,1)S(1)} %collective-permute-done.1.after_ref), custom_call_target="tpu_custom_call" | custom-call | flops 8429568 | tf_op jit(solution)/shard_map/pallas_call | solution.py:35
  40.7 0.0 collective-permute-done.7
  40.8 0.6 collective-permute-start.8
  41.4 3.6 %collective-permute-done.8 = bf16[192,128]{1,0:T(8,128)(2,1)S(1)} collective-permute-done((bf16[192,128]{1,0:T(8,128)(2,1)S(1)}, bf16[192,128]{1,0:T(8,128)(2,1)S(1)}, u32[]{:S(2)}, u32[]{:S(2)}) %collective-permute-start.8) | collective-permute-done | bytes 49184 | tf_op jit(solution)/shard_map/ppermute | solution.py:353
  45.0 0.6 collective-permute-start.9
  45.6 3.7 %collective-permute-done.9 = bf16[224,128]{1,0:T(8,128)(2,1)S(1)} collective-permute-done((bf16[224,128]{1,0:T(8,128)(2,1)S(1)}, bf16[224,128]{1,0:T(8,128)(2,1)S(1)}, u32[]{:S(2)}, u32[]{:S(2)}) %collective-permute-start.9) | collective-permute-done | bytes 57376 | tf_op jit(solution)/shard_map/ppermute | solution.py:353
  49.3 1.6 %collective-permute-start.10 = (bf16[160,128]{1,0:T(8,128)(2,1)S(1)}, bf16[160,128]{1,0:T(8,128)(2,1)S(1)}, u32[]{:S(2)}, u32[]{:S(2)}) collective-permute-start(bf16[160,128]{1,0:T(8,128)(2,1)S(1)} %reduce-precision_convert_fusion.2), channel_id=1, source_target_pairs={{0,1},{1,0},{2,3},{3,2},{4,5},{5,4},{6,7},{7,6},{8,9},{9,8},{10,11... | collective-permute-start | bytes 122888 | tf_op jit(solution)/shard_map/ppermute | solution.py:353
  50.9 2.4 %collective-permute-done.10 = bf16[160,128]{1,0:T(8,128)(2,1)S(1)} collective-permute-done((bf16[160,128]{1,0:T(8,128)(2,1)S(1)}, bf16[160,128]{1,0:T(8,128)(2,1)S(1)}, u32[]{:S(2)}, u32[]{:S(2)}) %collective-permute-start.10) | collective-permute-done | bytes 40992 | tf_op jit(solution)/shard_map/ppermute | solution.py:353
  53.3 1.6 %collective-permute-start.11 = (bf16[160,128]{1,0:T(8,128)(2,1)S(1)}, bf16[160,128]{1,0:T(8,128)(2,1)S(1)}, u32[]{:S(2)}, u32[]{:S(2)}) collective-permute-start(bf16[160,128]{1,0:T(8,128)(2,1)S(1)} %reduce-precision_convert_fusion.1), channel_id=1, source_target_pairs={{0,2},{1,3},{2,0},{3,1},{4,6},{5,7},{6,4},{7,5},{8,10},{9,11},{10,... | collective-permute-start | bytes 122888 | tf_op jit(solution)/shard_map/ppermute | solution.py:353
  54.9 3.4 %collective-permute-done.11 = bf16[160,128]{1,0:T(8,128)(2,1)S(1)} collective-permute-done((bf16[160,128]{1,0:T(8,128)(2,1)S(1)}, bf16[160,128]{1,0:T(8,128)(2,1)S(1)}, u32[]{:S(2)}, u32[]{:S(2)}) %collective-permute-start.11) | collective-permute-done | bytes 40992 | tf_op jit(solution)/shard_map/ppermute | solution.py:353
  58.3 0.1 collective-permute-start.12
  58.4 0.0 copy-done.9
  58.4 0.2 shard_map.90
  58.7 0.6 copy.10
  59.3 0.3 collective-permute-done.12.other_ref
  59.7 0.7 %copy.11 = f32[7,7,768]{2,1,0:T(8,128)} copy(f32[7,7,768]{2,1,0:T(8,128)S(1)} %shard_map.91) | data formatting | bytes 301056
  (19 shorter events, 0.2 us)
Async XLA Ops:
  0.6 1.6 %collective-permute-start.4 = (bf16[2,768]{1,0:T(2,128)(2,1)}, bf16[2,768]{1,0:T(2,128)(2,1)S(1)}, u32[]{:S(2)}, u32[]{:S(2)}) collective-permute-start(bf16[2,768]{1,0:T(2,128)(2,1)} %caps_ref.1), channel_id=1, source_target_pairs={{0,4},{4,0},{8,12},{12,8},{16,20},{20,16},{24,28},{28,24},{1,5},{5... | collective-permute-start | bytes 9224 | tf_op jit(solution)/shard_map/ppermute | solution.py:353
  3.0 12.7 %collective-permute-start.5 = (bf16[4,768]{1,0:T(4,128)(2,1)S(1)}, bf16[4,768]{1,0:T(4,128)(2,1)S(1)}, u32[]{:S(2)}, u32[]{:S(2)}) collective-permute-start(bf16[4,768]{1,0:T(4,128)(2,1)S(1)} %maximum_select_fusion.5), channel_id=1, source_target_pairs={{0,8},{4,12},{8,0},{12,4},{16,24},{20,28},{24,16},{28,20},{1,9},{5... | collective-permute-start | bytes 18440 | tf_op jit(solution)/shard_map/ppermute | solution.py:353
  6.8 10.5 %collective-permute-start = (bf16[2,3,8,768]{3,2,1,0:T(8,128)(2,1)S(1)}, bf16[2,3,8,768]{3,2,1,0:T(8,128)(2,1)S(1)}, u32[]{:S(2)}, u32[]{:S(2)}) collective-permute-start(bf16[2,3,8,768]{3,2,1,0:T(8,128)(2,1)S(1)} %get-tuple-element.24), channel_id=1, source_target_pairs={{0,1},{1,2},{2,3},{4,5},{5,6},{6,7},{8,9},{9,10},{10,11},{12,13},{... | collective-permute-start | bytes 221192 | tf_op jit(solution)/shard_map/ppermute | solution.py:383
  10.3 7.0 %collective-permute-start.1 = (bf16[2,3,8,768]{3,2,1,0:T(8,128)(2,1)S(1)}, bf16[2,3,8,768]{3,2,1,0:T(8,128)(2,1)S(1)}, u32[]{:S(2)}, u32[]{:S(2)}) collective-permute-start(bf16[2,3,8,768]{3,2,1,0:T(8,128)(2,1)S(1)} %get-tuple-element.23), channel_id=1, source_target_pairs={{1,0},{2,1},{3,2},{5,4},{6,5},{7,6},{9,8},{10,9},{11,10},{13,12},{... | collective-permute-start | bytes 221192 | tf_op jit(solution)/shard_map/ppermute | solution.py:384
  11.6 1.0 %copy-start.4 = (bf16[2,14,8,768]{3,2,1,0:T(8,128)(2,1)S(1)}, bf16[2,14,8,768]{3,2,1,0:T(8,128)(2,1)}, u32[]{:S(2)}) copy-start(bf16[2,14,8,768]{3,2,1,0:T(8,128)(2,1)} %x_ref.7) | copy-start | bytes 1032196
  12.6 0.9 %copy-start.8 = (bf16[7,7,768]{2,1,0:T(8,128)(2,1)S(1)}, bf16[7,7,768]{2,1,0:T(8,128)(2,1)}, u32[]{:S(2)}) copy-start(bf16[7,7,768]{2,1,0:T(8,128)(2,1)} %k_ref.1) | copy-start | bytes 225796
  15.7 16.2 %collective-permute-start.6 = (bf16[8,768]{1,0:T(8,128)(2,1)S(1)}, bf16[8,768]{1,0:T(8,128)(2,1)S(1)}, u32[]{:S(2)}, u32[]{:S(2)}) collective-permute-start(bf16[8,768]{1,0:T(8,128)(2,1)S(1)} %maximum_select_fusion.3), channel_id=1, source_target_pairs={{0,16},{4,20},{8,24},{12,28},{16,0},{20,4},{24,8},{28,12},{1,17},{... | collective-permute-start | bytes 36872 | tf_op jit(solution)/shard_map/ppermute | solution.py:353
  17.3 1.7 %copy-start = (bf16[768,1536]{1,0:T(8,128)(2,1)S(1)}, bf16[768,1536]{1,0:T(8,128)(2,1)}, u32[]{:S(2)}) copy-start(bf16[768,1536]{1,0:T(8,128)(2,1)} %win_ref.3) | copy-start | bytes 7077892
  19.0 1.7 %copy-start.2 = (bf16[1536,768]{1,0:T(8,128)(2,1)S(1)}, bf16[1536,768]{1,0:T(8,128)(2,1)}, u32[]{:S(2)}) copy-start(bf16[1536,768]{1,0:T(8,128)(2,1)} %wout_ref.3) | copy-start | bytes 7077892
  20.6 13.5 %copy-start.3 = (bf16[1536,768]{1,0:T(8,128)(2,1)S(1)}, bf16[1536,768]{1,0:T(8,128)(2,1)}, u32[]{:S(2)}) copy-start(bf16[1536,768]{1,0:T(8,128)(2,1)} %wout_ref.3) | copy-start | bytes 7077892
  23.5 1.1 %copy-start.6 = (f32[224,1536]{1,0:T(8,128)}, f32[224,1536]{1,0:T(8,128)S(1)}, u32[]{:S(2)}) copy-start(f32[224,1536]{1,0:T(8,128)S(1)} %get-tuple-element.16.hid_ref) | copy-start | bytes 4128772
  24.6 4.3 %collective-permute-start.2 = (f32[2,768]{1,0:T(2,128)S(1)}, f32[2,768]{1,0:T(2,128)S(1)}, u32[]{:S(2)}, u32[]{:S(2)}) collective-permute-start(f32[2,768]{1,0:T(2,128)S(1)} %get-tuple-element.15), channel_id=1, source_target_pairs={{0,1},{1,0},{2,3},{3,2},{4,5},{5,4},{6,7},{7,6},{8,9},{9,8},{10,11... | collective-permute-start | bytes 18440 | tf_op jit(solution)/shard_map/ppermute | solution.py:353
  28.9 5.2 %collective-permute-start.3 = (f32[2,768]{1,0:T(2,128)S(1)}, f32[2,768]{1,0:T(2,128)S(1)}, u32[]{:S(2)}, u32[]{:S(2)}) collective-permute-start(f32[2,768]{1,0:T(2,128)S(1)} %add.24), channel_id=1, source_target_pairs={{0,2},{1,3},{2,0},{3,1},{4,6},{5,7},{6,4},{7,5},{8,10},{9,11},{10,... | collective-permute-start | bytes 18440 | tf_op jit(solution)/shard_map/ppermute | solution.py:353
  31.9 1.3 %copy-start.7 = (f32[224,1536]{1,0:T(8,128)S(1)}, f32[224,1536]{1,0:T(8,128)}, u32[]{:S(2)}) copy-start(f32[224,1536]{1,0:T(8,128)} %copy-done.6) | copy-start | bytes 4128772
  33.3 1.7 %copy-start.1 = (bf16[768,1536]{1,0:T(8,128)(2,1)S(1)}, bf16[768,1536]{1,0:T(8,128)(2,1)}, u32[]{:S(2)}) copy-start(bf16[768,1536]{1,0:T(8,128)(2,1)} %win_ref.3) | copy-start | bytes 7077892
  33.3 1.7 %copy-start.5 = (bf16[2,14,8,768]{3,2,1,0:T(8,128)(2,1)S(1)}, bf16[2,14,8,768]{3,2,1,0:T(8,128)(2,1)}, u32[]{:S(2)}) copy-start(bf16[2,14,8,768]{3,2,1,0:T(8,128)(2,1)} %x_ref.7) | copy-start | bytes 1032196
  33.3 1.7 %copy-start.10 = (s32[2]{0:T(128)S(1)}, s32[2]{0:T(128)}, u32[]{:S(2)}) copy-start(s32[2]{0:T(128)} %pos_ref.1) | copy-start | bytes 28
  39.1 19.4 %copy-start.9 = (bf16[2,768]{1,0:T(2,128)(2,1)S(1)}, bf16[2,768]{1,0:T(2,128)(2,1)}, u32[]{:S(2)}) copy-start(bf16[2,768]{1,0:T(2,128)(2,1)} %caps_ref.1) | copy-start | bytes 9220
  39.1 1.6 %collective-permute-start.7 = (bf16[176,128]{1,0:T(8,128)(2,1)S(1)}, bf16[176,128]{1,0:T(8,128)(2,1)S(1)}, u32[]{:S(2)}, u32[]{:S(2)}) collective-permute-start(bf16[176,128]{1,0:T(8,128)(2,1)S(1)} %get-tuple-element.20), channel_id=1, source_target_pairs={{0,4},{4,0},{8,12},{12,8},{16,20},{20,16},{24,28},{28,24},{1,5},{5... | collective-permute-start | bytes 135176 | tf_op jit(solution)/shard_map/ppermute | solution.py:353
  40.8 4.2 %collective-permute-start.8 = (bf16[192,128]{1,0:T(8,128)(2,1)S(1)}, bf16[192,128]{1,0:T(8,128)(2,1)S(1)}, u32[]{:S(2)}, u32[]{:S(2)}) collective-permute-start(bf16[192,128]{1,0:T(8,128)(2,1)S(1)} %pad_maximum_fusion.1), channel_id=1, source_target_pairs={{0,8},{4,12},{8,0},{12,4},{16,24},{20,28},{24,16},{28,20},{1,9},{5... | collective-permute-start | bytes 147464 | tf_op jit(solution)/shard_map/ppermute | solution.py:353
  45.0 4.2 %collective-permute-start.9 = (bf16[224,128]{1,0:T(8,128)(2,1)S(1)}, bf16[224,128]{1,0:T(8,128)(2,1)S(1)}, u32[]{:S(2)}, u32[]{:S(2)}) collective-permute-start(bf16[224,128]{1,0:T(8,128)(2,1)S(1)} %pad_maximum_fusion), channel_id=1, source_target_pairs={{0,16},{4,20},{8,24},{12,28},{16,0},{20,4},{24,8},{28,12},{1,17},{... | collective-permute-start | bytes 172040 | tf_op jit(solution)/shard_map/ppermute | solution.py:353
  49.3 4.1 %collective-permute-start.10 = (bf16[160,128]{1,0:T(8,128)(2,1)S(1)}, bf16[160,128]{1,0:T(8,128)(2,1)S(1)}, u32[]{:S(2)}, u32[]{:S(2)}) collective-permute-start(bf16[160,128]{1,0:T(8,128)(2,1)S(1)} %reduce-precision_convert_fusion.2), channel_id=1, source_target_pairs={{0,1},{1,0},{2,3},{3,2},{4,5},{5,4},{6,7},{7,6},{8,9},{9,8},{10,11... | collective-permute-start | bytes 122888 | tf_op jit(solution)/shard_map/ppermute | solution.py:353
  53.3 5.0 %collective-permute-start.11 = (bf16[160,128]{1,0:T(8,128)(2,1)S(1)}, bf16[160,128]{1,0:T(8,128)(2,1)S(1)}, u32[]{:S(2)}, u32[]{:S(2)}) collective-permute-start(bf16[160,128]{1,0:T(8,128)(2,1)S(1)} %reduce-precision_convert_fusion.1), channel_id=1, source_target_pairs={{0,2},{1,3},{2,0},{3,1},{4,6},{5,7},{6,4},{7,5},{8,10},{9,11},{10,... | collective-permute-start | bytes 122888 | tf_op jit(solution)/shard_map/ppermute | solution.py:353
  58.3 1.3 %collective-permute-start.12 = (bf16[160,128]{1,0:T(8,128)(2,1)S(1)}, bf16[160,128]{1,0:T(8,128)(2,1)S(1)}, u32[]{:S(2)}, u32[]{:S(2)}) collective-permute-start(bf16[160,128]{1,0:T(8,128)(2,1)S(1)} %reduce-precision_convert_fusion.own_ref), channel_id=1, source_target_pairs={{0,4},{4,0},{8,12},{12,8},{16,20},{20,16},{24,28},{28,24},{1,5},{5... | collective-permute-start | bytes 122888 | tf_op jit(solution)/shard_map/ppermute | solution.py:353

commit v2 on v1

--- a/solution.py
+++ b/solution.py
@@ -26,12 +26,23 @@
     return pltpu.VMEM(shape, dtype)
 
 
-def call(body, outs, args, scratch=(), smem=(), limit=40, flops=0):
-    specs = [
-        pl.BlockSpec(memory_space=pltpu.SMEM if k in smem else pltpu.VMEM)
-        for k in range(len(args))
-    ]
-    args = [a if k in smem else in_vmem(a) for k, a in enumerate(args)]
+def in_hbm(array):
+    return pltpu.with_memory_space_constraint(array, pltpu.HBM)
+
+
+def call(body, outs, args, scratch=(), smem=(), hbm=(), limit=40, micros=1):
+    specs = []
+    placed = []
+    for k, arg in enumerate(args):
+        if k in smem:
+            specs.append(pl.BlockSpec(memory_space=pltpu.SMEM))
+            placed.append(arg)
+        elif k in hbm:
+            specs.append(pl.BlockSpec(memory_space=pl.ANY))
+            placed.append(in_hbm(arg))
+        else:
+            specs.append(pl.BlockSpec(memory_space=pltpu.VMEM))
+            placed.append(in_vmem(arg))
     return pl.pallas_call(
         body,
         out_shape=[vmem_out(shape, dtype) for shape, dtype in outs],
@@ -39,8 +50,10 @@
         out_specs=[pl.BlockSpec(memory_space=pltpu.VMEM) for _ in outs],
         scratch_shapes=list(scratch),
         compiler_params=pltpu.CompilerParams(vmem_limit_bytes=limit * 1024 * 1024),
-        cost_estimate=pl.CostEstimate(flops=flops, bytes_accessed=0, transcendentals=0),
-    )(*args)
+        cost_estimate=pl.CostEstimate(
+            flops=int(micros * 1.15e9), bytes_accessed=0, transcendentals=0
+        ),
+    )(*placed)
 
 
 def column_masks(cols, lanes=LANES):
@@ -54,14 +67,37 @@
     return pl.ds(pl.multiple_of(t * LANES, LANES), LANES)
 
 
-def conv_body(x_ref, k_ref, part_ref, kw_ref):
-    images, rows, cols, channels = x_ref.shape
+def load_body(x_hbm, k_hbm, x_ref, first_ref, last_ref, kw_ref, taps_ref, sems):
+    rows, cols, channels = x_hbm.shape[1:]
+    copies = [
+        pltpu.make_async_copy(k_hbm, taps_ref, sems.at[0]),
+        pltpu.make_async_copy(x_hbm.at[:, :SIDE], first_ref, sems.at[1]),
+        pltpu.make_async_copy(x_hbm.at[:, rows - SIDE :], last_ref, sems.at[2]),
+        pltpu.make_async_copy(x_hbm, x_ref, sems.at[3]),
+    ]
+    for copy in copies:
+        copy.start()
     masks = column_masks(cols, channels)
+    copies[0].wait()
     for i in range(TAPS):
-        taps = k_ref[i].astype(F32)
+        taps = taps_ref[i].astype(F32)
         for j in range(TAPS):
             spread = jnp.broadcast_to(taps[j : j + 1], (cols, channels))
             kw_ref[i * TAPS + j] = jnp.where(masks[j], spread, 0.0)
+    for copy in copies[1:]:
+        copy.wait()
+
+
+def conv_body(
+    x_ref, kw_ref, win_hbm, wout_hbm, part_ref, win_ref, wout_ref, sems
+):
+    images, rows, cols, channels = x_ref.shape
+    copies = [
+        pltpu.make_async_copy(win_hbm, win_ref, sems.at[0]),
+        pltpu.make_async_copy(wout_hbm, wout_ref, sems.at[1]),
+    ]
+    for copy in copies:
+        copy.start()
 
     def tile(t, carry):
         at = tile_at(t)
@@ -84,6 +120,8 @@
         return carry
 
     lax.fori_loop(0, channels // LANES, tile, 0)
+    for copy in copies:
+        copy.wait()
 
 
 def gelu_tanh(values):
@@ -105,12 +143,20 @@
 
 
 def forward_body(
-    part_ref, before_ref, after_ref, kw_ref, x_ref, win_ref, wout_ref,
-    sums_ref, normed_ref, inv_ref, hid_ref, conv_ref, cast_ref,
+    part_ref, below_ref, above_ref, kw_ref, x_ref, win_ref, wout_ref,
+    sums_ref, normed_ref, inv_ref, hid_ref, before_ref, after_ref, conv_ref, cast_ref,
 ):
     images, rows, cols, channels = x_ref.shape
     hidden_units = win_ref.shape[1]
     pixels = rows * cols
+    place = lax.axis_index("space")
+    zeros = jnp.zeros((cols, channels), BF)
+    for b in range(images):
+        for q in range(SIDE):
+            before_ref[b, q] = jnp.where(place > 0, below_ref[b, q], zeros)
+            after_ref[b, q] = jnp.where(
+                place < lax.axis_size("space") - 1, above_ref[b, q], zeros
+            )
 
     def tile(t, carry):
         at = tile_at(t)
@@ -349,8 +395,25 @@
                 out_ref[i, :, at] = wide_ref[pl.ds((t * TAPS + i) * TAPS, TAPS), :]
 
 
-def flip(array, axis, bit):
-    return lax.ppermute(array, axis, [(i, i ^ bit) for i in range(lax.axis_size(axis))])
+def shifted(array, axis, stride, step, size=4):
+    pairs = []
+    for i in range(lax.axis_size(axis)):
+        place = i // stride % size
+        pairs.append((i, i + ((place + step) % size - place) * stride))
+    return lax.ppermute(array, axis, pairs)
+
+
+def flip(array, axis, mask):
+    return lax.ppermute(array, axis, [(i, i ^ mask) for i in range(lax.axis_size(axis))])
+
+
+def groups(size, stride):
+    listed = []
+    while stride < size:
+        members = 4 if size // stride % 4 == 0 else 2
+        listed.append((stride, members))
+        stride *= members
+    return listed
 
 
 def bits(axis):
@@ -371,43 +434,68 @@
     return lax.reduce_precision(values, 8, 7).astype(BF)
 
 
+def group_sum(mine, axis, stride, members):
+    if members == 2:
+        return mine.astype(F32) + flip(mine, axis, stride).astype(F32)
+    one, two, three = [shifted(mine, axis, stride, k).astype(F32) for k in (1, 2, 3)]
+    return (mine.astype(F32) + two) + (one + three)
+
+
 def per_device(scenes, kernel, weight_in, weight_out, captions, positives):
     images, rows, cols, channels = scenes.shape
     hidden_units = weight_in.shape[1]
     space_count = lax.axis_size("space")
     pixels = images * rows * cols
     scene_pixels = rows * space_count * cols
-
-    up = [(i, i + 1) for i in range(space_count - 1)]
-    down = [(j, i) for i, j in up]
-    before = lax.ppermute(scenes[:, rows - SIDE :], "space", up)
-    after = lax.ppermute(scenes[:, :SIDE], "space", down)
-    macs = 2 * TAPS * TAPS * pixels * channels
-    part, spread = call(
-        conv_body,
-        [((images, rows, cols, channels), F32), ((TAPS * TAPS, cols, channels), F32)],
+    edge = (images, SIDE, cols, channels)
+
+    x, first, last, spread = call(
+        load_body,
+        [
+            (scenes.shape, BF),
+            (edge, BF),
+            (edge, BF),
+            ((TAPS * TAPS, cols, channels), F32),
+        ],
         [scenes, kernel],
-        flops=macs,
-    )
+        scratch=[pltpu.VMEM(kernel.shape, BF), pltpu.SemaphoreType.DMA((4,))],
+        hbm=(0, 1),
+    )
+    below = shifted(last, "space", 1, 1, space_count)
+    above = shifted(first, "space", 1, space_count - 1, space_count)
     gathered = captions
     for bit in bits("dp"):
         gathered = join(gathered, flip(gathered, "dp", bit), "dp", bit)
-
-    sums, normed, inv, hidden = call(
+    part, win, wout = call(
+        conv_body,
+        [
+            (scenes.shape, F32),
+            (weight_in.shape, BF),
+            (weight_out.shape, BF),
+        ],
+        [x, spread, weight_in, weight_out],
+        scratch=[pltpu.SemaphoreType.DMA((2,))],
+        hbm=(2, 3),
+        micros=2.3,
+    )
+
+    sums, normed, inv, hidden, before, after = call(
         forward_body,
         [
             ((images, channels), F32),
             ((pixels, channels), F32),
             ((pixels, LANES), F32),
             ((pixels, hidden_units), F32),
+            (edge, BF),
+            (edge, BF),
         ],
-        [part, before, after, spread, scenes, weight_in, weight_out],
+        [part, below, above, spread, x, win, wout],
         scratch=[pltpu.VMEM((pixels, channels), F32), pltpu.VMEM((pixels, channels), BF)],
-        flops=2 * pixels * channels * hidden_units,
-    )
-    for bit in bits("space"):
-        sums = sums + flip(sums, "space", bit)
-    (slope,) = call(slope_body, [((pixels, hidden_units), F32)], [hidden], flops=1000000)
+        micros=3,
+    )
+    for stride, members in groups(space_count, 1):
+        sums = group_sum(sums, "space", stride, members)
+    (slope,) = call(slope_body, [((pixels, hidden_units), F32)], [hidden], micros=0.8)
 
     listed = channels // LANES // 2 * TAPS * TAPS
     listed += -listed % 16
@@ -416,35 +504,43 @@
     grad, pay = call(
         functools.partial(backward_body, scene_pixels),
         [((pixels, channels), F32), ((listed + own_rows, LANES), BF)],
-        [sums, gathered, positives, slope, normed, inv, weight_in, weight_out, scenes, before, after],
+        [sums, gathered, positives, slope, normed, inv, win, wout, x, before, after],
         scratch=[
             pltpu.VMEM((listed, LANES), F32),
             pltpu.VMEM((pixels, hidden_units), BF),
             pltpu.VMEM((own_rows, LANES), F32),
         ],
         smem=(2,),
-        flops=macs,
+        micros=4,
     )
     other = flip(pay, "dp", 1)
     (own,) = call(
-        own_half_body, [((listed, LANES), F32)], [grad, scenes, before, after], flops=macs // 2
+        own_half_body, [((listed, LANES), F32)], [grad, x, before, after], micros=1.6
     )
     total = own + other[:listed].astype(F32)
     units = join(pay[listed:], other[listed:], "dp", 1)
-    for bit in bits("dp")[1:]:
+    for stride, members in groups(lax.axis_size("dp"), 2):
         mine = rounded(total)
-        other = flip(jnp.concatenate([mine, units], axis=0), "dp", bit)
-        total = mine.astype(F32) + other[:listed].astype(F32)
-        units = join(units, other[listed:], "dp", bit)
+        both = jnp.concatenate([mine, units], axis=0)
+        near = flip(both, "dp", stride)
+        total = mine.astype(F32) + near[:listed].astype(F32)
+        joined = join(units, near[listed:], "dp", stride)
+        if members == 4:
+            far = flip(both, "dp", 2 * stride)
+            cross = flip(both, "dp", 3 * stride)
+            total = total + (far[:listed].astype(F32) + cross[:listed].astype(F32))
+            joined = join(
+                joined, join(far[listed:], cross[listed:], "dp", stride), "dp", 2 * stride
+            )
+        units = joined
     text_grad, loss = call(
         text_body,
         [((images, channels), F32), ((1, 1), F32)],
         [units, captions],
         scratch=[pltpu.VMEM(units.shape, F32)],
     )
-    for bit in bits("space"):
-        mine = rounded(total)
-        total = mine.astype(F32) + flip(mine, "space", bit).astype(F32)
+    for stride, members in groups(space_count, 1):
+        total = group_sum(rounded(total), "space", stride, members)
     mine = rounded(total)
     other = flip(mine, "dp", 1)
     (kernel_grad,) = call(

time: 61.9 us -> 57.6 us (0.931)
  waiting for transfers between devices: 16 us -> 8.91 us
  starting transfers between devices: 20 us -> 21.7 us
  Pallas kernels: 11.7 us -> 13.1 us
    ppermute x13 -> x16, waiting for transfers between devices: 16 us -> 8.91 us  [the longest x8 4.66 us: shifted(): return lax.ppermute(array, axis, pairs)]
    ppermute x13 -> x16, starting transfers between devices: 20 us -> 21.7 us  [the longest x8 13 us: shifted(): return lax.ppermute(array, axis, pairs)]
    pallas_call x7 -> x8, Pallas kernels: 11.7 us -> 13.1 us  [call(): pl.pallas_call(body, out_shape=[vmem_out(shape, dtype) for shape, dtype i...]
    slice x3, local copies, waits for them, and re-layouts: 0.93 us -> 0.01 us  [the longest x1 0.01 us: per_device(): far[listed:]]
    unnamed x24 -> x22, local copies, waits for them, and re-layouts: 9.75 us -> 10.6 us
  transfers between devices with their start and end apart: 13 -> 16, of which waited for: 7 -> 9; matrix products, arithmetic and copies ran while one was open for 3% -> 1% of each run, Pallas kernels for 12% -> 11%
where the time goes in v2:
time: 57.6 us; the launch traced here: 57.3 us
  starting transfers between devices  21.7 us (38%)
  Pallas kernels  13.1 us (23%)
  local copies, waits for them, and re-layouts  10.6 us (18%)
  waiting for transfers between devices  8.91 us (15%)
  between operations  2.04 us (4%)
  other arithmetic  0.92 us (2%)
    pallas_call x8, Pallas kernels, call(): pl.pallas_call(body, out_shape=[vmem_out(shape, dtype) for shape, dtype i...  13.1 us
    ppermute x8, starting transfers between devices, shifted(): return lax.ppermute(array, axis, pairs)  13 us
    unnamed x22, local copies, waits for them, and re-layouts  10.6 us
    ppermute x8, starting transfers between devices, flip(): lax.ppermute(array, axis, [(i, i ^ mask) for i in range(lax.axis_size(axi...  8.69 us
    ppermute x8, waiting for transfers between devices, shifted(): return lax.ppermute(array, axis, pairs)  4.66 us
    ppermute x8, waiting for transfers between devices, flip(): lax.ppermute(array, axis, [(i, i ^ mask) for i in range(lax.axis_size(axi...  4.25 us
  transfers between devices with their start and end apart: 16, of which 9 were waited for; matrix products, arithmetic and copies ran while one was open for 1% of the time, Pallas kernels for 11%

profile of v2, /device:TPU:0, one launch (start us, length us, event | category | flops | bytes accessed | tf_op | source)
XLA Modules:
  0.0 57.3 jit_solution(4726495056068544697)
XLA Ops:
  0.6 0.5 collective-permute-start.5
  1.1 1.0 %collective-permute-done.5 = bf16[2,768]{1,0:T(2,128)(2,1)S(1)} collective-permute-done((bf16[2,768]{1,0:T(2,128)(2,1)}, bf16[2,768]{1,0:T(2,128)(2,1)S(1)}, u32[]{:S(2)}, u32[]{:S(2)}) %collective-permute-start.5) | collective-permute-done | bytes 3104 | tf_op jit(solution)/shard_map/ppermute | solution.py:407
  2.2 0.8 %maximum_select_fusion.6 = bf16[4,768]{1,0:T(4,128)(2,1)S(1)} fusion(bf16[2,768]{1,0:T(2,128)(2,1)} %caps_ref.1, bf16[2,768]{1,0:T(2,128)(2,1)S(1)} %collective-permute-done.5, pred[]{:T(512)S(6)} %eq.15), kind=kLoop, calls=%fused_computation.10 | loop fusion | flops 27648 | bytes 12289 | tf_op jit(solution)/shard_map/jit(_where)/select_n | solution.py:426
  3.0 2.9 %collective-permute-start.6 = (bf16[4,768]{1,0:T(4,128)(2,1)S(1)}, bf16[4,768]{1,0:T(4,128)(2,1)S(1)}, u32[]{:S(2)}, u32[]{:S(2)}) collective-permute-start(bf16[4,768]{1,0:T(4,128)(2,1)S(1)} %maximum_select_fusion.6), channel_id=1, source_target_pairs={{0,8},{4,12},{8,0},{12,4},{16,24},{20,28},{24,16},{28,20},{1,9},{5... | collective-permute-start | bytes 18440 | tf_op jit(solution)/shard_map/ppermute | solution.py:407
  5.9 1.1 %shard_map.85 = (bf16[2,14,8,768]{3,2,1,0:T(8,128)(2,1)S(1)}, bf16[2,3,8,768]{3,2,1,0:T(8,128)(2,1)S(1)}, bf16[2,3,8,768]{3,2,1,0:T(8,128)(2,1)S(1)}, f32[49,8,768]{2,1,0:T(8,128)S(1)}) custom-call(bf16[2,14,8,768]{3,2,1,0:T(8,128)(2,1)} %x_hbm.1, bf16[7,7,768]{2,1,0:T(8,128)(2,1)} %k_hbm.1), custom_call_target="tpu_custom_call" | custom-call | flops 1150000000 | tf_op jit(solution)/shard_map/pallas_call | solution.py:46
  7.0 0.0 copy-start.4
  7.0 1.0 %copy-done.4 = f32[49,8,768]{2,1,0:T(8,128)} copy-done((f32[49,8,768]{2,1,0:T(8,128)}, f32[49,8,768]{2,1,0:T(8,128)S(1)}, u32[]{:S(2)}) %copy-start.4) | copy-done | bytes 1204248
  8.0 0.0 copy-start.7
  8.0 0.7 %copy-done.7 = bf16[2,14,8,768]{3,2,1,0:T(8,128)(2,1)} copy-done((bf16[2,14,8,768]{3,2,1,0:T(8,128)(2,1)}, bf16[2,14,8,768]{3,2,1,0:T(8,128)(2,1)S(1)}, u32[]{:S(2)}) %copy-start.7) | copy-done | bytes 344088
  8.7 1.6 %collective-permute-start = (bf16[2,3,8,768]{3,2,1,0:T(8,128)(2,1)S(1)}, bf16[2,3,8,768]{3,2,1,0:T(8,128)(2,1)S(1)}, u32[]{:S(2)}, u32[]{:S(2)}) collective-permute-start(bf16[2,3,8,768]{3,2,1,0:T(8,128)(2,1)S(1)} %get-tuple-element.23), channel_id=1, source_target_pairs={{0,1},{1,2},{2,3},{3,0},{4,5},{5,6},{6,7},{7,4},{8,9},{9,10},{10,1... | collective-permute-start | bytes 221192 | tf_op jit(solution)/shard_map/ppermute | solution.py:403
  10.3 2.2 %collective-permute-start.1 = (bf16[2,3,8,768]{3,2,1,0:T(8,128)(2,1)S(1)}, bf16[2,3,8,768]{3,2,1,0:T(8,128)(2,1)S(1)}, u32[]{:S(2)}, u32[]{:S(2)}) collective-permute-start(bf16[2,3,8,768]{3,2,1,0:T(8,128)(2,1)S(1)} %get-tuple-element.24), channel_id=1, source_target_pairs={{0,3},{1,0},{2,1},{3,2},{4,7},{5,4},{6,5},{7,6},{8,11},{9,8},{10,9... | collective-permute-start | bytes 221192 | tf_op jit(solution)/shard_map/ppermute | solution.py:403
  12.6 0.0 collective-permute-done.6
  12.6 1.6 %collective-permute-start.7 = (bf16[8,768]{1,0:T(8,128)(2,1)S(1)}, bf16[8,768]{1,0:T(8,128)(2,1)S(1)}, u32[]{:S(2)}, u32[]{:S(2)}) collective-permute-start(bf16[8,768]{1,0:T(8,128)(2,1)S(1)} %maximum_select_fusion.4), channel_id=1, source_target_pairs={{0,16},{4,20},{8,24},{12,28},{16,0},{20,4},{24,8},{28,12},{1,17},{... | collective-permute-start | bytes 36872 | tf_op jit(solution)/shard_map/ppermute | solution.py:407
  14.2 0.0 copy-start.5
  14.2 1.3 %copy-done.5 = f32[49,8,768]{2,1,0:T(8,128)S(1)} copy-done((f32[49,8,768]{2,1,0:T(8,128)S(1)}, f32[49,8,768]{2,1,0:T(8,128)}, u32[]{:S(2)}) %copy-start.5) | copy-done | bytes 1204248
  15.4 0.0 copy-start.8
  15.4 1.0 %copy-done.8 = bf16[2,14,8,768]{3,2,1,0:T(8,128)(2,1)S(1)} copy-done((bf16[2,14,8,768]{3,2,1,0:T(8,128)(2,1)S(1)}, bf16[2,14,8,768]{3,2,1,0:T(8,128)(2,1)}, u32[]{:S(2)}) %copy-start.8) | copy-done | bytes 344088
  16.4 2.4 %shard_map.86 = (f32[2,14,8,768]{3,2,1,0:T(8,128)S(1)}, bf16[768,1536]{1,0:T(8,128)(2,1)S(1)}, bf16[1536,768]{1,0:T(8,128)(2,1)S(1)}) custom-call(bf16[2,14,8,768]{3,2,1,0:T(8,128)(2,1)S(1)} %copy-done.8, f32[49,8,768]{2,1,0:T(8,128)S(1)} %copy-done.5, bf16[768,1536]{1,0:T(8,128)(2,1)} %win_hbm.1, bf16[1536,768]{1,0:T(8,128)(2,1)} %wout_hbm.1), custom_call_target="tpu_custom_call" | custom-call | flops 2644999936 | tf_op jit(solution)/shard_map/pallas_call | solution.py:46
  18.8 0.0 copy-start.2
  18.8 1.4 %copy-done.2 = bf16[1536,768]{1,0:T(8,128)(2,1)} copy-done((bf16[1536,768]{1,0:T(8,128)(2,1)}, bf16[1536,768]{1,0:T(8,128)(2,1)S(1)}, u32[]{:S(2)}) %copy-start.2) | copy-done | bytes 2359320
  20.2 0.0 collective-permute-done.7
  20.3 0.0 collective-permute-done.below_ref
  20.3 0.0 collective-permute-done.1.above_ref
  20.3 0.0 copy-start.3
  20.3 1.7 %copy-done.3 = bf16[1536,768]{1,0:T(8,128)(2,1)S(1)} copy-done((bf16[1536,768]{1,0:T(8,128)(2,1)S(1)}, bf16[1536,768]{1,0:T(8,128)(2,1)}, u32[]{:S(2)}) %copy-start.3) | copy-done | bytes 2359320
  21.9 0.0 copy-start.6
  21.9 1.3 %copy-done.6 = f32[49,8,768]{2,1,0:T(8,128)S(1)} copy-done((f32[49,8,768]{2,1,0:T(8,128)S(1)}, f32[49,8,768]{2,1,0:T(8,128)}, u32[]{:S(2)}) %copy-start.6) | copy-done | bytes 1204248
  23.2 0.0 copy-start.9
  23.2 1.0 %copy-done.9 = bf16[2,14,8,768]{3,2,1,0:T(8,128)(2,1)S(1)} copy-done((bf16[2,14,8,768]{3,2,1,0:T(8,128)(2,1)S(1)}, bf16[2,14,8,768]{3,2,1,0:T(8,128)(2,1)}, u32[]{:S(2)}) %copy-start.9) | copy-done | bytes 344088
  24.2 2.9 %shard_map.87 = (f32[2,768]{1,0:T(2,128)S(1)}, f32[224,768]{1,0:T(8,128)S(1)}, f32[224,128]{1,0:T(8,128)S(1)}, f32[224,1536]{1,0:T(8,128)S(1)}, bf16[2,3,8,768]{...) custom-call(f32[2,14,8,768]{3,2,1,0:T(8,128)S(1)} %get-tuple-element.22.part_ref, ...), custom_call_target="tpu_custom_call" | custom-call | flops 3449999872 | tf_op jit(solution)/shard_map/pallas_call | solution.py:46
  27.1 0.0 copy-start.1
  27.1 0.9 %collective-permute-start.2 = (f32[2,768]{1,0:T(2,128)S(1)}, f32[2,768]{1,0:T(2,128)S(1)}, u32[]{:S(2)}, u32[]{:S(2)}) collective-permute-start(f32[2,768]{1,0:T(2,128)S(1)} %get-tuple-element.27), channel_id=1, source_target_pairs={{0,2},{1,3},{2,0},{3,1},{4,6},{5,7},{6,4},{7,5},{8,10},{9,11},{10,... | collective-permute-start | bytes 18440 | tf_op jit(solution)/shard_map/ppermute | solution.py:403
  27.9 1.6 %collective-permute-start.3 = (f32[2,768]{1,0:T(2,128)S(1)}, f32[2,768]{1,0:T(2,128)S(1)}, u32[]{:S(2)}, u32[]{:S(2)}) collective-permute-start(f32[2,768]{1,0:T(2,128)S(1)} %get-tuple-element.27), channel_id=1, source_target_pairs={{0,1},{1,2},{2,3},{3,0},{4,5},{5,6},{6,7},{7,4},{8,9},{9,10},{10,1... | collective-permute-start | bytes 18440 | tf_op jit(solution)/shard_map/ppermute | solution.py:403
  29.5 2.2 %collective-permute-start.4 = (f32[2,768]{1,0:T(2,128)S(1)}, f32[2,768]{1,0:T(2,128)S(1)}, u32[]{:S(2)}, u32[]{:S(2)}) collective-permute-start(f32[2,768]{1,0:T(2,128)S(1)} %get-tuple-element.27), channel_id=1, source_target_pairs={{0,3},{1,0},{2,1},{3,2},{4,7},{5,4},{6,5},{7,6},{8,11},{9,8},{10,9... | collective-permute-start | bytes 18440 | tf_op jit(solution)/shard_map/ppermute | solution.py:403
  31.8 0.8 %shard_map.88.slope_ref = f32[224,1536]{1,0:T(8,128)S(1)} custom-call(f32[224,1536]{1,0:T(8,128)S(1)} %get-tuple-element.28.hid_ref), custom_call_target="tpu_custom_call" | custom-call | flops 920000000 | tf_op jit(solution)/shard_map/pallas_call | solution.py:46
  32.6 0.0 collective-permute-done.2
  32.6 0.8 %collective-permute-done.3 = f32[2,768]{1,0:T(2,128)S(1)} collective-permute-done((f32[2,768]{1,0:T(2,128)S(1)}, f32[2,768]{1,0:T(2,128)S(1)}, u32[]{:S(2)}, u32[]{:S(2)}) %collective-permute-start.3) | collective-permute-done | bytes 6176 | tf_op jit(solution)/shard_map/ppermute | solution.py:403
  33.4 0.0 collective-permute-done.4
  33.4 0.0 copy-done.1
  33.4 4.1 %shard_map.89 = (f32[224,768]{1,0:T(8,128)S(1)}, bf16[176,128]{1,0:T(8,128)(2,1)S(1)}) custom-call(f32[2,768]{1,0:T(2,128)S(1)} %add_add_fusion.total_ref, bf16[16,768]{1,0:T(8,128)(2,1)S(1)} %maximum_select_fusion.1.caps_ref, s32[2]{0:T(128)S(1)} %copy-done.1, f32[224,1536]{1,0:T(8,128)S(1)} %shard_map.88.slope_ref, ...), custom_call_target="tpu_custom_call" | custom-call | flops 4600000000 | tf_op jit(solution)/shard_map/pallas_call | solution.py:46
  37.5 0.1 collective-permute-start.8
  37.6 0.0 copy-start
  37.6 1.5 %shard_map.90 = f32[160,128]{1,0:T(8,128)S(1)} custom-call(f32[224,768]{1,0:T(8,128)S(1)} %get-tuple-element.33.grad_ref, bf16[2,14,8,768]{3,2,1,0:T(8,128)(2,1)S(1)} %copy-done.9, bf16[2,3,8,768]{3,2,1,0:T(8,128)(2,1)S(1)} %get-tuple-element.31.before_ref, bf16[2,3,8,768]{3,2,1,0:T(8,128)(2,1)S(1)} %get-tuple-element.32.after_ref), custom_call_target="tpu_custom_call" | custom-call | flops 1840000000 | tf_op jit(solution)/shard_map/pallas_call | solution.py:46
  39.1 0.0 collective-permute-done.8
  39.2 0.6 collective-permute-start.10
  39.8 0.5 collective-permute-start.11
  40.3 2.4 %collective-permute-start.9 = (bf16[192,128]{1,0:T(8,128)(2,1)S(1)}, bf16[192,128]{1,0:T(8,128)(2,1)S(1)}, u32[]{:S(2)}, u32[]{:S(2)}) collective-permute-start(bf16[192,128]{1,0:T(8,128)(2,1)S(1)} %pad_maximum_fusion), channel_id=1, source_target_pairs={{0,24},{4,28},{8,16},{12,20},{16,8},{20,12},{24,0},{28,4},{1,25},{... | collective-permute-start | bytes 147464 | tf_op jit(solution)/shard_map/ppermute | solution.py:407
  42.8 0.6 %collective-permute-done.10 = bf16[192,128]{1,0:T(8,128)(2,1)S(1)} collective-permute-done((bf16[192,128]{1,0:T(8,128)(2,1)S(1)}, bf16[192,128]{1,0:T(8,128)(2,1)S(1)}, u32[]{:S(2)}, u32[]{:S(2)}) %collective-permute-start.10) | collective-permute-done | bytes 49184 | tf_op jit(solution)/shard_map/ppermute | solution.py:407
  43.4 0.6 %collective-permute-done.11 = bf16[192,128]{1,0:T(8,128)(2,1)S(1)} collective-permute-done((bf16[192,128]{1,0:T(8,128)(2,1)S(1)}, bf16[192,128]{1,0:T(8,128)(2,1)S(1)}, u32[]{:S(2)}, u32[]{:S(2)}) %collective-permute-start.11) | collective-permute-done | bytes 49184 | tf_op jit(solution)/shard_map/ppermute | solution.py:407
  44.0 1.6 %collective-permute-done.9 = bf16[192,128]{1,0:T(8,128)(2,1)S(1)} collective-permute-done((bf16[192,128]{1,0:T(8,128)(2,1)S(1)}, bf16[192,128]{1,0:T(8,128)(2,1)S(1)}, u32[]{:S(2)}, u32[]{:S(2)}) %collective-permute-start.9) | collective-permute-done | bytes 49184 | tf_op jit(solution)/shard_map/ppermute | solution.py:407
  45.7 0.7 %collective-permute-start.12 = (bf16[160,128]{1,0:T(8,128)(2,1)S(1)}, bf16[160,128]{1,0:T(8,128)(2,1)S(1)}, u32[]{:S(2)}, u32[]{:S(2)}) collective-permute-start(bf16[160,128]{1,0:T(8,128)(2,1)S(1)} %reduce-precision_convert_fusion.1), channel_id=1, source_target_pairs={{0,2},{1,3},{2,0},{3,1},{4,6},{5,7},{6,4},{7,5},{8,10},{9,11},{10,... | collective-permute-start | bytes 122888 | tf_op jit(solution)/shard_map/ppermute | solution.py:403
  46.4 3.8 %collective-permute-start.13 = (bf16[160,128]{1,0:T(8,128)(2,1)S(1)}, bf16[160,128]{1,0:T(8,128)(2,1)S(1)}, u32[]{:S(2)}, u32[]{:S(2)}) collective-permute-start(bf16[160,128]{1,0:T(8,128)(2,1)S(1)} %reduce-precision_convert_fusion.1), channel_id=1, source_target_pairs={{0,1},{1,2},{2,3},{3,0},{4,5},{5,6},{6,7},{7,4},{8,9},{9,10},{10,1... | collective-permute-start | bytes 122888 | tf_op jit(solution)/shard_map/ppermute | solution.py:403
  50.1 0.1 collective-permute-start.14
  50.3 0.5 collective-permute-done.12
  50.8 1.5 %collective-permute-done.13 = bf16[160,128]{1,0:T(8,128)(2,1)S(1)} collective-permute-done((bf16[160,128]{1,0:T(8,128)(2,1)S(1)}, bf16[160,128]{1,0:T(8,128)(2,1)S(1)}, u32[]{:S(2)}, u32[]{:S(2)}) %collective-permute-start.13) | collective-permute-done | bytes 40992 | tf_op jit(solution)/shard_map/ppermute | solution.py:403
  52.3 1.8 %collective-permute-done.14 = bf16[160,128]{1,0:T(8,128)(2,1)S(1)} collective-permute-done((bf16[160,128]{1,0:T(8,128)(2,1)S(1)}, bf16[160,128]{1,0:T(8,128)(2,1)S(1)}, u32[]{:S(2)}, u32[]{:S(2)}) %collective-permute-start.14) | collective-permute-done | bytes 40992 | tf_op jit(solution)/shard_map/ppermute | solution.py:403
  54.1 0.1 collective-permute-start.15
  54.2 0.0 copy-done
  54.2 0.2 shard_map.91
  54.5 0.6 %copy.10 = f32[2,768]{1,0:T(2,128)} copy(f32[2,768]{1,0:T(2,128)S(1)} %get-tuple-element.38) | data formatting | bytes 12288
  55.1 0.3 collective-permute-done.15.other_ref
  55.5 0.7 %copy.11 = f32[7,7,768]{2,1,0:T(8,128)} copy(f32[7,7,768]{2,1,0:T(8,128)S(1)} %shard_map.92) | data formatting | bytes 301056
  (17 shorter events, 0.2 us)
Async XLA Ops:
  0.6 1.6 %collective-permute-start.5 = (bf16[2,768]{1,0:T(2,128)(2,1)}, bf16[2,768]{1,0:T(2,128)(2,1)S(1)}, u32[]{:S(2)}, u32[]{:S(2)}) collective-permute-start(bf16[2,768]{1,0:T(2,128)(2,1)} %caps_ref.1), channel_id=1, source_target_pairs={{0,4},{4,0},{8,12},{12,8},{16,20},{20,16},{24,28},{28,24},{1,5},{5... | collective-permute-start | bytes 9224 | tf_op jit(solution)/shard_map/ppermute | solution.py:407
  3.0 9.6 %collective-permute-start.6 = (bf16[4,768]{1,0:T(4,128)(2,1)S(1)}, bf16[4,768]{1,0:T(4,128)(2,1)S(1)}, u32[]{:S(2)}, u32[]{:S(2)}) collective-permute-start(bf16[4,768]{1,0:T(4,128)(2,1)S(1)} %maximum_select_fusion.6), channel_id=1, source_target_pairs={{0,8},{4,12},{8,0},{12,4},{16,24},{20,28},{24,16},{28,20},{1,9},{5... | collective-permute-start | bytes 18440 | tf_op jit(solution)/shard_map/ppermute | solution.py:407
  7.0 1.0 %copy-start.4 = (f32[49,8,768]{2,1,0:T(8,128)}, f32[49,8,768]{2,1,0:T(8,128)S(1)}, u32[]{:S(2)}) copy-start(f32[49,8,768]{2,1,0:T(8,128)S(1)} %get-tuple-element.21.kw_ref) | copy-start | bytes 3612676
  8.0 0.7 %copy-start.7 = (bf16[2,14,8,768]{3,2,1,0:T(8,128)(2,1)}, bf16[2,14,8,768]{3,2,1,0:T(8,128)(2,1)S(1)}, u32[]{:S(2)}) copy-start(bf16[2,14,8,768]{3,2,1,0:T(8,128)(2,1)S(1)} %get-tuple-element.20.x_ref) | copy-start | bytes 1032196
  8.7 11.5 %collective-permute-start = (bf16[2,3,8,768]{3,2,1,0:T(8,128)(2,1)S(1)}, bf16[2,3,8,768]{3,2,1,0:T(8,128)(2,1)S(1)}, u32[]{:S(2)}, u32[]{:S(2)}) collective-permute-start(bf16[2,3,8,768]{3,2,1,0:T(8,128)(2,1)S(1)} %get-tuple-element.23), channel_id=1, source_target_pairs={{0,1},{1,2},{2,3},{3,0},{4,5},{5,6},{6,7},{7,4},{8,9},{9,10},{10,1... | collective-permute-start | bytes 221192 | tf_op jit(solution)/shard_map/ppermute | solution.py:403
  10.3 10.0 %collective-permute-start.1 = (bf16[2,3,8,768]{3,2,1,0:T(8,128)(2,1)S(1)}, bf16[2,3,8,768]{3,2,1,0:T(8,128)(2,1)S(1)}, u32[]{:S(2)}, u32[]{:S(2)}) collective-permute-start(bf16[2,3,8,768]{3,2,1,0:T(8,128)(2,1)S(1)} %get-tuple-element.24), channel_id=1, source_target_pairs={{0,3},{1,0},{2,1},{3,2},{4,7},{5,4},{6,5},{7,6},{8,11},{9,8},{10,9... | collective-permute-start | bytes 221192 | tf_op jit(solution)/shard_map/ppermute | solution.py:403
  12.6 7.7 %collective-permute-start.7 = (bf16[8,768]{1,0:T(8,128)(2,1)S(1)}, bf16[8,768]{1,0:T(8,128)(2,1)S(1)}, u32[]{:S(2)}, u32[]{:S(2)}) collective-permute-start(bf16[8,768]{1,0:T(8,128)(2,1)S(1)} %maximum_select_fusion.4), channel_id=1, source_target_pairs={{0,16},{4,20},{8,24},{12,28},{16,0},{20,4},{24,8},{28,12},{1,17},{... | collective-permute-start | bytes 36872 | tf_op jit(solution)/shard_map/ppermute | solution.py:407
  14.2 1.3 %copy-start.5 = (f32[49,8,768]{2,1,0:T(8,128)S(1)}, f32[49,8,768]{2,1,0:T(8,128)}, u32[]{:S(2)}) copy-start(f32[49,8,768]{2,1,0:T(8,128)} %copy-done.4) | copy-start | bytes 3612676
  15.4 1.0 %copy-start.8 = (bf16[2,14,8,768]{3,2,1,0:T(8,128)(2,1)S(1)}, bf16[2,14,8,768]{3,2,1,0:T(8,128)(2,1)}, u32[]{:S(2)}) copy-start(bf16[2,14,8,768]{3,2,1,0:T(8,128)(2,1)} %copy-done.7) | copy-start | bytes 1032196
  18.8 1.4 %copy-start.2 = (bf16[1536,768]{1,0:T(8,128)(2,1)}, bf16[1536,768]{1,0:T(8,128)(2,1)S(1)}, u32[]{:S(2)}) copy-start(bf16[1536,768]{1,0:T(8,128)(2,1)S(1)} %get-tuple-element.26.wout_ref) | copy-start | bytes 7077892
  20.3 1.7 %copy-start.3 = (bf16[1536,768]{1,0:T(8,128)(2,1)S(1)}, bf16[1536,768]{1,0:T(8,128)(2,1)}, u32[]{:S(2)}) copy-start(bf16[1536,768]{1,0:T(8,128)(2,1)} %copy-done.2) | copy-start | bytes 7077892
  21.9 1.3 %copy-start.6 = (f32[49,8,768]{2,1,0:T(8,128)S(1)}, f32[49,8,768]{2,1,0:T(8,128)}, u32[]{:S(2)}) copy-start(f32[49,8,768]{2,1,0:T(8,128)} %copy-done.4) | copy-start | bytes 3612676
  23.2 1.0 %copy-start.9 = (bf16[2,14,8,768]{3,2,1,0:T(8,128)(2,1)S(1)}, bf16[2,14,8,768]{3,2,1,0:T(8,128)(2,1)}, u32[]{:S(2)}) copy-start(bf16[2,14,8,768]{3,2,1,0:T(8,128)(2,1)} %copy-done.7) | copy-start | bytes 1032196
  27.1 6.3 %copy-start.1 = (s32[2]{0:T(128)S(1)}, s32[2]{0:T(128)}, u32[]{:S(2)}) copy-start(s32[2]{0:T(128)} %pos_ref.1) | copy-start | bytes 28
  27.1 5.5 %collective-permute-start.2 = (f32[2,768]{1,0:T(2,128)S(1)}, f32[2,768]{1,0:T(2,128)S(1)}, u32[]{:S(2)}, u32[]{:S(2)}) collective-permute-start(f32[2,768]{1,0:T(2,128)S(1)} %get-tuple-element.27), channel_id=1, source_target_pairs={{0,2},{1,3},{2,0},{3,1},{4,6},{5,7},{6,4},{7,5},{8,10},{9,11},{10,... | collective-permute-start | bytes 18440 | tf_op jit(solution)/shard_map/ppermute | solution.py:403
  27.9 5.4 %collective-permute-start.3 = (f32[2,768]{1,0:T(2,128)S(1)}, f32[2,768]{1,0:T(2,128)S(1)}, u32[]{:S(2)}, u32[]{:S(2)}) collective-permute-start(f32[2,768]{1,0:T(2,128)S(1)} %get-tuple-element.27), channel_id=1, source_target_pairs={{0,1},{1,2},{2,3},{3,0},{4,5},{5,6},{6,7},{7,4},{8,9},{9,10},{10,1... | collective-permute-start | bytes 18440 | tf_op jit(solution)/shard_map/ppermute | solution.py:403
  29.5 3.9 %collective-permute-start.4 = (f32[2,768]{1,0:T(2,128)S(1)}, f32[2,768]{1,0:T(2,128)S(1)}, u32[]{:S(2)}, u32[]{:S(2)}) collective-permute-start(f32[2,768]{1,0:T(2,128)S(1)} %get-tuple-element.27), channel_id=1, source_target_pairs={{0,3},{1,0},{2,1},{3,2},{4,7},{5,4},{6,5},{7,6},{8,11},{9,8},{10,9... | collective-permute-start | bytes 18440 | tf_op jit(solution)/shard_map/ppermute | solution.py:403
  37.5 1.6 %collective-permute-start.8 = (bf16[176,128]{1,0:T(8,128)(2,1)S(1)}, bf16[176,128]{1,0:T(8,128)(2,1)S(1)}, u32[]{:S(2)}, u32[]{:S(2)}) collective-permute-start(bf16[176,128]{1,0:T(8,128)(2,1)S(1)} %get-tuple-element.34), channel_id=1, source_target_pairs={{0,4},{4,0},{8,12},{12,8},{16,20},{20,16},{24,28},{28,24},{1,5},{5... | collective-permute-start | bytes 135176 | tf_op jit(solution)/shard_map/ppermute | solution.py:407
  37.6 16.6 %copy-start = (bf16[2,768]{1,0:T(2,128)(2,1)S(1)}, bf16[2,768]{1,0:T(2,128)(2,1)}, u32[]{:S(2)}) copy-start(bf16[2,768]{1,0:T(2,128)(2,1)} %caps_ref.1) | copy-start | bytes 9220
  39.2 4.2 %collective-permute-start.10 = (bf16[192,128]{1,0:T(8,128)(2,1)S(1)}, bf16[192,128]{1,0:T(8,128)(2,1)S(1)}, u32[]{:S(2)}, u32[]{:S(2)}) collective-permute-start(bf16[192,128]{1,0:T(8,128)(2,1)S(1)} %pad_maximum_fusion), channel_id=1, source_target_pairs={{0,16},{4,20},{8,24},{12,28},{16,0},{20,4},{24,8},{28,12},{1,17},{... | collective-permute-start | bytes 147464 | tf_op jit(solution)/shard_map/ppermute | solution.py:407
  39.8 4.3 %collective-permute-start.11 = (bf16[192,128]{1,0:T(8,128)(2,1)S(1)}, bf16[192,128]{1,0:T(8,128)(2,1)S(1)}, u32[]{:S(2)}, u32[]{:S(2)}) collective-permute-start(bf16[192,128]{1,0:T(8,128)(2,1)S(1)} %pad_maximum_fusion), channel_id=1, source_target_pairs={{0,8},{4,12},{8,0},{12,4},{16,24},{20,28},{24,16},{28,20},{1,9},{5... | collective-permute-start | bytes 147464 | tf_op jit(solution)/shard_map/ppermute | solution.py:407
  40.3 5.3 %collective-permute-start.9 = (bf16[192,128]{1,0:T(8,128)(2,1)S(1)}, bf16[192,128]{1,0:T(8,128)(2,1)S(1)}, u32[]{:S(2)}, u32[]{:S(2)}) collective-permute-start(bf16[192,128]{1,0:T(8,128)(2,1)S(1)} %pad_maximum_fusion), channel_id=1, source_target_pairs={{0,24},{4,28},{8,16},{12,20},{16,8},{20,12},{24,0},{28,4},{1,25},{... | collective-permute-start | bytes 147464 | tf_op jit(solution)/shard_map/ppermute | solution.py:407
  45.7 5.1 %collective-permute-start.12 = (bf16[160,128]{1,0:T(8,128)(2,1)S(1)}, bf16[160,128]{1,0:T(8,128)(2,1)S(1)}, u32[]{:S(2)}, u32[]{:S(2)}) collective-permute-start(bf16[160,128]{1,0:T(8,128)(2,1)S(1)} %reduce-precision_convert_fusion.1), channel_id=1, source_target_pairs={{0,2},{1,3},{2,0},{3,1},{4,6},{5,7},{6,4},{7,5},{8,10},{9,11},{10,... | collective-permute-start | bytes 122888 | tf_op jit(solution)/shard_map/ppermute | solution.py:403
  46.4 6.0 %collective-permute-start.13 = (bf16[160,128]{1,0:T(8,128)(2,1)S(1)}, bf16[160,128]{1,0:T(8,128)(2,1)S(1)}, u32[]{:S(2)}, u32[]{:S(2)}) collective-permute-start(bf16[160,128]{1,0:T(8,128)(2,1)S(1)} %reduce-precision_convert_fusion.1), channel_id=1, source_target_pairs={{0,1},{1,2},{2,3},{3,0},{4,5},{5,6},{6,7},{7,4},{8,9},{9,10},{10,1... | collective-permute-start | bytes 122888 | tf_op jit(solution)/shard_map/ppermute | solution.py:403
  50.1 4.0 %collective-permute-start.14 = (bf16[160,128]{1,0:T(8,128)(2,1)S(1)}, bf16[160,128]{1,0:T(8,128)(2,1)S(1)}, u32[]{:S(2)}, u32[]{:S(2)}) collective-permute-start(bf16[160,128]{1,0:T(8,128)(2,1)S(1)} %reduce-precision_convert_fusion.1), channel_id=1, source_target_pairs={{0,3},{1,0},{2,1},{3,2},{4,7},{5,4},{6,5},{7,6},{8,11},{9,8},{10,9... | collective-permute-start | bytes 122888 | tf_op jit(solution)/shard_map/ppermute | solution.py:403
  54.1 1.3 %collective-permute-start.15 = (bf16[160,128]{1,0:T(8,128)(2,1)S(1)}, bf16[160,128]{1,0:T(8,128)(2,1)S(1)}, u32[]{:S(2)}, u32[]{:S(2)}) collective-permute-start(bf16[160,128]{1,0:T(8,128)(2,1)S(1)} %reduce-precision_convert_fusion.own_ref), channel_id=1, source_target_pairs={{0,4},{4,0},{8,12},{12,8},{16,20},{20,16},{24,28},{28,24},{1,5},{5... | collective-permute-start | bytes 122888 | tf_op jit(solution)/shard_map/ppermute | solution.py:407

commit v3 on v2

--- a/solution.py
+++ b/solution.py
@@ -30,7 +30,7 @@
     return pltpu.with_memory_space_constraint(array, pltpu.HBM)
 
 
-def call(body, outs, args, scratch=(), smem=(), hbm=(), limit=40, micros=1):
+def call(body, outs, args, scratch=(), smem=(), hbm=(), limit=10):
     specs = []
     placed = []
     for k, arg in enumerate(args):
@@ -50,9 +50,7 @@
         out_specs=[pl.BlockSpec(memory_space=pltpu.VMEM) for _ in outs],
         scratch_shapes=list(scratch),
         compiler_params=pltpu.CompilerParams(vmem_limit_bytes=limit * 1024 * 1024),
-        cost_estimate=pl.CostEstimate(
-            flops=int(micros * 1.15e9), bytes_accessed=0, transcendentals=0
-        ),
+        cost_estimate=pl.CostEstimate(flops=0, bytes_accessed=0, transcendentals=0),
     )(*placed)
 
 
@@ -67,13 +65,16 @@
     return pl.ds(pl.multiple_of(t * LANES, LANES), LANES)
 
 
-def load_body(x_hbm, k_hbm, x_ref, first_ref, last_ref, kw_ref, taps_ref, sems):
+def load_body(
+    x_hbm, k_hbm, caps_hbm, x_ref, first_ref, last_ref, kw_ref, caps_ref, taps_ref, sems
+):
     rows, cols, channels = x_hbm.shape[1:]
     copies = [
         pltpu.make_async_copy(k_hbm, taps_ref, sems.at[0]),
         pltpu.make_async_copy(x_hbm.at[:, :SIDE], first_ref, sems.at[1]),
         pltpu.make_async_copy(x_hbm.at[:, rows - SIDE :], last_ref, sems.at[2]),
         pltpu.make_async_copy(x_hbm, x_ref, sems.at[3]),
+        pltpu.make_async_copy(caps_hbm, caps_ref, sems.at[4]),
     ]
     for copy in copies:
         copy.start()
@@ -291,9 +292,12 @@
     positive = jnp.zeros((images, count), jnp.int32)
     for b in range(images):
         positive = jnp.where(row_at == b, pos_ref[b], positive)
-    labels = jnp.where(
-        positive == lax.broadcasted_iota(jnp.int32, (images, count), 1), 1.0, -1.0
-    ).astype(F32)
+    place = lax.broadcasted_iota(jnp.int32, (images, count), 1)
+    core = (place >= count // 2).astype(jnp.int32)
+    rest = place - core * (count // 2)
+    group = rest // images
+    caption = (group * 2 + core) * images + (rest - group * images)
+    labels = jnp.where(positive == caption, 1.0, -1.0).astype(F32)
     margin = -labels * logits
     losses = jnp.maximum(margin, 0.0) + jnp.log(1.0 + jnp.exp(-jnp.abs(margin)))
     loss_part = jnp.sum(jnp.sum(losses, axis=1, keepdims=True), axis=0, keepdims=True)
@@ -355,7 +359,8 @@
     groups = lax.axis_size("dp")
     wide_ref[...] = rows_ref[...].astype(F32)
     lane = lax.broadcasted_iota(jnp.int32, (groups, LANES), 1)
-    first = lax.axis_index("dp") * images
+    me = lax.axis_index("dp")
+    first = (lax.rem(me, 2) * (groups // 2) + me // 2) * images
     caption_side = [[jnp.zeros((1, LANES), F32) for _ in range(chunks)] for _ in range(images)]
     loss = jnp.zeros((1, 1), F32)
     for b in range(images):
@@ -449,23 +454,26 @@
     scene_pixels = rows * space_count * cols
     edge = (images, SIDE, cols, channels)
 
-    x, first, last, spread = call(
+    x, first, last, spread, own_captions = call(
         load_body,
         [
             (scenes.shape, BF),
             (edge, BF),
             (edge, BF),
             ((TAPS * TAPS, cols, channels), F32),
+            (captions.shape, BF),
         ],
-        [scenes, kernel],
-        scratch=[pltpu.VMEM(kernel.shape, BF), pltpu.SemaphoreType.DMA((4,))],
-        hbm=(0, 1),
+        [scenes, kernel, captions],
+        scratch=[pltpu.VMEM(kernel.shape, BF), pltpu.SemaphoreType.DMA((5,))],
+        hbm=(0, 1, 2),
     )
     below = shifted(last, "space", 1, 1, space_count)
     above = shifted(first, "space", 1, space_count - 1, space_count)
-    gathered = captions
-    for bit in bits("dp"):
-        gathered = join(gathered, flip(gathered, "dp", bit), "dp", bit)
+    theirs = captions
+    gathered = own_captions
+    for bit in bits("dp")[1:] + [1]:
+        theirs = flip(theirs, "dp", bit)
+        gathered = theirs = join(gathered, theirs, "dp", bit)
     part, win, wout = call(
         conv_body,
         [
@@ -476,7 +484,6 @@
         [x, spread, weight_in, weight_out],
         scratch=[pltpu.SemaphoreType.DMA((2,))],
         hbm=(2, 3),
-        micros=2.3,
     )
 
     sums, normed, inv, hidden, before, after = call(
@@ -491,11 +498,10 @@
         ],
         [part, below, above, spread, x, win, wout],
         scratch=[pltpu.VMEM((pixels, channels), F32), pltpu.VMEM((pixels, channels), BF)],
-        micros=3,
     )
     for stride, members in groups(space_count, 1):
         sums = group_sum(sums, "space", stride, members)
-    (slope,) = call(slope_body, [((pixels, hidden_units), F32)], [hidden], micros=0.8)
+    (slope,) = call(slope_body, [((pixels, hidden_units), F32)], [hidden])
 
     listed = channels // LANES // 2 * TAPS * TAPS
     listed += -listed % 16
@@ -511,11 +517,10 @@
             pltpu.VMEM((own_rows, LANES), F32),
         ],
         smem=(2,),
-        micros=4,
     )
     other = flip(pay, "dp", 1)
     (own,) = call(
-        own_half_body, [((listed, LANES), F32)], [grad, x, before, after], micros=1.6
+        own_half_body, [((listed, LANES), F32)], [grad, x, before, after]
     )
     total = own + other[:listed].astype(F32)
     units = join(pay[listed:], other[listed:], "dp", 1)
@@ -536,7 +541,7 @@
     text_grad, loss = call(
         text_body,
         [((images, channels), F32), ((1, 1), F32)],
-        [units, captions],
+        [units, own_captions],
         scratch=[pltpu.VMEM(units.shape, F32)],
     )
     for stride, members in groups(space_count, 1):

time: 57.6 us -> 49.6 us (0.86)
  local copies, waits for them, and re-layouts: 10.6 us -> 1.29 us
  waiting for transfers between devices: 8.91 us -> 14.2 us
  starting transfers between devices: 21.7 us -> 18.7 us
  other arithmetic: 0.92 us -> 0.16 us
    unnamed x22 -> x4, local copies, waits for them, and re-layouts: 10.6 us -> 1.27 us
    ppermute x8, waiting for transfers between devices: 4.66 us -> 9.74 us  [shifted(): return lax.ppermute(array, axis, pairs)]
    ppermute x8, starting transfers between devices: 13 us -> 9.85 us  [shifted(): return lax.ppermute(array, axis, pairs)]
    select_n x7, other arithmetic: 0.84 us -> 0.08 us  [join(): jnp.where(upper, jnp.concatenate([theirs, mine], axis=0), jnp.concatenate...]
  transfers between devices with their start and end apart: 16 -> 16, of which waited for: 9 -> 11; matrix products, arithmetic and copies ran while one was open for 1% -> 1% of each run, Pallas kernels for 11% -> 18%
where the time goes in v3:
time: 49.6 us; the launch traced here: 49.5 us
  starting transfers between devices  18.7 us (38%)
  waiting for transfers between devices  14.2 us (29%)
  Pallas kernels  13.1 us (26%)
  between operations  1.99 us (4%)
  local copies, waits for them, and re-layouts  1.29 us (3%)
    pallas_call x8, Pallas kernels, call(): pl.pallas_call(body, out_shape=[vmem_out(shape, dtype) for shape, dtype i...  13.1 us
    ppermute x8, starting transfers between devices, shifted(): return lax.ppermute(array, axis, pairs)  9.85 us
    ppermute x8, waiting for transfers between devices, shifted(): return lax.ppermute(array, axis, pairs)  9.74 us
    ppermute x8, starting transfers between devices, flip(): lax.ppermute(array, axis, [(i, i ^ mask) for i in range(lax.axis_size(axi...  8.88 us
    ppermute x8, waiting for transfers between devices, flip(): lax.ppermute(array, axis, [(i, i ^ mask) for i in range(lax.axis_size(axi...  4.46 us
    unnamed x4, local copies, waits for them, and re-layouts  1.27 us
  transfers between devices with their start and end apart: 16, of which 11 were waited for; matrix products, arithmetic and copies ran while one was open for 1% of the time, Pallas kernels for 18%

profile of v3, /device:TPU:0, one launch (start us, length us, event | category | flops | bytes accessed | tf_op | source)
XLA Modules:
  0.0 49.5 jit_solution(10942899611564980411)
XLA Ops:
  0.6 3.0 %collective-permute-start.5 = (bf16[2,768]{1,0:T(2,128)(2,1)}, bf16[2,768]{1,0:T(2,128)(2,1)S(1)}, u32[]{:S(2)}, u32[]{:S(2)}) collective-permute-start(bf16[2,768]{1,0:T(2,128)(2,1)} %caps_hbm.1), channel_id=1, source_target_pairs={{0,8},{4,12},{8,0},{12,4},{16,24},{20,28},{24,16},{28,20},{1,9},{5... | collective-permute-start | bytes 9224 | tf_op jit(solution)/shard_map/ppermute | solution.py:412
  3.6 1.1 %shard_map.85 = (bf16[2,14,8,768]{3,2,1,0:T(8,128)(2,1)S(1)}, bf16[2,3,8,768]{3,2,1,0:T(8,128)(2,1)S(1)}, bf16[2,3,8,768]{3,2,1,0:T(8,128)(2,1)S(1)}, f32[49,8,768]{2,1,0:T(8,128)S(1)}, bf16[2,768]{1,0:T(2,128)(2,1)S(1)}) custom-call(bf16[2,14,8,768]{3,2,1,0:T(8,128)(2,1)} %x_hbm.1, bf16[7,7,768]{2,1,0:T(8,128)(2,1)} %k_hbm.1, bf16[2,768]{1,0:T(2,128)(2,1)} %caps_hbm.1), custom_call_target="tpu_custom_call" | custom-call | tf_op jit(solution)/shard_map/pallas_call | solution.py:46
  4.8 0.6 %collective-permute-done.5 = bf16[2,768]{1,0:T(2,128)(2,1)S(1)} collective-permute-done((bf16[2,768]{1,0:T(2,128)(2,1)}, bf16[2,768]{1,0:T(2,128)(2,1)S(1)}, u32[]{:S(2)}, u32[]{:S(2)}) %collective-permute-start.5) | collective-permute-done | bytes 3104 | tf_op jit(solution)/shard_map/ppermute | solution.py:412
  5.4 2.1 %collective-permute-start.6 = (bf16[4,768]{1,0:T(4,128)(2,1)S(1)}, bf16[4,768]{1,0:T(4,128)(2,1)S(1)}, u32[]{:S(2)}, u32[]{:S(2)}) collective-permute-start(bf16[4,768]{1,0:T(4,128)(2,1)S(1)} %maximum_select_fusion.6), channel_id=1, source_target_pairs={{0,16},{4,20},{8,24},{12,28},{16,0},{20,4},{24,8},{28,12},{1,17},{... | collective-permute-start | bytes 18440 | tf_op jit(solution)/shard_map/ppermute | solution.py:412
  7.6 1.6 %collective-permute-start = (bf16[2,3,8,768]{3,2,1,0:T(8,128)(2,1)S(1)}, bf16[2,3,8,768]{3,2,1,0:T(8,128)(2,1)S(1)}, u32[]{:S(2)}, u32[]{:S(2)}) collective-permute-start(bf16[2,3,8,768]{3,2,1,0:T(8,128)(2,1)S(1)} %get-tuple-element.24), channel_id=1, source_target_pairs={{0,1},{1,2},{2,3},{3,0},{4,5},{5,6},{6,7},{7,4},{8,9},{9,10},{10,1... | collective-permute-start | bytes 221192 | tf_op jit(solution)/shard_map/ppermute | solution.py:408
  9.1 2.2 %collective-permute-start.1 = (bf16[2,3,8,768]{3,2,1,0:T(8,128)(2,1)S(1)}, bf16[2,3,8,768]{3,2,1,0:T(8,128)(2,1)S(1)}, u32[]{:S(2)}, u32[]{:S(2)}) collective-permute-start(bf16[2,3,8,768]{3,2,1,0:T(8,128)(2,1)S(1)} %get-tuple-element.25), channel_id=1, source_target_pairs={{0,3},{1,0},{2,1},{3,2},{4,7},{5,4},{6,5},{7,6},{8,11},{9,8},{10,9... | collective-permute-start | bytes 221192 | tf_op jit(solution)/shard_map/ppermute | solution.py:408
  11.4 0.0 collective-permute-done.6
  11.4 0.1 collective-permute-start.7
  11.5 2.4 %shard_map.86 = (f32[2,14,8,768]{3,2,1,0:T(8,128)S(1)}, bf16[768,1536]{1,0:T(8,128)(2,1)S(1)}, bf16[1536,768]{1,0:T(8,128)(2,1)S(1)}) custom-call(bf16[2,14,8,768]{3,2,1,0:T(8,128)(2,1)S(1)} %get-tuple-element.21.x_ref, f32[49,8,768]{2,1,0:T(8,128)S(1)} %get-tuple-element.22.kw_ref, bf16[768,1536]{1,0:T(8,128)(2,1)} %win_hbm.1, bf16[1536,768]{1,0:T(8,128)(2,1)} %wout_hbm.1), custom_call_target="tpu_custom_call" | custom-call | tf_op jit(solution)/shard_map/pallas_call | solution.py:46
  13.9 0.0 collective-permute-done.below_ref
  13.9 0.4 collective-permute-done.1.above_ref
  14.3 2.9 %shard_map.87 = (f32[2,768]{1,0:T(2,128)S(1)}, f32[224,768]{1,0:T(8,128)S(1)}, f32[224,128]{1,0:T(8,128)S(1)}, f32[224,1536]{1,0:T(8,128)S(1)}, bf16[2,3,8,768]{...) custom-call(f32[2,14,8,768]{3,2,1,0:T(8,128)S(1)} %get-tuple-element.23.part_ref, ...), custom_call_target="tpu_custom_call" | custom-call | tf_op jit(solution)/shard_map/pallas_call | solution.py:46
  17.2 0.0 copy-start
  17.2 0.8 %collective-permute-start.3 = (f32[2,768]{1,0:T(2,128)S(1)}, f32[2,768]{1,0:T(2,128)S(1)}, u32[]{:S(2)}, u32[]{:S(2)}) collective-permute-start(f32[2,768]{1,0:T(2,128)S(1)} %get-tuple-element.28), channel_id=1, source_target_pairs={{0,1},{1,2},{2,3},{3,0},{4,5},{5,6},{6,7},{7,4},{8,9},{9,10},{10,1... | collective-permute-start | bytes 18440 | tf_op jit(solution)/shard_map/ppermute | solution.py:408
  18.0 3.0 %collective-permute-start.4 = (f32[2,768]{1,0:T(2,128)S(1)}, f32[2,768]{1,0:T(2,128)S(1)}, u32[]{:S(2)}, u32[]{:S(2)}) collective-permute-start(f32[2,768]{1,0:T(2,128)S(1)} %get-tuple-element.28), channel_id=1, source_target_pairs={{0,3},{1,0},{2,1},{3,2},{4,7},{5,4},{6,5},{7,6},{8,11},{9,8},{10,9... | collective-permute-start | bytes 18440 | tf_op jit(solution)/shard_map/ppermute | solution.py:408
  21.0 0.0 collective-permute-start.2
  21.0 0.0 collective-permute-done.7
  21.1 0.8 %shard_map.88.slope_ref = f32[224,1536]{1,0:T(8,128)S(1)} custom-call(f32[224,1536]{1,0:T(8,128)S(1)} %get-tuple-element.30.hid_ref), custom_call_target="tpu_custom_call" | custom-call | tf_op jit(solution)/shard_map/pallas_call | solution.py:46
  21.9 0.8 %collective-permute-done.3 = f32[2,768]{1,0:T(2,128)S(1)} collective-permute-done((f32[2,768]{1,0:T(2,128)S(1)}, f32[2,768]{1,0:T(2,128)S(1)}, u32[]{:S(2)}, u32[]{:S(2)}) %collective-permute-start.3) | collective-permute-done | bytes 6176 | tf_op jit(solution)/shard_map/ppermute | solution.py:408
  22.7 0.0 collective-permute-done.4
  22.7 2.9 %collective-permute-done.2 = f32[2,768]{1,0:T(2,128)S(1)} collective-permute-done((f32[2,768]{1,0:T(2,128)S(1)}, f32[2,768]{1,0:T(2,128)S(1)}, u32[]{:S(2)}, u32[]{:S(2)}) %collective-permute-start.2) | collective-permute-done | bytes 6176 | tf_op jit(solution)/shard_map/ppermute | solution.py:408
  25.6 0.0 copy-done
  25.6 4.1 %shard_map.89 = (f32[224,768]{1,0:T(8,128)S(1)}, bf16[176,128]{1,0:T(8,128)(2,1)S(1)}) custom-call(f32[2,768]{1,0:T(2,128)S(1)} %add_add_fusion.total_ref, bf16[16,768]{1,0:T(8,128)(2,1)S(1)} %maximum_select_fusion.1.caps_ref, s32[2]{0:T(128)S(1)} %copy-done, f32[224,1536]{1,0:T(8,128)S(1)} %shard_map.88.slope_ref, ...), custom_call_target="tpu_custom_call" | custom-call | tf_op jit(solution)/shard_map/pallas_call | solution.py:46
  29.7 0.1 collective-permute-start.8
  29.8 1.5 %shard_map.90 = f32[160,128]{1,0:T(8,128)S(1)} custom-call(f32[224,768]{1,0:T(8,128)S(1)} %get-tuple-element.35.grad_ref, bf16[2,14,8,768]{3,2,1,0:T(8,128)(2,1)S(1)} %get-tuple-element.21.x_ref, bf16[2,3,8,768]{3,2,1,0:T(8,128)(2,1)S(1)} %get-tuple-element.33.before_ref, bf16[2,3,8,768]{3,2,1,0:T(8,128)(2,1)S(1)} %get-tuple-element.34.after_ref), custom_call_target="tpu_custom_call" | custom-call | tf_op jit(solution)/shard_map/pallas_call | solution.py:46
  31.3 0.0 collective-permute-done.8
  31.4 1.6 %collective-permute-start.11 = (bf16[192,128]{1,0:T(8,128)(2,1)S(1)}, bf16[192,128]{1,0:T(8,128)(2,1)S(1)}, u32[]{:S(2)}, u32[]{:S(2)}) collective-permute-start(bf16[192,128]{1,0:T(8,128)(2,1)S(1)} %pad_maximum_fusion), channel_id=1, source_target_pairs={{0,8},{4,12},{8,0},{12,4},{16,24},{20,28},{24,16},{28,20},{1,9},{5... | collective-permute-start | bytes 147464 | tf_op jit(solution)/shard_map/ppermute | solution.py:412
  32.9 0.5 %collective-permute-start.10 = (bf16[192,128]{1,0:T(8,128)(2,1)S(1)}, bf16[192,128]{1,0:T(8,128)(2,1)S(1)}, u32[]{:S(2)}, u32[]{:S(2)}) collective-permute-start(bf16[192,128]{1,0:T(8,128)(2,1)S(1)} %pad_maximum_fusion), channel_id=1, source_target_pairs={{0,16},{4,20},{8,24},{12,28},{16,0},{20,4},{24,8},{28,12},{1,17},{... | collective-permute-start | bytes 147464 | tf_op jit(solution)/shard_map/ppermute | solution.py:412
  33.4 1.5 %collective-permute-start.9 = (bf16[192,128]{1,0:T(8,128)(2,1)S(1)}, bf16[192,128]{1,0:T(8,128)(2,1)S(1)}, u32[]{:S(2)}, u32[]{:S(2)}) collective-permute-start(bf16[192,128]{1,0:T(8,128)(2,1)S(1)} %pad_maximum_fusion), channel_id=1, source_target_pairs={{0,24},{4,28},{8,16},{12,20},{16,8},{20,12},{24,0},{28,4},{1,25},{... | collective-permute-start | bytes 147464 | tf_op jit(solution)/shard_map/ppermute | solution.py:412
  34.9 0.6 %collective-permute-done.11 = bf16[192,128]{1,0:T(8,128)(2,1)S(1)} collective-permute-done((bf16[192,128]{1,0:T(8,128)(2,1)S(1)}, bf16[192,128]{1,0:T(8,128)(2,1)S(1)}, u32[]{:S(2)}, u32[]{:S(2)}) %collective-permute-start.11) | collective-permute-done | bytes 49184 | tf_op jit(solution)/shard_map/ppermute | solution.py:412
  35.5 2.0 %collective-permute-done.10 = bf16[192,128]{1,0:T(8,128)(2,1)S(1)} collective-permute-done((bf16[192,128]{1,0:T(8,128)(2,1)S(1)}, bf16[192,128]{1,0:T(8,128)(2,1)S(1)}, u32[]{:S(2)}, u32[]{:S(2)}) %collective-permute-start.10) | collective-permute-done | bytes 49184 | tf_op jit(solution)/shard_map/ppermute | solution.py:412
  37.6 0.9 %collective-permute-done.9 = bf16[192,128]{1,0:T(8,128)(2,1)S(1)} collective-permute-done((bf16[192,128]{1,0:T(8,128)(2,1)S(1)}, bf16[192,128]{1,0:T(8,128)(2,1)S(1)}, u32[]{:S(2)}, u32[]{:S(2)}) %collective-permute-start.9) | collective-permute-done | bytes 49184 | tf_op jit(solution)/shard_map/ppermute | solution.py:412
  38.5 1.5 %collective-permute-start.14 = (bf16[160,128]{1,0:T(8,128)(2,1)S(1)}, bf16[160,128]{1,0:T(8,128)(2,1)S(1)}, u32[]{:S(2)}, u32[]{:S(2)}) collective-permute-start(bf16[160,128]{1,0:T(8,128)(2,1)S(1)} %reduce-precision_convert_fusion.1), channel_id=1, source_target_pairs={{0,3},{1,0},{2,1},{3,2},{4,7},{5,4},{6,5},{7,6},{8,11},{9,8},{10,9... | collective-permute-start | bytes 122888 | tf_op jit(solution)/shard_map/ppermute | solution.py:408
  40.0 0.6 %collective-permute-start.13 = (bf16[160,128]{1,0:T(8,128)(2,1)S(1)}, bf16[160,128]{1,0:T(8,128)(2,1)S(1)}, u32[]{:S(2)}, u32[]{:S(2)}) collective-permute-start(bf16[160,128]{1,0:T(8,128)(2,1)S(1)} %reduce-precision_convert_fusion.1), channel_id=1, source_target_pairs={{0,1},{1,2},{2,3},{3,0},{4,5},{5,6},{6,7},{7,4},{8,9},{9,10},{10,1... | collective-permute-start | bytes 122888 | tf_op jit(solution)/shard_map/ppermute | solution.py:408
  40.5 0.1 collective-permute-start.12
  40.7 2.6 %collective-permute-done.14 = bf16[160,128]{1,0:T(8,128)(2,1)S(1)} collective-permute-done((bf16[160,128]{1,0:T(8,128)(2,1)S(1)}, bf16[160,128]{1,0:T(8,128)(2,1)S(1)}, u32[]{:S(2)}, u32[]{:S(2)}) %collective-permute-start.14) | collective-permute-done | bytes 40992 | tf_op jit(solution)/shard_map/ppermute | solution.py:408
  43.3 2.6 %collective-permute-done.13 = bf16[160,128]{1,0:T(8,128)(2,1)S(1)} collective-permute-done((bf16[160,128]{1,0:T(8,128)(2,1)S(1)}, bf16[160,128]{1,0:T(8,128)(2,1)S(1)}, u32[]{:S(2)}, u32[]{:S(2)}) %collective-permute-start.13) | collective-permute-done | bytes 40992 | tf_op jit(solution)/shard_map/ppermute | solution.py:408
  45.9 0.4 collective-permute-done.12
  46.4 0.1 collective-permute-start.15
  46.4 0.2 shard_map.91
  46.7 0.6 %copy.10 = f32[2,768]{1,0:T(2,128)} copy(f32[2,768]{1,0:T(2,128)S(1)} %get-tuple-element.40) | data formatting | bytes 12288
  47.3 0.3 collective-permute-done.15.other_ref
  47.7 0.7 %copy.11 = f32[7,7,768]{2,1,0:T(8,128)} copy(f32[7,7,768]{2,1,0:T(8,128)S(1)} %shard_map.92) | data formatting | bytes 301056
  (18 shorter events, 0.2 us)
Async XLA Ops:
  0.6 4.8 %collective-permute-start.5 = (bf16[2,768]{1,0:T(2,128)(2,1)}, bf16[2,768]{1,0:T(2,128)(2,1)S(1)}, u32[]{:S(2)}, u32[]{:S(2)}) collective-permute-start(bf16[2,768]{1,0:T(2,128)(2,1)} %caps_hbm.1), channel_id=1, source_target_pairs={{0,8},{4,12},{8,0},{12,4},{16,24},{20,28},{24,16},{28,20},{1,9},{5... | collective-permute-start | bytes 9224 | tf_op jit(solution)/shard_map/ppermute | solution.py:412
  5.4 5.9 %collective-permute-start.6 = (bf16[4,768]{1,0:T(4,128)(2,1)S(1)}, bf16[4,768]{1,0:T(4,128)(2,1)S(1)}, u32[]{:S(2)}, u32[]{:S(2)}) collective-permute-start(bf16[4,768]{1,0:T(4,128)(2,1)S(1)} %maximum_select_fusion.6), channel_id=1, source_target_pairs={{0,16},{4,20},{8,24},{12,28},{16,0},{20,4},{24,8},{28,12},{1,17},{... | collective-permute-start | bytes 18440 | tf_op jit(solution)/shard_map/ppermute | solution.py:412
  7.6 6.3 %collective-permute-start = (bf16[2,3,8,768]{3,2,1,0:T(8,128)(2,1)S(1)}, bf16[2,3,8,768]{3,2,1,0:T(8,128)(2,1)S(1)}, u32[]{:S(2)}, u32[]{:S(2)}) collective-permute-start(bf16[2,3,8,768]{3,2,1,0:T(8,128)(2,1)S(1)} %get-tuple-element.24), channel_id=1, source_target_pairs={{0,1},{1,2},{2,3},{3,0},{4,5},{5,6},{6,7},{7,4},{8,9},{9,10},{10,1... | collective-permute-start | bytes 221192 | tf_op jit(solution)/shard_map/ppermute | solution.py:408
  9.1 5.1 %collective-permute-start.1 = (bf16[2,3,8,768]{3,2,1,0:T(8,128)(2,1)S(1)}, bf16[2,3,8,768]{3,2,1,0:T(8,128)(2,1)S(1)}, u32[]{:S(2)}, u32[]{:S(2)}) collective-permute-start(bf16[2,3,8,768]{3,2,1,0:T(8,128)(2,1)S(1)} %get-tuple-element.25), channel_id=1, source_target_pairs={{0,3},{1,0},{2,1},{3,2},{4,7},{5,4},{6,5},{7,6},{8,11},{9,8},{10,9... | collective-permute-start | bytes 221192 | tf_op jit(solution)/shard_map/ppermute | solution.py:408
  11.4 9.6 %collective-permute-start.7 = (bf16[8,768]{1,0:T(8,128)(2,1)S(1)}, bf16[8,768]{1,0:T(8,128)(2,1)S(1)}, u32[]{:S(2)}, u32[]{:S(2)}) collective-permute-start(bf16[8,768]{1,0:T(8,128)(2,1)S(1)} %maximum_select_fusion.4), channel_id=1, source_target_pairs={{0,4},{4,0},{8,12},{12,8},{16,20},{20,16},{24,28},{28,24},{1,5},{5... | collective-permute-start | bytes 36872 | tf_op jit(solution)/shard_map/ppermute | solution.py:412
  17.2 8.4 %copy-start = (s32[2]{0:T(128)S(1)}, s32[2]{0:T(128)}, u32[]{:S(2)}) copy-start(s32[2]{0:T(128)} %pos_ref.1) | copy-start | bytes 28
  17.2 5.5 %collective-permute-start.3 = (f32[2,768]{1,0:T(2,128)S(1)}, f32[2,768]{1,0:T(2,128)S(1)}, u32[]{:S(2)}, u32[]{:S(2)}) collective-permute-start(f32[2,768]{1,0:T(2,128)S(1)} %get-tuple-element.28), channel_id=1, source_target_pairs={{0,1},{1,2},{2,3},{3,0},{4,5},{5,6},{6,7},{7,4},{8,9},{9,10},{10,1... | collective-permute-start | bytes 18440 | tf_op jit(solution)/shard_map/ppermute | solution.py:408
  18.0 4.6 %collective-permute-start.4 = (f32[2,768]{1,0:T(2,128)S(1)}, f32[2,768]{1,0:T(2,128)S(1)}, u32[]{:S(2)}, u32[]{:S(2)}) collective-permute-start(f32[2,768]{1,0:T(2,128)S(1)} %get-tuple-element.28), channel_id=1, source_target_pairs={{0,3},{1,0},{2,1},{3,2},{4,7},{5,4},{6,5},{7,6},{8,11},{9,8},{10,9... | collective-permute-start | bytes 18440 | tf_op jit(solution)/shard_map/ppermute | solution.py:408
  21.0 4.5 %collective-permute-start.2 = (f32[2,768]{1,0:T(2,128)S(1)}, f32[2,768]{1,0:T(2,128)S(1)}, u32[]{:S(2)}, u32[]{:S(2)}) collective-permute-start(f32[2,768]{1,0:T(2,128)S(1)} %get-tuple-element.28), channel_id=1, source_target_pairs={{0,2},{1,3},{2,0},{3,1},{4,6},{5,7},{6,4},{7,5},{8,10},{9,11},{10,... | collective-permute-start | bytes 18440 | tf_op jit(solution)/shard_map/ppermute | solution.py:408
  29.7 1.6 %collective-permute-start.8 = (bf16[176,128]{1,0:T(8,128)(2,1)S(1)}, bf16[176,128]{1,0:T(8,128)(2,1)S(1)}, u32[]{:S(2)}, u32[]{:S(2)}) collective-permute-start(bf16[176,128]{1,0:T(8,128)(2,1)S(1)} %get-tuple-element.36), channel_id=1, source_target_pairs={{0,4},{4,0},{8,12},{12,8},{16,20},{20,16},{24,28},{28,24},{1,5},{5... | collective-permute-start | bytes 135176 | tf_op jit(solution)/shard_map/ppermute | solution.py:412
  31.4 4.2 %collective-permute-start.11 = (bf16[192,128]{1,0:T(8,128)(2,1)S(1)}, bf16[192,128]{1,0:T(8,128)(2,1)S(1)}, u32[]{:S(2)}, u32[]{:S(2)}) collective-permute-start(bf16[192,128]{1,0:T(8,128)(2,1)S(1)} %pad_maximum_fusion), channel_id=1, source_target_pairs={{0,8},{4,12},{8,0},{12,4},{16,24},{20,28},{24,16},{28,20},{1,9},{5... | collective-permute-start | bytes 147464 | tf_op jit(solution)/shard_map/ppermute | solution.py:412
  32.9 4.6 %collective-permute-start.10 = (bf16[192,128]{1,0:T(8,128)(2,1)S(1)}, bf16[192,128]{1,0:T(8,128)(2,1)S(1)}, u32[]{:S(2)}, u32[]{:S(2)}) collective-permute-start(bf16[192,128]{1,0:T(8,128)(2,1)S(1)} %pad_maximum_fusion), channel_id=1, source_target_pairs={{0,16},{4,20},{8,24},{12,28},{16,0},{20,4},{24,8},{28,12},{1,17},{... | collective-permute-start | bytes 147464 | tf_op jit(solution)/shard_map/ppermute | solution.py:412
  33.4 5.0 %collective-permute-start.9 = (bf16[192,128]{1,0:T(8,128)(2,1)S(1)}, bf16[192,128]{1,0:T(8,128)(2,1)S(1)}, u32[]{:S(2)}, u32[]{:S(2)}) collective-permute-start(bf16[192,128]{1,0:T(8,128)(2,1)S(1)} %pad_maximum_fusion), channel_id=1, source_target_pairs={{0,24},{4,28},{8,16},{12,20},{16,8},{20,12},{24,0},{28,4},{1,25},{... | collective-permute-start | bytes 147464 | tf_op jit(solution)/shard_map/ppermute | solution.py:412
  38.5 4.8 %collective-permute-start.14 = (bf16[160,128]{1,0:T(8,128)(2,1)S(1)}, bf16[160,128]{1,0:T(8,128)(2,1)S(1)}, u32[]{:S(2)}, u32[]{:S(2)}) collective-permute-start(bf16[160,128]{1,0:T(8,128)(2,1)S(1)} %reduce-precision_convert_fusion.1), channel_id=1, source_target_pairs={{0,3},{1,0},{2,1},{3,2},{4,7},{5,4},{6,5},{7,6},{8,11},{9,8},{10,9... | collective-permute-start | bytes 122888 | tf_op jit(solution)/shard_map/ppermute | solution.py:408
  40.0 5.9 %collective-permute-start.13 = (bf16[160,128]{1,0:T(8,128)(2,1)S(1)}, bf16[160,128]{1,0:T(8,128)(2,1)S(1)}, u32[]{:S(2)}, u32[]{:S(2)}) collective-permute-start(bf16[160,128]{1,0:T(8,128)(2,1)S(1)} %reduce-precision_convert_fusion.1), channel_id=1, source_target_pairs={{0,1},{1,2},{2,3},{3,0},{4,5},{5,6},{6,7},{7,4},{8,9},{9,10},{10,1... | collective-permute-start | bytes 122888 | tf_op jit(solution)/shard_map/ppermute | solution.py:408
  40.5 5.8 %collective-permute-start.12 = (bf16[160,128]{1,0:T(8,128)(2,1)S(1)}, bf16[160,128]{1,0:T(8,128)(2,1)S(1)}, u32[]{:S(2)}, u32[]{:S(2)}) collective-permute-start(bf16[160,128]{1,0:T(8,128)(2,1)S(1)} %reduce-precision_convert_fusion.1), channel_id=1, source_target_pairs={{0,2},{1,3},{2,0},{3,1},{4,6},{5,7},{6,4},{7,5},{8,10},{9,11},{10,... | collective-permute-start | bytes 122888 | tf_op jit(solution)/shard_map/ppermute | solution.py:408
  46.4 1.3 %collective-permute-start.15 = (bf16[160,128]{1,0:T(8,128)(2,1)S(1)}, bf16[160,128]{1,0:T(8,128)(2,1)S(1)}, u32[]{:S(2)}, u32[]{:S(2)}) collective-permute-start(bf16[160,128]{1,0:T(8,128)(2,1)S(1)} %reduce-precision_convert_fusion.own_ref), channel_id=1, source_target_pairs={{0,4},{4,0},{8,12},{12,8},{16,20},{20,16},{24,28},{28,24},{1,5},{5... | collective-permute-start | bytes 122888 | tf_op jit(solution)/shard_map/ppermute | solution.py:412

commit v4 on v3

--- a/solution.py
+++ b/solution.py
@@ -30,7 +30,7 @@
     return pltpu.with_memory_space_constraint(array, pltpu.HBM)
 
 
-def call(body, outs, args, scratch=(), smem=(), hbm=(), limit=10):
+def call(body, outs, args, scratch=(), smem=(), hbm=(), limit=10, placed_out=vmem_out):
     specs = []
     placed = []
     for k, arg in enumerate(args):
@@ -45,7 +45,7 @@
             placed.append(in_vmem(arg))
     return pl.pallas_call(
         body,
-        out_shape=[vmem_out(shape, dtype) for shape, dtype in outs],
+        out_shape=[placed_out(shape, dtype) for shape, dtype in outs],
         in_specs=specs,
         out_specs=[pl.BlockSpec(memory_space=pltpu.VMEM) for _ in outs],
         scratch_shapes=list(scratch),
@@ -65,8 +65,16 @@
     return pl.ds(pl.multiple_of(t * LANES, LANES), LANES)
 
 
+def own_half():
+    me = lax.axis_index("dp")
+    odd = 0
+    for k in range(lax.axis_size("dp").bit_length() - 1):
+        odd = odd + lax.rem(me // (1 << k), 2)
+    return lax.rem(odd, 2)
+
+
 def load_body(
-    x_hbm, k_hbm, caps_hbm, x_ref, first_ref, last_ref, kw_ref, caps_ref, taps_ref, sems
+    x_hbm, k_hbm, caps_hbm, x_ref, first_ref, last_ref, taps_ref, caps_ref, sems
 ):
     rows, cols, channels = x_hbm.shape[1:]
     copies = [
@@ -78,19 +86,13 @@
     ]
     for copy in copies:
         copy.start()
-    masks = column_masks(cols, channels)
-    copies[0].wait()
-    for i in range(TAPS):
-        taps = taps_ref[i].astype(F32)
-        for j in range(TAPS):
-            spread = jnp.broadcast_to(taps[j : j + 1], (cols, channels))
-            kw_ref[i * TAPS + j] = jnp.where(masks[j], spread, 0.0)
-    for copy in copies[1:]:
+    for copy in copies:
         copy.wait()
 
 
 def conv_body(
-    x_ref, kw_ref, win_hbm, wout_hbm, part_ref, win_ref, wout_ref, sems
+    x_ref, taps_ref, caps_ref, win_hbm, wout_hbm, part_ref, win_ref, wout_ref, same_caps_ref,
+    kw_ref, sems,
 ):
     images, rows, cols, channels = x_ref.shape
     copies = [
@@ -99,6 +101,13 @@
     ]
     for copy in copies:
         copy.start()
+    same_caps_ref[...] = caps_ref[...]
+    masks = column_masks(cols, channels)
+    for i in range(TAPS):
+        taps = taps_ref[i].astype(F32)
+        for j in range(TAPS):
+            spread = jnp.broadcast_to(taps[j : j + 1], (cols, channels))
+            kw_ref[i * TAPS + j] = jnp.where(masks[j], spread, 0.0)
 
     def tile(t, carry):
         at = tile_at(t)
@@ -144,8 +153,9 @@
 
 
 def forward_body(
-    part_ref, below_ref, above_ref, kw_ref, x_ref, win_ref, wout_ref,
-    sums_ref, normed_ref, inv_ref, hid_ref, before_ref, after_ref, conv_ref, cast_ref,
+    part_ref, below_ref, above_ref, kw_ref, x_ref, win_ref, wout_ref, caps_ref,
+    sums_ref, normed_ref, inv_ref, hid_ref, before_ref, after_ref, same_caps_ref,
+    conv_ref, cast_ref, act_ref,
 ):
     images, rows, cols, channels = x_ref.shape
     hidden_units = win_ref.shape[1]
@@ -197,8 +207,8 @@
         inv_ref[some, :] = jnp.broadcast_to(inv, (32, LANES))
         cast_ref[some, :] = normed.astype(BF)
 
+    same_caps_ref[...] = caps_ref[...]
     width = 256
-    mixed = jnp.zeros((8, channels), F32)
     for start in range(0, hidden_units, width):
         some = pl.ds(start, width)
         hidden = jnp.dot(cast_ref[...], win_ref[:, some], preferred_element_type=F32)
@@ -208,9 +218,9 @@
         for b in range(images):
             total = jnp.sum(activated[b * pixels : (b + 1) * pixels], axis=0, keepdims=True)
             listed.extend(three_terms(total))
-        listed.append(jnp.zeros((8 - 3 * images, width), F32))
-        terms = jnp.concatenate(listed, axis=0).astype(BF)
-        mixed = mixed + jnp.dot(terms, wout_ref[some, :], preferred_element_type=F32)
+        listed.append(jnp.zeros((act_ref.shape[0] - 3 * images, width), F32))
+        act_ref[:, some] = jnp.concatenate(listed, axis=0)
+    mixed = jnp.dot(act_ref[...].astype(BF), wout_ref[...], preferred_element_type=F32)
     for b in range(images):
         own = x_ref[b, 0].astype(F32)
         for r in range(1, rows):
@@ -229,6 +239,22 @@
 def unit_rows(values):
     norms = jnp.sqrt(jnp.sum(values * values, axis=-1, keepdims=True) + EPS)
     return (values / norms, norms)
+
+
+def joined(bit, mine_ref, theirs_ref):
+    upper = lax.rem(lax.axis_index("dp") // bit, 2) == 1
+    mine, theirs = mine_ref[...].astype(F32), theirs_ref[...].astype(F32)
+    return jnp.concatenate(
+        [jnp.where(upper, theirs, mine), jnp.where(upper, mine, theirs)], axis=0
+    )
+
+
+def join_body(bit, mine_ref, theirs_ref, out_ref):
+    out_ref[...] = joined(bit, mine_ref, theirs_ref).astype(BF)
+
+
+def text_cast_body(bit, mine_ref, theirs_ref, cast_ref):
+    cast_ref[...] = unit_rows(joined(bit, mine_ref, theirs_ref))[0].astype(BF)
 
 
 def kernel_sums(grad_ref, x_ref, before_ref, after_ref, list_ref, half):
@@ -269,18 +295,17 @@
 
 
 def backward_body(
-    scene_pixels, total_ref, caps_ref, pos_ref, slope_ref, normed_ref, inv_ref, win_ref, wout_ref,
-    x_ref, before_ref, after_ref,
-    grad_ref, pay_ref, list_ref, hg_ref, row_ref,
+    scene_pixels, text_ref, pos_ref, slope_ref, normed_ref, inv_ref, win_ref, wout_ref,
+    x_ref, before_ref, after_ref, *refs,
 ):
+    *part_refs, grad_ref, pay_ref, list_ref, hg_ref, row_ref = refs
     images, rows, cols, channels = x_ref.shape
     pixels = rows * cols
-    count = caps_ref.shape[0]
-    pooled = total_ref[...] / scene_pixels
+    count = text_ref.shape[0]
+    pooled = pair_sum([ref[...] for ref in part_refs]) / scene_pixels
     image_unit, pooled_norm = unit_rows(pooled)
     image_cast = image_unit.astype(BF)
-    text_unit, _ = unit_rows(caps_ref[...].astype(F32))
-    text_cast = text_unit.astype(BF)
+    text_cast = text_ref[...]
     logits = (
         LOGIT_SCALE
         * lax.dot_general(
@@ -322,7 +347,7 @@
         - jnp.mean(normed_grad, axis=-1, keepdims=True)
         - normed * jnp.mean(normed_grad * normed, axis=-1, keepdims=True)
     )
-    half = 1 - lax.rem(lax.axis_index("dp"), 2)
+    half = 1 - own_half()
     kernel_sums(grad_ref, x_ref, before_ref, after_ref, list_ref, half)
     listed = list_ref.shape[0]
     pay_ref[0:listed, :] = list_ref[...].astype(BF)
@@ -348,7 +373,7 @@
 
 
 def own_half_body(grad_ref, x_ref, before_ref, after_ref, list_ref):
-    half = lax.rem(lax.axis_index("dp"), 2)
+    half = own_half()
     kernel_sums(grad_ref, x_ref, before_ref, after_ref, list_ref, half)
 
 
@@ -391,7 +416,7 @@
 
 def merge_body(own_ref, other_ref, out_ref, wide_ref):
     tiles = out_ref.shape[2] // LANES // 2
-    half = lax.rem(lax.axis_index("dp"), 2)
+    half = own_half()
     for source, side in ((own_ref, half), (other_ref, 1 - half)):
         wide_ref[...] = source[...].astype(F32)
         for t in range(tiles):
@@ -439,11 +464,28 @@
     return lax.reduce_precision(values, 8, 7).astype(BF)
 
 
+def group_parts(mine, axis, stride, members):
+    if members == 2:
+        return [mine, flip(mine, axis, stride)]
+    one, two, three = [shifted(mine, axis, stride, k) for k in (1, 2, 3)]
+    return [mine, two, one, three]
+
+
+def pair_sum(parts):
+    parts = [part.astype(F32) for part in parts]
+    while len(parts) > 1:
+        parts = [parts[k] + parts[k + 1] for k in range(0, len(parts), 2)]
+    return parts[0]
+
+
 def group_sum(mine, axis, stride, members):
-    if members == 2:
-        return mine.astype(F32) + flip(mine, axis, stride).astype(F32)
-    one, two, three = [shifted(mine, axis, stride, k).astype(F32) for k in (1, 2, 3)]
-    return (mine.astype(F32) + two) + (one + three)
+    return pair_sum(group_parts(mine, axis, stride, members))
+
+
+def rows_joined(body, mine, theirs, bit):
+    shape = (2 * mine.shape[0], mine.shape[1])
+    (out,) = call(functools.partial(body, bit), [(shape, BF)], [mine, theirs])
+    return out
 
 
 def per_device(scenes, kernel, weight_in, weight_out, captions, positives):
@@ -454,39 +496,40 @@
     scene_pixels = rows * space_count * cols
     edge = (images, SIDE, cols, channels)
 
-    x, first, last, spread, own_captions = call(
+    x, first, last, taps, own_captions = call(
         load_body,
         [
             (scenes.shape, BF),
             (edge, BF),
             (edge, BF),
-            ((TAPS * TAPS, cols, channels), F32),
+            (kernel.shape, BF),
             (captions.shape, BF),
         ],
         [scenes, kernel, captions],
-        scratch=[pltpu.VMEM(kernel.shape, BF), pltpu.SemaphoreType.DMA((5,))],
+        scratch=[pltpu.SemaphoreType.DMA((5,))],
         hbm=(0, 1, 2),
     )
     below = shifted(last, "space", 1, 1, space_count)
     above = shifted(first, "space", 1, space_count - 1, space_count)
-    theirs = captions
-    gathered = own_captions
-    for bit in bits("dp")[1:] + [1]:
-        theirs = flip(theirs, "dp", bit)
-        gathered = theirs = join(gathered, theirs, "dp", bit)
-    part, win, wout = call(
+    dp_bits = bits("dp")
+    theirs = flip(captions, "dp", dp_bits[1])
+    part, win, wout, same_captions, spread = call(
         conv_body,
         [
             (scenes.shape, F32),
             (weight_in.shape, BF),
             (weight_out.shape, BF),
+            (captions.shape, BF),
+            ((TAPS * TAPS, cols, channels), F32),
         ],
-        [x, spread, weight_in, weight_out],
+        [x, taps, own_captions, weight_in, weight_out],
         scratch=[pltpu.SemaphoreType.DMA((2,))],
-        hbm=(2, 3),
-    )
-
-    sums, normed, inv, hidden, before, after = call(
+        hbm=(3, 4),
+    )
+
+    gathered = rows_joined(join_body, same_captions, theirs, dp_bits[1])
+    theirs = flip(gathered, "dp", dp_bits[2])
+    sums, normed, inv, hidden, before, after, gathered = call(
         forward_body,
         [
             ((images, channels), F32),
@@ -495,12 +538,23 @@
             ((pixels, hidden_units), F32),
             (edge, BF),
             (edge, BF),
+            (gathered.shape, BF),
         ],
-        [part, below, above, spread, x, win, wout],
-        scratch=[pltpu.VMEM((pixels, channels), F32), pltpu.VMEM((pixels, channels), BF)],
-    )
-    for stride, members in groups(space_count, 1):
+        [part, below, above, spread, x, win, wout, gathered],
+        scratch=[
+            pltpu.VMEM((pixels, channels), F32),
+            pltpu.VMEM((pixels, channels), BF),
+            pltpu.VMEM((3 * images + -3 * images % 8, hidden_units), F32),
+        ],
+    )
+    for bit in dp_bits[2:]:
+        gathered = rows_joined(join_body, gathered, theirs, bit)
+        theirs = flip(gathered, "dp", 1 if bit == dp_bits[-1] else 2 * bit)
+    text_cast = rows_joined(text_cast_body, gathered, theirs, 1)
+    space_groups = groups(space_count, 1)
+    for stride, members in space_groups[:-1]:
         sums = group_sum(sums, "space", stride, members)
+    parts = group_parts(sums, "space", *space_groups[-1])
     (slope,) = call(slope_body, [((pixels, hidden_units), F32)], [hidden])
 
     listed = channels // LANES // 2 * TAPS * TAPS
@@ -510,13 +564,16 @@
     grad, pay = call(
         functools.partial(backward_body, scene_pixels),
         [((pixels, channels), F32), ((listed + own_rows, LANES), BF)],
-        [sums, gathered, positives, slope, normed, inv, win, wout, x, before, after],
+        [
+            text_cast, positives, slope, normed, inv, weight_in, weight_out, x, before, after,
+            *parts,
+        ],
         scratch=[
             pltpu.VMEM((listed, LANES), F32),
             pltpu.VMEM((pixels, hidden_units), BF),
             pltpu.VMEM((own_rows, LANES), F32),
         ],
-        smem=(2,),
+        smem=(1,),
     )
     other = flip(pay, "dp", 1)
     (own,) = call(
@@ -527,11 +584,11 @@
     for stride, members in groups(lax.axis_size("dp"), 2):
         mine = rounded(total)
         both = jnp.concatenate([mine, units], axis=0)
-        near = flip(both, "dp", stride)
+        near = flip(both, "dp", stride + 1)
         total = mine.astype(F32) + near[:listed].astype(F32)
         joined = join(units, near[listed:], "dp", stride)
         if members == 4:
-            far = flip(both, "dp", 2 * stride)
+            far = flip(both, "dp", 2 * stride + 1)
             cross = flip(both, "dp", 3 * stride)
             total = total + (far[:listed].astype(F32) + cross[:listed].astype(F32))
             joined = join(
@@ -543,6 +600,7 @@
         [((images, channels), F32), ((1, 1), F32)],
         [units, own_captions],
         scratch=[pltpu.VMEM(units.shape, F32)],
+        placed_out=jax.ShapeDtypeStruct,
     )
     for stride, members in groups(space_count, 1):
         total = group_sum(rounded(total), "space", stride, members)
@@ -553,6 +611,7 @@
         [((TAPS, TAPS, channels), F32)],
         [mine, other],
         scratch=[pltpu.VMEM((listed, LANES), F32)],
+        placed_out=jax.ShapeDtypeStruct,
     )
     return (loss.reshape(()), text_grad, kernel_grad)
 

time: 49.6 us -> 45.3 us (0.913)
  waiting for transfers between devices: 14.2 us -> 9.6 us
  starting transfers between devices: 18.7 us -> 21.1 us
  local copies, waits for them, and re-layouts: 1.29 us -> 0.03 us
  between operations: 1.99 us -> 0.84 us
    ppermute x8, waiting for transfers between devices: 9.74 us -> 4.55 us  [shifted(): return lax.ppermute(array, axis, pairs)]
    ppermute x8, starting transfers between devices: 9.85 us -> 14.4 us  [shifted(): return lax.ppermute(array, axis, pairs)]
    ppermute x8, starting transfers between devices: 8.88 us -> 6.72 us  [flip(): lax.ppermute(array, axis, [(i, i ^ mask) for i in range(lax.axis_size(axi...]
    unnamed x4 -> x6, local copies, waits for them, and re-layouts: 1.27 us -> 0.02 us
    ppermute x8, waiting for transfers between devices: 4.46 us -> 5.05 us  [flip(): lax.ppermute(array, axis, [(i, i ^ mask) for i in range(lax.axis_size(axi...]
    pallas_call x8 -> x11, Pallas kernels: 13.1 us -> 13.5 us  [call(): pl.pallas_call(body, out_shape=[placed_out(shape, dtype) for shape, dtype...]
  transfers between devices with their start and end apart: 16 -> 16, of which waited for: 11 -> 8; matrix products, arithmetic and copies ran while one was open for 1% -> 0% of each run, Pallas kernels for 18% -> 17%
where the time goes in v4:
time: 45.3 us; the launch traced here: 45.2 us
  starting transfers between devices  21.1 us (47%)
  Pallas kernels  13.5 us (30%)
  waiting for transfers between devices  9.6 us (21%)
  between operations  0.84 us (2%)
    ppermute x8, starting transfers between devices, shifted(): return lax.ppermute(array, axis, pairs)  14.4 us
    pallas_call x11, Pallas kernels, call(): pl.pallas_call(body, out_shape=[placed_out(shape, dtype) for shape, dtype...  13.5 us
    ppermute x8, starting transfers between devices, flip(): lax.ppermute(array, axis, [(i, i ^ mask) for i in range(lax.axis_size(axi...  6.72 us
    ppermute x8, waiting for transfers between devices, flip(): lax.ppermute(array, axis, [(i, i ^ mask) for i in range(lax.axis_size(axi...  5.05 us
    ppermute x8, waiting for transfers between devices, shifted(): return lax.ppermute(array, axis, pairs)  4.55 us
  transfers between devices with their start and end apart: 16, of which 8 were waited for; matrix products, arithmetic and copies ran while one was open for 0% of the time, Pallas kernels for 17%

profile of v4, /device:TPU:0, one launch (start us, length us, event | category | flops | bytes accessed | tf_op | source)
XLA Modules:
  0.0 45.2 jit_solution(5799606334616849375)
XLA Ops:
  0.6 1.1 %shard_map.85 = (bf16[2,14,8,768]{3,2,1,0:T(8,128)(2,1)S(1)}, bf16[2,3,8,768]{3,2,1,0:T(8,128)(2,1)S(1)}, bf16[2,3,8,768]{3,2,1,0:T(8,128)(2,1)S(1)}, bf16[7,7,768]{2,1,0:T(8,128)(2,1)S(1)}, bf16[2,768]{1,0:T(2,128)(2,1)S(1)}) custom-call(bf16[2,14,8,768]{3,2,1,0:T(8,128)(2,1)} %x_hbm.1, bf16[7,7,768]{2,1,0:T(8,128)(2,1)} %k_hbm.1, bf16[2,768]{1,0:T(2,128)(2,1)} %caps_hbm.1), custom_call_target="tpu_custom_call" | custom-call | tf_op jit(solution)/shard_map/pallas_call | solution.py:46
  1.8 3.1 %collective-permute-start = (bf16[2,3,8,768]{3,2,1,0:T(8,128)(2,1)S(1)}, bf16[2,3,8,768]{3,2,1,0:T(8,128)(2,1)S(1)}, u32[]{:S(2)}, u32[]{:S(2)}) collective-permute-start(bf16[2,3,8,768]{3,2,1,0:T(8,128)(2,1)S(1)} %get-tuple-element.28), channel_id=1, source_target_pairs={{0,1},{1,2},{2,3},{3,0},{4,5},{5,6},{6,7},{7,4},{8,9},{9,10},{10,1... | collective-permute-start | bytes 221192 | tf_op jit(solution)/shard_map/ppermute | solution.py:433
  4.9 2.1 %collective-permute-start.1 = (bf16[2,3,8,768]{3,2,1,0:T(8,128)(2,1)S(1)}, bf16[2,3,8,768]{3,2,1,0:T(8,128)(2,1)S(1)}, u32[]{:S(2)}, u32[]{:S(2)}) collective-permute-start(bf16[2,3,8,768]{3,2,1,0:T(8,128)(2,1)S(1)} %get-tuple-element.29), channel_id=1, source_target_pairs={{0,3},{1,0},{2,1},{3,2},{4,7},{5,4},{6,5},{7,6},{8,11},{9,8},{10,9... | collective-permute-start | bytes 221192 | tf_op jit(solution)/shard_map/ppermute | solution.py:433
  7.0 1.6 %collective-permute-start.2 = (bf16[2,768]{1,0:T(2,128)(2,1)}, bf16[2,768]{1,0:T(2,128)(2,1)S(1)}, u32[]{:S(2)}, u32[]{:S(2)}) collective-permute-start(bf16[2,768]{1,0:T(2,128)(2,1)} %caps_hbm.1), channel_id=1, source_target_pairs={{0,8},{4,12},{8,0},{12,4},{16,24},{20,28},{24,16},{28,20},{1,9},{5... | collective-permute-start | bytes 9224 | tf_op jit(solution)/shard_map/ppermute | solution.py:437
  8.6 2.4 %shard_map.86 = (f32[2,14,8,768]{3,2,1,0:T(8,128)S(1)}, bf16[768,1536]{1,0:T(8,128)(2,1)S(1)}, bf16[1536,768]{1,0:T(8,128)(2,1)S(1)}, bf16[2,768]{1,0:T(2,128)(2,1)S(1)}, f32[49,8,768]{2,1,0:T(8,128)S(1)}) custom-call(bf16[2,14,8,768]{3,2,1,0:T(8,128)(2,1)S(1)} %get-tuple-element.24.x_ref, bf16[7,7,768]{2,1,0:T(8,128)(2,1)S(1)} %get-tuple-element.25.taps_ref, ...), custom_call_target="tpu_custom_call" | custom-call | tf_op jit(solution)/shard_map/pallas_call | solution.py:46
  11.0 0.0 collective-permute-done.2.theirs_ref
  11.0 1.6 %collective-permute-start.3 = (bf16[4,768]{1,0:T(4,128)(2,1)S(1)}, bf16[4,768]{1,0:T(4,128)(2,1)S(1)}, u32[]{:S(2)}, u32[]{:S(2)}) collective-permute-start(bf16[4,768]{1,0:T(4,128)(2,1)S(1)} %shard_map.87.caps_ref), channel_id=1, source_target_pairs={{0,16},{4,20},{8,24},{12,28},{16,0},{20,4},{24,8},{28,12},{1,17},{... | collective-permute-start | bytes 18440 | tf_op jit(solution)/shard_map/ppermute | solution.py:437
  12.6 0.0 collective-permute-done.below_ref
  12.6 0.0 collective-permute-done.1.above_ref
  12.6 0.0 copy-start.1
  12.6 1.8 %shard_map.88 = (f32[2,768]{1,0:T(2,128)S(1)}, f32[224,768]{1,0:T(8,128)S(1)}, f32[224,128]{1,0:T(8,128)S(1)}, f32[224,1536]{1,0:T(8,128)S(1)}, bf16[2,3,8,768]{...) custom-call(f32[2,14,8,768]{3,2,1,0:T(8,128)S(1)} %get-tuple-element.27.part_ref, ...), custom_call_target="tpu_custom_call" | custom-call | tf_op jit(solution)/shard_map/pallas_call | solution.py:46
  14.5 0.0 copy-start
  14.5 0.0 copy-start.2
  14.5 0.3 collective-permute-done.3.theirs_ref
  14.8 0.1 collective-permute-start.4
  14.8 0.9 %collective-permute-start.5 = (f32[2,768]{1,0:T(2,128)S(1)}, f32[2,768]{1,0:T(2,128)S(1)}, u32[]{:S(2)}, u32[]{:S(2)}) collective-permute-start(f32[2,768]{1,0:T(2,128)S(1)} %get-tuple-element.40.refs_0_), channel_id=1, source_target_pairs={{0,2},{1,3},{2,0},{3,1},{4,6},{5,7},{6,4},{7,5},{8,10},{9,11},{10,... | collective-permute-start | bytes 18440 | tf_op jit(solution)/shard_map/ppermute | solution.py:433
  15.7 1.6 %collective-permute-start.6 = (f32[2,768]{1,0:T(2,128)S(1)}, f32[2,768]{1,0:T(2,128)S(1)}, u32[]{:S(2)}, u32[]{:S(2)}) collective-permute-start(f32[2,768]{1,0:T(2,128)S(1)} %get-tuple-element.40.refs_0_), channel_id=1, source_target_pairs={{0,1},{1,2},{2,3},{3,0},{4,5},{5,6},{6,7},{7,4},{8,9},{9,10},{10,1... | collective-permute-start | bytes 18440 | tf_op jit(solution)/shard_map/ppermute | solution.py:433
  17.3 2.2 %collective-permute-start.7 = (f32[2,768]{1,0:T(2,128)S(1)}, f32[2,768]{1,0:T(2,128)S(1)}, u32[]{:S(2)}, u32[]{:S(2)}) collective-permute-start(f32[2,768]{1,0:T(2,128)S(1)} %get-tuple-element.40.refs_0_), channel_id=1, source_target_pairs={{0,3},{1,0},{2,1},{3,2},{4,7},{5,4},{6,5},{7,6},{8,11},{9,8},{10,9... | collective-permute-start | bytes 18440 | tf_op jit(solution)/shard_map/ppermute | solution.py:433
  19.5 0.8 %shard_map.91.slope_ref = f32[224,1536]{1,0:T(8,128)S(1)} custom-call(f32[224,1536]{1,0:T(8,128)S(1)} %get-tuple-element.35.hid_ref), custom_call_target="tpu_custom_call" | custom-call | tf_op jit(solution)/shard_map/pallas_call | solution.py:46
  20.3 0.0 collective-permute-done.4.theirs_ref
  20.3 0.1 shard_map.90.text_ref
  20.4 0.0 collective-permute-done.5.refs_1_
  20.5 0.7 %collective-permute-done.6.refs_2_ = f32[2,768]{1,0:T(2,128)S(1)} collective-permute-done((f32[2,768]{1,0:T(2,128)S(1)}, f32[2,768]{1,0:T(2,128)S(1)}, u32[]{:S(2)}, u32[]{:S(2)}) %collective-permute-start.6) | collective-permute-done | bytes 6176 | tf_op jit(solution)/shard_map/ppermute | solution.py:433
  21.1 0.0 collective-permute-done.7.refs_3_
  21.1 0.0 copy-done.1
  21.1 0.0 copy-done
  21.1 0.0 copy-done.2
  21.1 4.1 %shard_map.92 = (f32[224,768]{1,0:T(8,128)S(1)}, bf16[176,128]{1,0:T(8,128)(2,1)S(1)}) custom-call(bf16[16,768]{1,0:T(8,128)(2,1)S(1)} %shard_map.90.text_ref, s32[2]{0:T(128)S(1)} %copy-done.2, f32[224,1536]{1,0:T(8,128)S(1)} %shard_map.91.slope_ref, f32[224,768]{1,0:T(8,128)S(1)} %get-tuple-element.36.normed_ref, ...), custom_call_target="tpu_custom_call" | custom-call | tf_op jit(solution)/shard_map/pallas_call | solution.py:46
  25.3 0.1 collective-permute-start.8
  25.4 1.5 %shard_map.93 = f32[160,128]{1,0:T(8,128)S(1)} custom-call(f32[224,768]{1,0:T(8,128)S(1)} %get-tuple-element.41.grad_ref, bf16[2,14,8,768]{3,2,1,0:T(8,128)(2,1)S(1)} %get-tuple-element.24.x_ref, bf16[2,3,8,768]{3,2,1,0:T(8,128)(2,1)S(1)} %get-tuple-element.38.before_ref, bf16[2,3,8,768]{3,2,1,0:T(8,128)(2,1)S(1)} %get-tuple-element.39.after_ref), custom_call_target="tpu_custom_call" | custom-call | tf_op jit(solution)/shard_map/pallas_call | solution.py:46
  26.9 0.0 collective-permute-done.8
  27.0 1.7 %collective-permute-start.10 = (bf16[192,128]{1,0:T(8,128)(2,1)S(1)}, bf16[192,128]{1,0:T(8,128)(2,1)S(1)}, u32[]{:S(2)}, u32[]{:S(2)}) collective-permute-start(bf16[192,128]{1,0:T(8,128)(2,1)S(1)} %pad_maximum_fusion), channel_id=1, source_target_pairs={{0,20},{4,16},{8,28},{12,24},{16,4},{20,0},{24,12},{28,8},{1,21},{... | collective-permute-start | bytes 147464 | tf_op jit(solution)/shard_map/ppermute | solution.py:437
  28.6 1.0 %collective-permute-start.11 = (bf16[192,128]{1,0:T(8,128)(2,1)S(1)}, bf16[192,128]{1,0:T(8,128)(2,1)S(1)}, u32[]{:S(2)}, u32[]{:S(2)}) collective-permute-start(bf16[192,128]{1,0:T(8,128)(2,1)S(1)} %pad_maximum_fusion), channel_id=1, source_target_pairs={{0,12},{4,8},{8,4},{12,0},{16,28},{20,24},{24,20},{28,16},{1,13},{... | collective-permute-start | bytes 147464 | tf_op jit(solution)/shard_map/ppermute | solution.py:437
  29.6 0.6 %collective-permute-start.9 = (bf16[192,128]{1,0:T(8,128)(2,1)S(1)}, bf16[192,128]{1,0:T(8,128)(2,1)S(1)}, u32[]{:S(2)}, u32[]{:S(2)}) collective-permute-start(bf16[192,128]{1,0:T(8,128)(2,1)S(1)} %pad_maximum_fusion), channel_id=1, source_target_pairs={{0,24},{4,28},{8,16},{12,20},{16,8},{20,12},{24,0},{28,4},{1,25},{... | collective-permute-start | bytes 147464 | tf_op jit(solution)/shard_map/ppermute | solution.py:437
  30.2 0.3 collective-permute-done.10
  30.5 1.9 %collective-permute-done.11 = bf16[192,128]{1,0:T(8,128)(2,1)S(1)} collective-permute-done((bf16[192,128]{1,0:T(8,128)(2,1)S(1)}, bf16[192,128]{1,0:T(8,128)(2,1)S(1)}, u32[]{:S(2)}, u32[]{:S(2)}) %collective-permute-start.11) | collective-permute-done | bytes 49184 | tf_op jit(solution)/shard_map/ppermute | solution.py:437
  32.5 2.2 %collective-permute-done.9 = bf16[192,128]{1,0:T(8,128)(2,1)S(1)} collective-permute-done((bf16[192,128]{1,0:T(8,128)(2,1)S(1)}, bf16[192,128]{1,0:T(8,128)(2,1)S(1)}, u32[]{:S(2)}, u32[]{:S(2)}) %collective-permute-start.9) | collective-permute-done | bytes 49184 | tf_op jit(solution)/shard_map/ppermute | solution.py:437
  34.7 0.7 %collective-permute-start.12 = (bf16[160,128]{1,0:T(8,128)(2,1)S(1)}, bf16[160,128]{1,0:T(8,128)(2,1)S(1)}, u32[]{:S(2)}, u32[]{:S(2)}) collective-permute-start(bf16[160,128]{1,0:T(8,128)(2,1)S(1)} %reduce-precision_convert_fusion.1), channel_id=1, source_target_pairs={{0,2},{1,3},{2,0},{3,1},{4,6},{5,7},{6,4},{7,5},{8,10},{9,11},{10,... | collective-permute-start | bytes 122888 | tf_op jit(solution)/shard_map/ppermute | solution.py:433
  35.4 3.8 %collective-permute-start.13 = (bf16[160,128]{1,0:T(8,128)(2,1)S(1)}, bf16[160,128]{1,0:T(8,128)(2,1)S(1)}, u32[]{:S(2)}, u32[]{:S(2)}) collective-permute-start(bf16[160,128]{1,0:T(8,128)(2,1)S(1)} %reduce-precision_convert_fusion.1), channel_id=1, source_target_pairs={{0,1},{1,2},{2,3},{3,0},{4,5},{5,6},{6,7},{7,4},{8,9},{9,10},{10,1... | collective-permute-start | bytes 122888 | tf_op jit(solution)/shard_map/ppermute | solution.py:433
  39.1 0.1 collective-permute-start.14
  39.3 2.3 %collective-permute-done.12 = bf16[160,128]{1,0:T(8,128)(2,1)S(1)} collective-permute-done((bf16[160,128]{1,0:T(8,128)(2,1)S(1)}, bf16[160,128]{1,0:T(8,128)(2,1)S(1)}, u32[]{:S(2)}, u32[]{:S(2)}) %collective-permute-start.12) | collective-permute-done | bytes 40992 | tf_op jit(solution)/shard_map/ppermute | solution.py:433
  41.6 0.0 collective-permute-done.13
  41.6 1.5 %collective-permute-done.14 = bf16[160,128]{1,0:T(8,128)(2,1)S(1)} collective-permute-done((bf16[160,128]{1,0:T(8,128)(2,1)S(1)}, bf16[160,128]{1,0:T(8,128)(2,1)S(1)}, u32[]{:S(2)}, u32[]{:S(2)}) %collective-permute-start.14) | collective-permute-done | bytes 40992 | tf_op jit(solution)/shard_map/ppermute | solution.py:433
  43.2 0.1 collective-permute-start.15
  43.3 0.8 %shard_map.94 = (f32[2,768]{1,0:T(2,128)}, f32[1,1]{1,0:T(1,128)}) custom-call(bf16[128,128]{1,0:T(8,128)(2,1)S(1)} %maximum_select_fusion.rows_ref, bf16[2,768]{1,0:T(2,128)(2,1)S(1)} %get-tuple-element.26.caps_ref), custom_call_target="tpu_custom_call" | custom-call | tf_op jit(solution)/shard_map/pallas_call | solution.py:46
  44.1 0.4 collective-permute-done.15.other_ref
  44.5 0.7 %shard_map.95 = f32[7,7,768]{2,1,0:T(8,128)} custom-call(bf16[160,128]{1,0:T(8,128)(2,1)S(1)} %reduce-precision_convert_fusion.own_ref, bf16[160,128]{1,0:T(8,128)(2,1)S(1)} %collective-permute-done.15.other_ref), custom_call_target="tpu_custom_call" | custom-call | tf_op jit(solution)/shard_map/pallas_call | solution.py:46
  (15 shorter events, 0.2 us)
Async XLA Ops:
  1.8 10.9 %collective-permute-start = (bf16[2,3,8,768]{3,2,1,0:T(8,128)(2,1)S(1)}, bf16[2,3,8,768]{3,2,1,0:T(8,128)(2,1)S(1)}, u32[]{:S(2)}, u32[]{:S(2)}) collective-permute-start(bf16[2,3,8,768]{3,2,1,0:T(8,128)(2,1)S(1)} %get-tuple-element.28), channel_id=1, source_target_pairs={{0,1},{1,2},{2,3},{3,0},{4,5},{5,6},{6,7},{7,4},{8,9},{9,10},{10,1... | collective-permute-start | bytes 221192 | tf_op jit(solution)/shard_map/ppermute | solution.py:433
  4.9 7.8 %collective-permute-start.1 = (bf16[2,3,8,768]{3,2,1,0:T(8,128)(2,1)S(1)}, bf16[2,3,8,768]{3,2,1,0:T(8,128)(2,1)S(1)}, u32[]{:S(2)}, u32[]{:S(2)}) collective-permute-start(bf16[2,3,8,768]{3,2,1,0:T(8,128)(2,1)S(1)} %get-tuple-element.29), channel_id=1, source_target_pairs={{0,3},{1,0},{2,1},{3,2},{4,7},{5,4},{6,5},{7,6},{8,11},{9,8},{10,9... | collective-permute-start | bytes 221192 | tf_op jit(solution)/shard_map/ppermute | solution.py:433
  7.0 4.1 %collective-permute-start.2 = (bf16[2,768]{1,0:T(2,128)(2,1)}, bf16[2,768]{1,0:T(2,128)(2,1)S(1)}, u32[]{:S(2)}, u32[]{:S(2)}) collective-permute-start(bf16[2,768]{1,0:T(2,128)(2,1)} %caps_hbm.1), channel_id=1, source_target_pairs={{0,8},{4,12},{8,0},{12,4},{16,24},{20,28},{24,16},{28,20},{1,9},{5... | collective-permute-start | bytes 9224 | tf_op jit(solution)/shard_map/ppermute | solution.py:437
  11.0 3.7 %collective-permute-start.3 = (bf16[4,768]{1,0:T(4,128)(2,1)S(1)}, bf16[4,768]{1,0:T(4,128)(2,1)S(1)}, u32[]{:S(2)}, u32[]{:S(2)}) collective-permute-start(bf16[4,768]{1,0:T(4,128)(2,1)S(1)} %shard_map.87.caps_ref), channel_id=1, source_target_pairs={{0,16},{4,20},{8,24},{12,28},{16,0},{20,4},{24,8},{28,12},{1,17},{... | collective-permute-start | bytes 18440 | tf_op jit(solution)/shard_map/ppermute | solution.py:437
  12.6 8.5 %copy-start.1 = (bf16[1536,768]{1,0:T(8,128)(2,1)S(1)}, bf16[1536,768]{1,0:T(8,128)(2,1)}, u32[]{:S(2)}) copy-start(bf16[1536,768]{1,0:T(8,128)(2,1)} %wout_ref.1) | copy-start | bytes 7077892
  14.5 6.7 %copy-start = (bf16[768,1536]{1,0:T(8,128)(2,1)S(1)}, bf16[768,1536]{1,0:T(8,128)(2,1)}, u32[]{:S(2)}) copy-start(bf16[768,1536]{1,0:T(8,128)(2,1)} %win_ref.1) | copy-start | bytes 7077892
  14.5 6.7 %copy-start.2 = (s32[2]{0:T(128)S(1)}, s32[2]{0:T(128)}, u32[]{:S(2)}) copy-start(s32[2]{0:T(128)} %pos_ref.1) | copy-start | bytes 28
  14.8 5.6 %collective-permute-start.4 = (bf16[8,768]{1,0:T(8,128)(2,1)S(1)}, bf16[8,768]{1,0:T(8,128)(2,1)S(1)}, u32[]{:S(2)}, u32[]{:S(2)}) collective-permute-start(bf16[8,768]{1,0:T(8,128)(2,1)S(1)} %shard_map.89.mine_ref), channel_id=1, source_target_pairs={{0,4},{4,0},{8,12},{12,8},{16,20},{20,16},{24,28},{28,24},{1,5},{5... | collective-permute-start | bytes 36872 | tf_op jit(solution)/shard_map/ppermute | solution.py:437
  14.8 5.6 %collective-permute-start.5 = (f32[2,768]{1,0:T(2,128)S(1)}, f32[2,768]{1,0:T(2,128)S(1)}, u32[]{:S(2)}, u32[]{:S(2)}) collective-permute-start(f32[2,768]{1,0:T(2,128)S(1)} %get-tuple-element.40.refs_0_), channel_id=1, source_target_pairs={{0,2},{1,3},{2,0},{3,1},{4,6},{5,7},{6,4},{7,5},{8,10},{9,11},{10,... | collective-permute-start | bytes 18440 | tf_op jit(solution)/shard_map/ppermute | solution.py:433
  15.7 5.4 %collective-permute-start.6 = (f32[2,768]{1,0:T(2,128)S(1)}, f32[2,768]{1,0:T(2,128)S(1)}, u32[]{:S(2)}, u32[]{:S(2)}) collective-permute-start(f32[2,768]{1,0:T(2,128)S(1)} %get-tuple-element.40.refs_0_), channel_id=1, source_target_pairs={{0,1},{1,2},{2,3},{3,0},{4,5},{5,6},{6,7},{7,4},{8,9},{9,10},{10,1... | collective-permute-start | bytes 18440 | tf_op jit(solution)/shard_map/ppermute | solution.py:433
  17.3 3.9 %collective-permute-start.7 = (f32[2,768]{1,0:T(2,128)S(1)}, f32[2,768]{1,0:T(2,128)S(1)}, u32[]{:S(2)}, u32[]{:S(2)}) collective-permute-start(f32[2,768]{1,0:T(2,128)S(1)} %get-tuple-element.40.refs_0_), channel_id=1, source_target_pairs={{0,3},{1,0},{2,1},{3,2},{4,7},{5,4},{6,5},{7,6},{8,11},{9,8},{10,9... | collective-permute-start | bytes 18440 | tf_op jit(solution)/shard_map/ppermute | solution.py:433
  25.3 1.6 %collective-permute-start.8 = (bf16[176,128]{1,0:T(8,128)(2,1)S(1)}, bf16[176,128]{1,0:T(8,128)(2,1)S(1)}, u32[]{:S(2)}, u32[]{:S(2)}) collective-permute-start(bf16[176,128]{1,0:T(8,128)(2,1)S(1)} %get-tuple-element.42), channel_id=1, source_target_pairs={{0,4},{4,0},{8,12},{12,8},{16,20},{20,16},{24,28},{28,24},{1,5},{5... | collective-permute-start | bytes 135176 | tf_op jit(solution)/shard_map/ppermute | solution.py:437
  27.0 3.6 %collective-permute-start.10 = (bf16[192,128]{1,0:T(8,128)(2,1)S(1)}, bf16[192,128]{1,0:T(8,128)(2,1)S(1)}, u32[]{:S(2)}, u32[]{:S(2)}) collective-permute-start(bf16[192,128]{1,0:T(8,128)(2,1)S(1)} %pad_maximum_fusion), channel_id=1, source_target_pairs={{0,20},{4,16},{8,28},{12,24},{16,4},{20,0},{24,12},{28,8},{1,21},{... | collective-permute-start | bytes 147464 | tf_op jit(solution)/shard_map/ppermute | solution.py:437
  28.6 3.8 %collective-permute-start.11 = (bf16[192,128]{1,0:T(8,128)(2,1)S(1)}, bf16[192,128]{1,0:T(8,128)(2,1)S(1)}, u32[]{:S(2)}, u32[]{:S(2)}) collective-permute-start(bf16[192,128]{1,0:T(8,128)(2,1)S(1)} %pad_maximum_fusion), channel_id=1, source_target_pairs={{0,12},{4,8},{8,4},{12,0},{16,28},{20,24},{24,20},{28,16},{1,13},{... | collective-permute-start | bytes 147464 | tf_op jit(solution)/shard_map/ppermute | solution.py:437
  29.6 5.0 %collective-permute-start.9 = (bf16[192,128]{1,0:T(8,128)(2,1)S(1)}, bf16[192,128]{1,0:T(8,128)(2,1)S(1)}, u32[]{:S(2)}, u32[]{:S(2)}) collective-permute-start(bf16[192,128]{1,0:T(8,128)(2,1)S(1)} %pad_maximum_fusion), channel_id=1, source_target_pairs={{0,24},{4,28},{8,16},{12,20},{16,8},{20,12},{24,0},{28,4},{1,25},{... | collective-permute-start | bytes 147464 | tf_op jit(solution)/shard_map/ppermute | solution.py:437
  34.7 6.9 %collective-permute-start.12 = (bf16[160,128]{1,0:T(8,128)(2,1)S(1)}, bf16[160,128]{1,0:T(8,128)(2,1)S(1)}, u32[]{:S(2)}, u32[]{:S(2)}) collective-permute-start(bf16[160,128]{1,0:T(8,128)(2,1)S(1)} %reduce-precision_convert_fusion.1), channel_id=1, source_target_pairs={{0,2},{1,3},{2,0},{3,1},{4,6},{5,7},{6,4},{7,5},{8,10},{9,11},{10,... | collective-permute-start | bytes 122888 | tf_op jit(solution)/shard_map/ppermute | solution.py:433
  35.4 6.2 %collective-permute-start.13 = (bf16[160,128]{1,0:T(8,128)(2,1)S(1)}, bf16[160,128]{1,0:T(8,128)(2,1)S(1)}, u32[]{:S(2)}, u32[]{:S(2)}) collective-permute-start(bf16[160,128]{1,0:T(8,128)(2,1)S(1)} %reduce-precision_convert_fusion.1), channel_id=1, source_target_pairs={{0,1},{1,2},{2,3},{3,0},{4,5},{5,6},{6,7},{7,4},{8,9},{9,10},{10,1... | collective-permute-start | bytes 122888 | tf_op jit(solution)/shard_map/ppermute | solution.py:433
  39.1 4.0 %collective-permute-start.14 = (bf16[160,128]{1,0:T(8,128)(2,1)S(1)}, bf16[160,128]{1,0:T(8,128)(2,1)S(1)}, u32[]{:S(2)}, u32[]{:S(2)}) collective-permute-start(bf16[160,128]{1,0:T(8,128)(2,1)S(1)} %reduce-precision_convert_fusion.1), channel_id=1, source_target_pairs={{0,3},{1,0},{2,1},{3,2},{4,7},{5,4},{6,5},{7,6},{8,11},{9,8},{10,9... | collective-permute-start | bytes 122888 | tf_op jit(solution)/shard_map/ppermute | solution.py:433
  43.2 1.3 %collective-permute-start.15 = (bf16[160,128]{1,0:T(8,128)(2,1)S(1)}, bf16[160,128]{1,0:T(8,128)(2,1)S(1)}, u32[]{:S(2)}, u32[]{:S(2)}) collective-permute-start(bf16[160,128]{1,0:T(8,128)(2,1)S(1)} %reduce-precision_convert_fusion.own_ref), channel_id=1, source_target_pairs={{0,4},{4,0},{8,12},{12,8},{16,20},{20,16},{24,28},{28,24},{1,5},{5... | collective-permute-start | bytes 122888 | tf_op jit(solution)/shard_map/ppermute | solution.py:437

commit v5 on v4

--- a/solution.py
+++ b/solution.py
@@ -74,13 +74,15 @@
 
 
 def load_body(
-    x_hbm, k_hbm, caps_hbm, x_ref, first_ref, last_ref, taps_ref, caps_ref, sems
+    x_hbm, k_hbm, caps_hbm, x_ref, one_ref, two_ref, taps_ref, caps_ref, sems
 ):
-    rows, cols, channels = x_hbm.shape[1:]
+    rows = x_hbm.shape[1]
+    odd = lax.rem(lax.axis_index("space"), 2)
+    low, high = odd * (rows - SIDE), (1 - odd) * (rows - SIDE)
     copies = [
         pltpu.make_async_copy(k_hbm, taps_ref, sems.at[0]),
-        pltpu.make_async_copy(x_hbm.at[:, :SIDE], first_ref, sems.at[1]),
-        pltpu.make_async_copy(x_hbm.at[:, rows - SIDE :], last_ref, sems.at[2]),
+        pltpu.make_async_copy(x_hbm.at[:, pl.ds(high, SIDE)], one_ref, sems.at[1]),
+        pltpu.make_async_copy(x_hbm.at[:, pl.ds(low, SIDE)], two_ref, sems.at[2]),
         pltpu.make_async_copy(x_hbm, x_ref, sems.at[3]),
         pltpu.make_async_copy(caps_hbm, caps_ref, sems.at[4]),
     ]
@@ -90,17 +92,35 @@
         copy.wait()
 
 
-def conv_body(
-    x_ref, taps_ref, caps_ref, win_hbm, wout_hbm, part_ref, win_ref, wout_ref, same_caps_ref,
-    kw_ref, sems,
-):
-    images, rows, cols, channels = x_ref.shape
-    copies = [
-        pltpu.make_async_copy(win_hbm, win_ref, sems.at[0]),
-        pltpu.make_async_copy(wout_hbm, wout_ref, sems.at[1]),
-    ]
-    for copy in copies:
-        copy.start()
+def conv_rows(x_ref, kw_ref, part_ref, image):
+    rows, cols, channels = x_ref.shape[1:]
+
+    def tile(t, carry):
+        at = tile_at(t)
+        xs = [x_ref[image, r, :, at].astype(F32) for r in range(rows)]
+        outs = [None] * rows
+        for j in range(TAPS):
+            ws = [kw_ref[i * TAPS + j, :, at] for i in range(TAPS)]
+            for r in range(rows):
+                total = None
+                for i in range(TAPS):
+                    if 0 <= r + i - SIDE < rows:
+                        term = ws[i] * xs[r + i - SIDE]
+                        total = term if total is None else total + term
+                if j != SIDE:
+                    total = pltpu.roll(total, (SIDE - j) % cols, 0)
+                outs[r] = total if outs[r] is None else outs[r] + total
+        for r in range(rows):
+            part_ref[r, :, at] = outs[r]
+        return carry
+
+    lax.fori_loop(0, channels // LANES, tile, 0)
+
+
+def first_conv_body(x_ref, taps_ref, caps_ref, w_hbm, part_ref, kw_ref, same_caps_ref, w_ref, sem):
+    cols, channels = x_ref.shape[2:]
+    copy = pltpu.make_async_copy(w_hbm, w_ref, sem)
+    copy.start()
     same_caps_ref[...] = caps_ref[...]
     masks = column_masks(cols, channels)
     for i in range(TAPS):
@@ -108,30 +128,15 @@
         for j in range(TAPS):
             spread = jnp.broadcast_to(taps[j : j + 1], (cols, channels))
             kw_ref[i * TAPS + j] = jnp.where(masks[j], spread, 0.0)
-
-    def tile(t, carry):
-        at = tile_at(t)
-        for b in range(images):
-            xs = [x_ref[b, r, :, at].astype(F32) for r in range(rows)]
-            outs = [None] * rows
-            for j in range(TAPS):
-                ws = [kw_ref[i * TAPS + j, :, at] for i in range(TAPS)]
-                for r in range(rows):
-                    total = None
-                    for i in range(TAPS):
-                        if 0 <= r + i - SIDE < rows:
-                            term = ws[i] * xs[r + i - SIDE]
-                            total = term if total is None else total + term
-                    if j != SIDE:
-                        total = pltpu.roll(total, (SIDE - j) % cols, 0)
-                    outs[r] = total if outs[r] is None else outs[r] + total
-            for r in range(rows):
-                part_ref[b, r, :, at] = outs[r]
-        return carry
-
-    lax.fori_loop(0, channels // LANES, tile, 0)
-    for copy in copies:
-        copy.wait()
+    conv_rows(x_ref, kw_ref, part_ref, 0)
+    copy.wait()
+
+
+def later_conv_body(image, x_ref, kw_ref, w_hbm, part_ref, w_ref, sem):
+    copy = pltpu.make_async_copy(w_hbm, w_ref, sem)
+    copy.start()
+    conv_rows(x_ref, kw_ref, part_ref, image)
+    copy.wait()
 
 
 def gelu_tanh(values):
@@ -153,7 +158,7 @@
 
 
 def forward_body(
-    part_ref, below_ref, above_ref, kw_ref, x_ref, win_ref, wout_ref, caps_ref,
+    one_ref, two_ref, kw_ref, x_ref, win_ref, wout_ref, caps_ref, first_ref, second_ref,
     sums_ref, normed_ref, inv_ref, hid_ref, before_ref, after_ref, same_caps_ref,
     conv_ref, cast_ref, act_ref,
 ):
@@ -161,12 +166,14 @@
     hidden_units = win_ref.shape[1]
     pixels = rows * cols
     place = lax.axis_index("space")
+    odd = lax.rem(place, 2) == 1
     zeros = jnp.zeros((cols, channels), BF)
     for b in range(images):
         for q in range(SIDE):
-            before_ref[b, q] = jnp.where(place > 0, below_ref[b, q], zeros)
+            one, two = one_ref[b, q], two_ref[b, q]
+            before_ref[b, q] = jnp.where(place > 0, jnp.where(odd, one, two), zeros)
             after_ref[b, q] = jnp.where(
-                place < lax.axis_size("space") - 1, above_ref[b, q], zeros
+                place < lax.axis_size("space") - 1, jnp.where(odd, two, one), zeros
             )
 
     def tile(t, carry):
@@ -174,7 +181,8 @@
         for b in range(images):
             heads = [before_ref[b, q, :, at].astype(F32) for q in range(SIDE)]
             tails = [after_ref[b, q, :, at].astype(F32) for q in range(SIDE)]
-            outs = [part_ref[b, r, :, at] for r in range(rows)]
+            part_ref = (first_ref, second_ref)[b]
+            outs = [part_ref[r, :, at] for r in range(rows)]
             for j in range(TAPS):
                 ws = [kw_ref[i * TAPS + j, :, at] for i in range(TAPS)]
                 for r in list(range(SIDE)) + list(range(rows - SIDE, rows)):
@@ -230,7 +238,14 @@
         )
 
 
-def slope_body(hid_ref, slope_ref):
+def slope_body(hid_ref, x_ref, before_ref, after_ref, slope_ref, wide_ref):
+    images, rows = x_ref.shape[:2]
+    for b in range(images):
+        for q in range(SIDE):
+            wide_ref[b, q] = before_ref[b, q].astype(F32)
+            wide_ref[b, rows + SIDE + q] = after_ref[b, q].astype(F32)
+        for r in range(rows):
+            wide_ref[b, SIDE + r] = x_ref[b, r].astype(F32)
     for start in range(0, hid_ref.shape[1], 256):
         some = pl.ds(start, 256)
         slope_ref[:, some] = gelu_slope(hid_ref[:, some])
@@ -257,10 +272,12 @@
     cast_ref[...] = unit_rows(joined(bit, mine_ref, theirs_ref))[0].astype(BF)
 
 
-def kernel_sums(grad_ref, x_ref, before_ref, after_ref, list_ref, half):
-    images, rows, cols, channels = x_ref.shape
+def kernel_sums(grad_ref, wide_ref, list_ref, tap_ref, half):
+    images, padded_rows, cols, channels = wide_ref.shape
+    rows = padded_rows - 2 * SIDE
     masks = column_masks(cols)
     tiles = channels // LANES // 2
+    taps = TAPS * TAPS
 
     def tile(t, carry):
         at = tile_at(half * tiles + t)
@@ -271,23 +288,18 @@
                 for r in range(rows):
                     grad = grad_ref[pl.ds((b * rows + r) * cols, cols), at]
                     grads.append(grad if j == SIDE else pltpu.roll(grad, (j - SIDE) % cols, 0))
-                for q in range(rows + 2 * SIDE):
-                    if q < SIDE:
-                        here = before_ref[b, q, :, at]
-                    elif q < rows + SIDE:
-                        here = x_ref[b, q - SIDE, :, at]
-                    else:
-                        here = after_ref[b, q - rows - SIDE, :, at]
-                    here = here.astype(F32)
+                for q in range(padded_rows):
+                    here = wide_ref[b, q, :, at]
                     for i in range(TAPS):
                         if 0 <= q - i < rows:
                             term = here * grads[q - i]
                             sums[i] = term if sums[i] is None else sums[i] + term
             for i in range(TAPS):
-                kept = jnp.where(masks[j], sums[i], 0.0)
-                list_ref[pl.ds(t * TAPS * TAPS + i * TAPS + j, 1), :] = jnp.sum(
-                    kept, axis=0, keepdims=True
-                )
+                tap_ref[pl.ds((i * TAPS + j) * cols, cols), :] = jnp.where(masks[j], sums[i], 0.0)
+        total = tap_ref[pl.ds(0, taps, stride=cols), :]
+        for w in range(1, cols):
+            total = total + tap_ref[pl.ds(w, taps, stride=cols), :]
+        list_ref[pl.ds(t * taps, taps), :] = total
         return carry
 
     list_ref[...] = jnp.zeros_like(list_ref)
@@ -296,11 +308,11 @@
 
 def backward_body(
     scene_pixels, text_ref, pos_ref, slope_ref, normed_ref, inv_ref, win_ref, wout_ref,
-    x_ref, before_ref, after_ref, *refs,
+    wide_ref, *refs,
 ):
-    *part_refs, grad_ref, pay_ref, list_ref, hg_ref, row_ref = refs
-    images, rows, cols, channels = x_ref.shape
-    pixels = rows * cols
+    *part_refs, grad_ref, pay_ref, list_ref, tap_ref, hg_ref, row_ref = refs
+    images, padded_rows, cols, channels = wide_ref.shape
+    pixels = (padded_rows - 2 * SIDE) * cols
     count = text_ref.shape[0]
     pooled = pair_sum([ref[...] for ref in part_refs]) / scene_pixels
     image_unit, pooled_norm = unit_rows(pooled)
@@ -317,12 +329,9 @@
     positive = jnp.zeros((images, count), jnp.int32)
     for b in range(images):
         positive = jnp.where(row_at == b, pos_ref[b], positive)
-    place = lax.broadcasted_iota(jnp.int32, (images, count), 1)
-    core = (place >= count // 2).astype(jnp.int32)
-    rest = place - core * (count // 2)
-    group = rest // images
-    caption = (group * 2 + core) * images + (rest - group * images)
-    labels = jnp.where(positive == caption, 1.0, -1.0).astype(F32)
+    labels = jnp.where(
+        positive == lax.broadcasted_iota(jnp.int32, (images, count), 1), 1.0, -1.0
+    ).astype(F32)
     margin = -labels * logits
     losses = jnp.maximum(margin, 0.0) + jnp.log(1.0 + jnp.exp(-jnp.abs(margin)))
     loss_part = jnp.sum(jnp.sum(losses, axis=1, keepdims=True), axis=0, keepdims=True)
@@ -348,7 +357,7 @@
         - normed * jnp.mean(normed_grad * normed, axis=-1, keepdims=True)
     )
     half = 1 - own_half()
-    kernel_sums(grad_ref, x_ref, before_ref, after_ref, list_ref, half)
+    kernel_sums(grad_ref, wide_ref, list_ref, tap_ref, half)
     listed = list_ref.shape[0]
     pay_ref[0:listed, :] = list_ref[...].astype(BF)
 
@@ -372,9 +381,9 @@
     pay_ref[listed:, :] = row_ref[...].astype(BF)
 
 
-def own_half_body(grad_ref, x_ref, before_ref, after_ref, list_ref):
+def own_half_body(grad_ref, wide_ref, list_ref, tap_ref):
     half = own_half()
-    kernel_sums(grad_ref, x_ref, before_ref, after_ref, list_ref, half)
+    kernel_sums(grad_ref, wide_ref, list_ref, tap_ref, half)
 
 
 def text_body(rows_ref, caps_ref, text_ref, loss_ref, wide_ref):
@@ -384,8 +393,7 @@
     groups = lax.axis_size("dp")
     wide_ref[...] = rows_ref[...].astype(F32)
     lane = lax.broadcasted_iota(jnp.int32, (groups, LANES), 1)
-    me = lax.axis_index("dp")
-    first = (lax.rem(me, 2) * (groups // 2) + me // 2) * images
+    first = lax.axis_index("dp") * images
     caption_side = [[jnp.zeros((1, LANES), F32) for _ in range(chunks)] for _ in range(images)]
     loss = jnp.zeros((1, 1), F32)
     for b in range(images):
@@ -471,6 +479,25 @@
     return [mine, two, one, three]
 
 
+def flipped_parts(mine, axis, stride, members):
+    return [mine] + [flip(mine, axis, k * stride) for k in range(1, members)]
+
+
+def swap_edges(array, second):
+    dp, space = lax.axis_size("dp"), lax.axis_size("space")
+    pairs = []
+    for d in range(dp):
+        for s in range(space):
+            if not second:
+                other = d * space + (s ^ 1)
+            elif s in (0, space - 1):
+                other = (d ^ 1) * space + s
+            else:
+                other = d * space + ((s + 1) ^ 1) - 1
+            pairs.append((d * space + s, other))
+    return lax.ppermute(array, ("dp", "space"), pairs)
+
+
 def pair_sum(parts):
     parts = [part.astype(F32) for part in parts]
     while len(parts) > 1:
@@ -496,7 +523,7 @@
     scene_pixels = rows * space_count * cols
     edge = (images, SIDE, cols, channels)
 
-    x, first, last, taps, own_captions = call(
+    x, one, two, taps, own_captions = call(
         load_body,
         [
             (scenes.shape, BF),
@@ -509,26 +536,27 @@
         scratch=[pltpu.SemaphoreType.DMA((5,))],
         hbm=(0, 1, 2),
     )
-    below = shifted(last, "space", 1, 1, space_count)
-    above = shifted(first, "space", 1, space_count - 1, space_count)
+    one = swap_edges(one, False)
+    two = swap_edges(two, True)
+    theirs = flip(own_captions, "dp", 1)
+    part = (scenes.shape[1:], F32)
+    first, spread, gathered, win = call(
+        first_conv_body,
+        [part, ((TAPS * TAPS, cols, channels), F32), (captions.shape, BF), (weight_in.shape, BF)],
+        [x, taps, own_captions, weight_in],
+        scratch=[pltpu.SemaphoreType.DMA],
+        hbm=(3,),
+    )
+    gathered = rows_joined(join_body, gathered, theirs, 1)
     dp_bits = bits("dp")
-    theirs = flip(captions, "dp", dp_bits[1])
-    part, win, wout, same_captions, spread = call(
-        conv_body,
-        [
-            (scenes.shape, F32),
-            (weight_in.shape, BF),
-            (weight_out.shape, BF),
-            (captions.shape, BF),
-            ((TAPS * TAPS, cols, channels), F32),
-        ],
-        [x, taps, own_captions, weight_in, weight_out],
-        scratch=[pltpu.SemaphoreType.DMA((2,))],
-        hbm=(3, 4),
-    )
-
-    gathered = rows_joined(join_body, same_captions, theirs, dp_bits[1])
-    theirs = flip(gathered, "dp", dp_bits[2])
+    theirs = flip(gathered, "dp", dp_bits[1] + 1)
+    second, wout = call(
+        functools.partial(later_conv_body, 1),
+        [part, (weight_out.shape, BF)],
+        [x, spread, weight_out],
+        scratch=[pltpu.SemaphoreType.DMA],
+        hbm=(2,),
+    )
     sums, normed, inv, hidden, before, after, gathered = call(
         forward_body,
         [
@@ -540,22 +568,26 @@
             (edge, BF),
             (gathered.shape, BF),
         ],
-        [part, below, above, spread, x, win, wout, gathered],
+        [one, two, spread, x, win, wout, gathered, first, second],
         scratch=[
             pltpu.VMEM((pixels, channels), F32),
             pltpu.VMEM((pixels, channels), BF),
             pltpu.VMEM((3 * images + -3 * images % 8, hidden_units), F32),
         ],
     )
-    for bit in dp_bits[2:]:
+    for bit in dp_bits[1:-1]:
         gathered = rows_joined(join_body, gathered, theirs, bit)
-        theirs = flip(gathered, "dp", 1 if bit == dp_bits[-1] else 2 * bit)
-    text_cast = rows_joined(text_cast_body, gathered, theirs, 1)
+        theirs = flip(gathered, "dp", 2 * bit + 1)
+    text_cast = rows_joined(text_cast_body, gathered, theirs, dp_bits[-1])
     space_groups = groups(space_count, 1)
     for stride, members in space_groups[:-1]:
-        sums = group_sum(sums, "space", stride, members)
-    parts = group_parts(sums, "space", *space_groups[-1])
-    (slope,) = call(slope_body, [((pixels, hidden_units), F32)], [hidden])
+        sums = pair_sum(flipped_parts(sums, "space", stride, members))
+    parts = flipped_parts(sums, "space", *space_groups[-1])
+    slope, wide = call(
+        slope_body,
+        [((pixels, hidden_units), F32), ((images, rows + 2 * SIDE, cols, channels), F32)],
+        [hidden, x, before, after],
+    )
 
     listed = channels // LANES // 2 * TAPS * TAPS
     listed += -listed % 16
@@ -565,11 +597,11 @@
         functools.partial(backward_body, scene_pixels),
         [((pixels, channels), F32), ((listed + own_rows, LANES), BF)],
         [
-            text_cast, positives, slope, normed, inv, weight_in, weight_out, x, before, after,
-            *parts,
+            text_cast, positives, slope, normed, inv, weight_in, weight_out, wide, *parts,
         ],
         scratch=[
             pltpu.VMEM((listed, LANES), F32),
+            pltpu.VMEM((TAPS * TAPS * cols, LANES), F32),
             pltpu.VMEM((pixels, hidden_units), BF),
             pltpu.VMEM((own_rows, LANES), F32),
         ],
@@ -577,7 +609,10 @@
     )
     other = flip(pay, "dp", 1)
     (own,) = call(
-        own_half_body, [((listed, LANES), F32)], [grad, x, before, after]
+        own_half_body,
+        [((listed, LANES), F32)],
+        [grad, wide],
+        scratch=[pltpu.VMEM((TAPS * TAPS * cols, LANES), F32)],
     )
     total = own + other[:listed].astype(F32)
     units = join(pay[listed:], other[listed:], "dp", 1)

time: 45.3 us -> 43.4 us (0.958)
  starting transfers between devices: 21.1 us -> 19.5 us
  waiting for transfers between devices: 9.6 us -> 8.63 us
  Pallas kernels: 13.5 us -> 14 us
    ppermute x8 -> x3, starting transfers between devices: 14.4 us -> 4.62 us  [shifted(): return lax.ppermute(array, axis, pairs)]
    ppermute x8 -> x11, starting transfers between devices: 6.72 us -> 11.8 us  [flip(): lax.ppermute(array, axis, [(i, i ^ mask) for i in range(lax.axis_size(axi...]
    ppermute x0 -> x2, starting transfers between devices: none -> 3.09 us  [swap_edges(): return lax.ppermute(array, ('dp', 'space'), pairs)]
    ppermute x8 -> x3, waiting for transfers between devices: 4.55 us -> 2.36 us  [shifted(): return lax.ppermute(array, axis, pairs)]
    ppermute x8 -> x11, waiting for transfers between devices: 5.05 us -> 6.26 us  [flip(): lax.ppermute(array, axis, [(i, i ^ mask) for i in range(lax.axis_size(axi...]
    pallas_call x11 -> x12, Pallas kernels: 13.5 us -> 14 us  [call(): pl.pallas_call(body, out_shape=[placed_out(shape, dtype) for shape, dtype...]
  transfers between devices with their start and end apart: 16 -> 16, of which waited for: 8 -> 9; matrix products, arithmetic and copies ran while one was open for 0% -> 0% of each run, Pallas kernels for 17% -> 19%
where the time goes in v5:
time: 43.4 us; the launch traced here: 43.2 us
  starting transfers between devices  19.5 us (45%)
  Pallas kernels  14 us (32%)
  waiting for transfers between devices  8.63 us (20%)
  between operations  0.88 us (2%)
    pallas_call x12, Pallas kernels, call(): pl.pallas_call(body, out_shape=[placed_out(shape, dtype) for shape, dtype...  14 us
    ppermute x11, starting transfers between devices, flip(): lax.ppermute(array, axis, [(i, i ^ mask) for i in range(lax.axis_size(axi...  11.8 us
    ppermute x11, waiting for transfers between devices, flip(): lax.ppermute(array, axis, [(i, i ^ mask) for i in range(lax.axis_size(axi...  6.26 us
    ppermute x3, starting transfers between devices, shifted(): return lax.ppermute(array, axis, pairs)  4.62 us
    ppermute x2, starting transfers between devices, swap_edges(): return lax.ppermute(array, ('dp', 'space'), pairs)  3.09 us
    ppermute x3, waiting for transfers between devices, shifted(): return lax.ppermute(array, axis, pairs)  2.36 us
  transfers between devices with their start and end apart: 16, of which 9 were waited for; matrix products, arithmetic and copies ran while one was open for 0% of the time, Pallas kernels for 19%

profile of v5, /device:TPU:0, one launch (start us, length us, event | category | flops | bytes accessed | tf_op | source)
XLA Modules:
  0.0 43.2 jit_solution(16426206929475566298)
XLA Ops:
  0.6 1.1 %shard_map.85 = (bf16[2,14,8,768]{3,2,1,0:T(8,128)(2,1)S(1)}, bf16[2,3,8,768]{3,2,1,0:T(8,128)(2,1)S(1)}, bf16[2,3,8,768]{3,2,1,0:T(8,128)(2,1)S(1)}, bf16[7,7,768]{2,1,0:T(8,128)(2,1)S(1)}, bf16[2,768]{1,0:T(2,128)(2,1)S(1)}) custom-call(bf16[2,14,8,768]{3,2,1,0:T(8,128)(2,1)} %x_hbm.1, bf16[7,7,768]{2,1,0:T(8,128)(2,1)} %k_hbm.1, bf16[2,768]{1,0:T(2,128)(2,1)} %caps_hbm.1), custom_call_target="tpu_custom_call" | custom-call | tf_op jit(solution)/shard_map/pallas_call | solution.py:46
  1.8 3.1 %collective-permute-start = (bf16[2,3,8,768]{3,2,1,0:T(8,128)(2,1)S(1)}, bf16[2,3,8,768]{3,2,1,0:T(8,128)(2,1)S(1)}, u32[]{:S(2)}, u32[]{:S(2)}) collective-permute-start(bf16[2,3,8,768]{3,2,1,0:T(8,128)(2,1)S(1)} %get-tuple-element.27), channel_id=1, source_target_pairs={{0,1},{1,0},{2,3},{3,2},{4,5},{5,4},{6,7},{7,6},{8,9},{9,8},{10,11... | collective-permute-start | bytes 221192 | tf_op jit(solution)/shard_map/ppermute | solution.py:498
  4.9 0.0 collective-permute-start.1
  4.9 0.5 %collective-permute-start.2 = (bf16[2,768]{1,0:T(2,128)(2,1)S(1)}, bf16[2,768]{1,0:T(2,128)(2,1)S(1)}, u32[]{:S(2)}, u32[]{:S(2)}) collective-permute-start(bf16[2,768]{1,0:T(2,128)(2,1)S(1)} %get-tuple-element.31.caps_ref), channel_id=1, source_target_pairs={{0,4},{4,0},{8,12},{12,8},{16,20},{20,16},{24,28},{28,24},{1,5},{5... | collective-permute-start | bytes 9224 | tf_op jit(solution)/shard_map/ppermute | solution.py:445
  5.4 1.7 %shard_map.86 = (f32[14,8,768]{2,1,0:T(8,128)S(1)}, f32[49,8,768]{2,1,0:T(8,128)S(1)}, bf16[2,768]{1,0:T(2,128)(2,1)S(1)}, bf16[768,1536]{1,0:T(8,128)(2,1)S(1)}) custom-call(bf16[2,14,8,768]{3,2,1,0:T(8,128)(2,1)S(1)} %get-tuple-element.29.x_ref, bf16[7,7,768]{2,1,0:T(8,128)(2,1)S(1)} %get-tuple-element.30.taps_ref, ...), custom_call_target="tpu_custom_call" | custom-call | tf_op jit(solution)/shard_map/pallas_call | solution.py:46
  7.1 0.0 collective-permute-done.2.theirs_ref
  7.1 1.2 %collective-permute-start.3 = (bf16[4,768]{1,0:T(4,128)(2,1)S(1)}, bf16[4,768]{1,0:T(4,128)(2,1)S(1)}, u32[]{:S(2)}, u32[]{:S(2)}) collective-permute-start(bf16[4,768]{1,0:T(4,128)(2,1)S(1)} %shard_map.88.caps_ref), channel_id=1, source_target_pairs={{0,12},{4,8},{8,4},{12,0},{16,28},{20,24},{24,20},{28,16},{1,13},{... | collective-permute-start | bytes 18440 | tf_op jit(solution)/shard_map/ppermute | solution.py:445
  8.3 1.7 %shard_map.87 = (f32[14,8,768]{2,1,0:T(8,128)S(1)}, bf16[1536,768]{1,0:T(8,128)(2,1)S(1)}) custom-call(bf16[2,14,8,768]{3,2,1,0:T(8,128)(2,1)S(1)} %get-tuple-element.29.x_ref, f32[49,8,768]{2,1,0:T(8,128)S(1)} %get-tuple-element.32.kw_ref, bf16[1536,768]{1,0:T(8,128)(2,1)} %wout_ref.1), custom_call_target="tpu_custom_call" | custom-call | tf_op jit(solution)/shard_map/pallas_call | solution.py:46
  10.0 0.0 collective-permute-done.one_ref
  10.0 0.0 collective-permute-done.1.two_ref
  10.0 0.0 copy-start
  10.0 0.0 copy-start.1
  10.0 0.0 copy-start.2
  10.0 1.8 %shard_map.89 = (f32[2,768]{1,0:T(2,128)S(1)}, f32[224,768]{1,0:T(8,128)S(1)}, f32[224,128]{1,0:T(8,128)S(1)}, f32[224,1536]{1,0:T(8,128)S(1)}, bf16[2,3,8,768]{...) custom-call(bf16[2,3,8,768]{3,2,1,0:T(8,128)(2,1)S(1)} %collective-permute-done.one_ref, ...), custom_call_target="tpu_custom_call" | custom-call | tf_op jit(solution)/shard_map/pallas_call | solution.py:46
  11.8 0.0 collective-permute-done.3.theirs_ref
  11.9 1.7 %collective-permute-start.4 = (bf16[8,768]{1,0:T(8,128)(2,1)S(1)}, bf16[8,768]{1,0:T(8,128)(2,1)S(1)}, u32[]{:S(2)}, u32[]{:S(2)}) collective-permute-start(bf16[8,768]{1,0:T(8,128)(2,1)S(1)} %shard_map.90.mine_ref), channel_id=1, source_target_pairs={{0,20},{4,16},{8,28},{12,24},{16,4},{20,0},{24,12},{28,8},{1,21},{... | collective-permute-start | bytes 36872 | tf_op jit(solution)/shard_map/ppermute | solution.py:445
  13.6 2.6 %collective-permute-start.5 = (f32[2,768]{1,0:T(2,128)S(1)}, f32[2,768]{1,0:T(2,128)S(1)}, u32[]{:S(2)}, u32[]{:S(2)}) collective-permute-start(f32[2,768]{1,0:T(2,128)S(1)} %get-tuple-element.46.refs_0_), channel_id=1, source_target_pairs={{0,1},{1,0},{2,3},{3,2},{4,5},{5,4},{6,7},{7,6},{8,9},{9,8},{10,11... | collective-permute-start | bytes 18440 | tf_op jit(solution)/shard_map/ppermute | solution.py:445
  16.2 0.4 collective-permute-start.6
  16.6 2.0 %collective-permute-start.7 = (f32[2,768]{1,0:T(2,128)S(1)}, f32[2,768]{1,0:T(2,128)S(1)}, u32[]{:S(2)}, u32[]{:S(2)}) collective-permute-start(f32[2,768]{1,0:T(2,128)S(1)} %get-tuple-element.46.refs_0_), channel_id=1, source_target_pairs={{0,3},{1,2},{2,1},{3,0},{4,7},{5,6},{6,5},{7,4},{8,11},{9,10},{10,... | collective-permute-start | bytes 18440 | tf_op jit(solution)/shard_map/ppermute | solution.py:445
  18.6 0.9 %shard_map.92 = (f32[224,1536]{1,0:T(8,128)S(1)}, f32[2,20,8,768]{3,2,1,0:T(8,128)S(1)}) custom-call(f32[224,1536]{1,0:T(8,128)S(1)} %get-tuple-element.39.hid_ref, bf16[2,14,8,768]{3,2,1,0:T(8,128)(2,1)S(1)} %get-tuple-element.29.x_ref, bf16[2,3,8,768]{3,2,1,0:T(8,128)(2,1)S(1)} %get-tuple-element.40.before_ref, ...), custom_call_target="tpu_custom_call" | custom-call | tf_op jit(solution)/shard_map/pallas_call | solution.py:46
  19.5 0.0 collective-permute-done.4.theirs_ref
  19.5 0.1 shard_map.91.text_ref
  19.6 0.0 collective-permute-done.5.refs_1_
  19.6 1.2 %collective-permute-done.6.refs_2_ = f32[2,768]{1,0:T(2,128)S(1)} collective-permute-done((f32[2,768]{1,0:T(2,128)S(1)}, f32[2,768]{1,0:T(2,128)S(1)}, u32[]{:S(2)}, u32[]{:S(2)}) %collective-permute-start.6) | collective-permute-done | bytes 6176 | tf_op jit(solution)/shard_map/ppermute | solution.py:445
  20.8 1.3 %collective-permute-done.7.refs_3_ = f32[2,768]{1,0:T(2,128)S(1)} collective-permute-done((f32[2,768]{1,0:T(2,128)S(1)}, f32[2,768]{1,0:T(2,128)S(1)}, u32[]{:S(2)}, u32[]{:S(2)}) %collective-permute-start.7) | collective-permute-done | bytes 6176 | tf_op jit(solution)/shard_map/ppermute | solution.py:445
  22.1 0.0 copy-done
  22.1 0.0 copy-done.1
  22.1 0.0 copy-done.2
  22.1 3.9 %shard_map.93 = (f32[224,768]{1,0:T(8,128)S(1)}, bf16[176,128]{1,0:T(8,128)(2,1)S(1)}) custom-call(bf16[16,768]{1,0:T(8,128)(2,1)S(1)} %shard_map.91.text_ref, s32[2]{0:T(128)S(1)} %copy-done.2, f32[224,1536]{1,0:T(8,128)S(1)} %get-tuple-element.42.slope_ref, f32[224,768]{1,0:T(8,128)S(1)} %get-tuple-element.43.normed_ref, ...), custom_call_target="tpu_custom_call" | custom-call | tf_op jit(solution)/shard_map/pallas_call | solution.py:46
  25.9 0.1 collective-permute-start.8
  26.0 1.3 %shard_map.94 = f32[160,128]{1,0:T(8,128)S(1)} custom-call(f32[224,768]{1,0:T(8,128)S(1)} %get-tuple-element.47.grad_ref, f32[2,20,8,768]{3,2,1,0:T(8,128)S(1)} %get-tuple-element.45.wide_ref), custom_call_target="tpu_custom_call" | custom-call | tf_op jit(solution)/shard_map/pallas_call | solution.py:46
  27.3 0.0 collective-permute-done.8
  27.4 0.7 %collective-permute-start.10 = (bf16[192,128]{1,0:T(8,128)(2,1)S(1)}, bf16[192,128]{1,0:T(8,128)(2,1)S(1)}, u32[]{:S(2)}, u32[]{:S(2)}) collective-permute-start(bf16[192,128]{1,0:T(8,128)(2,1)S(1)} %pad_maximum_fusion), channel_id=1, source_target_pairs={{0,20},{4,16},{8,28},{12,24},{16,4},{20,0},{24,12},{28,8},{1,21},{... | collective-permute-start | bytes 147464 | tf_op jit(solution)/shard_map/ppermute | solution.py:445
  28.0 0.2 collective-permute-start.11
  28.2 2.4 %collective-permute-start.9 = (bf16[192,128]{1,0:T(8,128)(2,1)S(1)}, bf16[192,128]{1,0:T(8,128)(2,1)S(1)}, u32[]{:S(2)}, u32[]{:S(2)}) collective-permute-start(bf16[192,128]{1,0:T(8,128)(2,1)S(1)} %pad_maximum_fusion), channel_id=1, source_target_pairs={{0,24},{4,28},{8,16},{12,20},{16,8},{20,12},{24,0},{28,4},{1,25},{... | collective-permute-start | bytes 147464 | tf_op jit(solution)/shard_map/ppermute | solution.py:445
  30.7 0.3 collective-permute-done.10
  31.0 0.9 %collective-permute-done.11 = bf16[192,128]{1,0:T(8,128)(2,1)S(1)} collective-permute-done((bf16[192,128]{1,0:T(8,128)(2,1)S(1)}, bf16[192,128]{1,0:T(8,128)(2,1)S(1)}, u32[]{:S(2)}, u32[]{:S(2)}) %collective-permute-start.11) | collective-permute-done | bytes 49184 | tf_op jit(solution)/shard_map/ppermute | solution.py:445
  31.9 2.2 %collective-permute-done.9 = bf16[192,128]{1,0:T(8,128)(2,1)S(1)} collective-permute-done((bf16[192,128]{1,0:T(8,128)(2,1)S(1)}, bf16[192,128]{1,0:T(8,128)(2,1)S(1)}, u32[]{:S(2)}, u32[]{:S(2)}) %collective-permute-start.9) | collective-permute-done | bytes 49184 | tf_op jit(solution)/shard_map/ppermute | solution.py:445
  34.1 0.8 %collective-permute-start.12 = (bf16[160,128]{1,0:T(8,128)(2,1)S(1)}, bf16[160,128]{1,0:T(8,128)(2,1)S(1)}, u32[]{:S(2)}, u32[]{:S(2)}) collective-permute-start(bf16[160,128]{1,0:T(8,128)(2,1)S(1)} %reduce-precision_convert_fusion.1), channel_id=1, source_target_pairs={{0,2},{1,3},{2,0},{3,1},{4,6},{5,7},{6,4},{7,5},{8,10},{9,11},{10,... | collective-permute-start | bytes 122888 | tf_op jit(solution)/shard_map/ppermute | solution.py:441
  34.9 1.8 %collective-permute-start.13 = (bf16[160,128]{1,0:T(8,128)(2,1)S(1)}, bf16[160,128]{1,0:T(8,128)(2,1)S(1)}, u32[]{:S(2)}, u32[]{:S(2)}) collective-permute-start(bf16[160,128]{1,0:T(8,128)(2,1)S(1)} %reduce-precision_convert_fusion.1), channel_id=1, source_target_pairs={{0,1},{1,2},{2,3},{3,0},{4,5},{5,6},{6,7},{7,4},{8,9},{9,10},{10,1... | collective-permute-start | bytes 122888 | tf_op jit(solution)/shard_map/ppermute | solution.py:441
  36.7 2.0 %collective-permute-start.14 = (bf16[160,128]{1,0:T(8,128)(2,1)S(1)}, bf16[160,128]{1,0:T(8,128)(2,1)S(1)}, u32[]{:S(2)}, u32[]{:S(2)}) collective-permute-start(bf16[160,128]{1,0:T(8,128)(2,1)S(1)} %reduce-precision_convert_fusion.1), channel_id=1, source_target_pairs={{0,3},{1,0},{2,1},{3,2},{4,7},{5,4},{6,5},{7,6},{8,11},{9,8},{10,9... | collective-permute-start | bytes 122888 | tf_op jit(solution)/shard_map/ppermute | solution.py:441
  38.8 0.9 %collective-permute-done.12 = bf16[160,128]{1,0:T(8,128)(2,1)S(1)} collective-permute-done((bf16[160,128]{1,0:T(8,128)(2,1)S(1)}, bf16[160,128]{1,0:T(8,128)(2,1)S(1)}, u32[]{:S(2)}, u32[]{:S(2)}) %collective-permute-start.12) | collective-permute-done | bytes 40992 | tf_op jit(solution)/shard_map/ppermute | solution.py:441
  39.7 1.1 %collective-permute-done.13 = bf16[160,128]{1,0:T(8,128)(2,1)S(1)} collective-permute-done((bf16[160,128]{1,0:T(8,128)(2,1)S(1)}, bf16[160,128]{1,0:T(8,128)(2,1)S(1)}, u32[]{:S(2)}, u32[]{:S(2)}) %collective-permute-start.13) | collective-permute-done | bytes 40992 | tf_op jit(solution)/shard_map/ppermute | solution.py:441
  40.8 0.4 collective-permute-done.14
  41.2 0.1 collective-permute-start.15
  41.3 0.8 %shard_map.95 = (f32[2,768]{1,0:T(2,128)}, f32[1,1]{1,0:T(1,128)}) custom-call(bf16[128,128]{1,0:T(8,128)(2,1)S(1)} %maximum_select_fusion.rows_ref, bf16[2,768]{1,0:T(2,128)(2,1)S(1)} %get-tuple-element.31.caps_ref), custom_call_target="tpu_custom_call" | custom-call | tf_op jit(solution)/shard_map/pallas_call | solution.py:46
  42.1 0.4 collective-permute-done.15.other_ref
  42.5 0.7 %shard_map.96 = f32[7,7,768]{2,1,0:T(8,128)} custom-call(bf16[160,128]{1,0:T(8,128)(2,1)S(1)} %reduce-precision_convert_fusion.own_ref, bf16[160,128]{1,0:T(8,128)(2,1)S(1)} %collective-permute-done.15.other_ref), custom_call_target="tpu_custom_call" | custom-call | tf_op jit(solution)/shard_map/pallas_call | solution.py:46
  (15 shorter events, 0.2 us)
Async XLA Ops:
  1.8 8.2 %collective-permute-start = (bf16[2,3,8,768]{3,2,1,0:T(8,128)(2,1)S(1)}, bf16[2,3,8,768]{3,2,1,0:T(8,128)(2,1)S(1)}, u32[]{:S(2)}, u32[]{:S(2)}) collective-permute-start(bf16[2,3,8,768]{3,2,1,0:T(8,128)(2,1)S(1)} %get-tuple-element.27), channel_id=1, source_target_pairs={{0,1},{1,0},{2,3},{3,2},{4,5},{5,4},{6,7},{7,6},{8,9},{9,8},{10,11... | collective-permute-start | bytes 221192 | tf_op jit(solution)/shard_map/ppermute | solution.py:498
  4.9 5.1 %collective-permute-start.1 = (bf16[2,3,8,768]{3,2,1,0:T(8,128)(2,1)S(1)}, bf16[2,3,8,768]{3,2,1,0:T(8,128)(2,1)S(1)}, u32[]{:S(2)}, u32[]{:S(2)}) collective-permute-start(bf16[2,3,8,768]{3,2,1,0:T(8,128)(2,1)S(1)} %get-tuple-element.28), channel_id=1, source_target_pairs={{0,4},{1,2},{2,1},{3,7},{4,0},{5,6},{6,5},{7,3},{8,12},{9,10},{10,... | collective-permute-start | bytes 221192 | tf_op jit(solution)/shard_map/ppermute | solution.py:498
  4.9 2.2 %collective-permute-start.2 = (bf16[2,768]{1,0:T(2,128)(2,1)S(1)}, bf16[2,768]{1,0:T(2,128)(2,1)S(1)}, u32[]{:S(2)}, u32[]{:S(2)}) collective-permute-start(bf16[2,768]{1,0:T(2,128)(2,1)S(1)} %get-tuple-element.31.caps_ref), channel_id=1, source_target_pairs={{0,4},{4,0},{8,12},{12,8},{16,20},{20,16},{24,28},{28,24},{1,5},{5... | collective-permute-start | bytes 9224 | tf_op jit(solution)/shard_map/ppermute | solution.py:445
  7.1 4.7 %collective-permute-start.3 = (bf16[4,768]{1,0:T(4,128)(2,1)S(1)}, bf16[4,768]{1,0:T(4,128)(2,1)S(1)}, u32[]{:S(2)}, u32[]{:S(2)}) collective-permute-start(bf16[4,768]{1,0:T(4,128)(2,1)S(1)} %shard_map.88.caps_ref), channel_id=1, source_target_pairs={{0,12},{4,8},{8,4},{12,0},{16,28},{20,24},{24,20},{28,16},{1,13},{... | collective-permute-start | bytes 18440 | tf_op jit(solution)/shard_map/ppermute | solution.py:445
  10.0 12.1 %copy-start = (bf16[768,1536]{1,0:T(8,128)(2,1)S(1)}, bf16[768,1536]{1,0:T(8,128)(2,1)}, u32[]{:S(2)}) copy-start(bf16[768,1536]{1,0:T(8,128)(2,1)} %win_ref.1) | copy-start | bytes 7077892
  10.0 12.1 %copy-start.1 = (bf16[1536,768]{1,0:T(8,128)(2,1)S(1)}, bf16[1536,768]{1,0:T(8,128)(2,1)}, u32[]{:S(2)}) copy-start(bf16[1536,768]{1,0:T(8,128)(2,1)} %wout_ref.1) | copy-start | bytes 7077892
  10.0 12.1 %copy-start.2 = (s32[2]{0:T(128)S(1)}, s32[2]{0:T(128)}, u32[]{:S(2)}) copy-start(s32[2]{0:T(128)} %pos_ref.1) | copy-start | bytes 28
  11.9 7.6 %collective-permute-start.4 = (bf16[8,768]{1,0:T(8,128)(2,1)S(1)}, bf16[8,768]{1,0:T(8,128)(2,1)S(1)}, u32[]{:S(2)}, u32[]{:S(2)}) collective-permute-start(bf16[8,768]{1,0:T(8,128)(2,1)S(1)} %shard_map.90.mine_ref), channel_id=1, source_target_pairs={{0,20},{4,16},{8,28},{12,24},{16,4},{20,0},{24,12},{28,8},{1,21},{... | collective-permute-start | bytes 36872 | tf_op jit(solution)/shard_map/ppermute | solution.py:445
  13.6 6.0 %collective-permute-start.5 = (f32[2,768]{1,0:T(2,128)S(1)}, f32[2,768]{1,0:T(2,128)S(1)}, u32[]{:S(2)}, u32[]{:S(2)}) collective-permute-start(f32[2,768]{1,0:T(2,128)S(1)} %get-tuple-element.46.refs_0_), channel_id=1, source_target_pairs={{0,1},{1,0},{2,3},{3,2},{4,5},{5,4},{6,7},{7,6},{8,9},{9,8},{10,11... | collective-permute-start | bytes 18440 | tf_op jit(solution)/shard_map/ppermute | solution.py:445
  16.2 4.5 %collective-permute-start.6 = (f32[2,768]{1,0:T(2,128)S(1)}, f32[2,768]{1,0:T(2,128)S(1)}, u32[]{:S(2)}, u32[]{:S(2)}) collective-permute-start(f32[2,768]{1,0:T(2,128)S(1)} %get-tuple-element.46.refs_0_), channel_id=1, source_target_pairs={{0,2},{1,3},{2,0},{3,1},{4,6},{5,7},{6,4},{7,5},{8,10},{9,11},{10,... | collective-permute-start | bytes 18440 | tf_op jit(solution)/shard_map/ppermute | solution.py:445
  16.6 5.4 %collective-permute-start.7 = (f32[2,768]{1,0:T(2,128)S(1)}, f32[2,768]{1,0:T(2,128)S(1)}, u32[]{:S(2)}, u32[]{:S(2)}) collective-permute-start(f32[2,768]{1,0:T(2,128)S(1)} %get-tuple-element.46.refs_0_), channel_id=1, source_target_pairs={{0,3},{1,2},{2,1},{3,0},{4,7},{5,6},{6,5},{7,4},{8,11},{9,10},{10,... | collective-permute-start | bytes 18440 | tf_op jit(solution)/shard_map/ppermute | solution.py:445
  25.9 1.4 %collective-permute-start.8 = (bf16[176,128]{1,0:T(8,128)(2,1)S(1)}, bf16[176,128]{1,0:T(8,128)(2,1)S(1)}, u32[]{:S(2)}, u32[]{:S(2)}) collective-permute-start(bf16[176,128]{1,0:T(8,128)(2,1)S(1)} %get-tuple-element.48), channel_id=1, source_target_pairs={{0,4},{4,0},{8,12},{12,8},{16,20},{20,16},{24,28},{28,24},{1,5},{5... | collective-permute-start | bytes 135176 | tf_op jit(solution)/shard_map/ppermute | solution.py:445
  27.4 3.6 %collective-permute-start.10 = (bf16[192,128]{1,0:T(8,128)(2,1)S(1)}, bf16[192,128]{1,0:T(8,128)(2,1)S(1)}, u32[]{:S(2)}, u32[]{:S(2)}) collective-permute-start(bf16[192,128]{1,0:T(8,128)(2,1)S(1)} %pad_maximum_fusion), channel_id=1, source_target_pairs={{0,20},{4,16},{8,28},{12,24},{16,4},{20,0},{24,12},{28,8},{1,21},{... | collective-permute-start | bytes 147464 | tf_op jit(solution)/shard_map/ppermute | solution.py:445
  28.0 3.8 %collective-permute-start.11 = (bf16[192,128]{1,0:T(8,128)(2,1)S(1)}, bf16[192,128]{1,0:T(8,128)(2,1)S(1)}, u32[]{:S(2)}, u32[]{:S(2)}) collective-permute-start(bf16[192,128]{1,0:T(8,128)(2,1)S(1)} %pad_maximum_fusion), channel_id=1, source_target_pairs={{0,12},{4,8},{8,4},{12,0},{16,28},{20,24},{24,20},{28,16},{1,13},{... | collective-permute-start | bytes 147464 | tf_op jit(solution)/shard_map/ppermute | solution.py:445
  28.2 5.9 %collective-permute-start.9 = (bf16[192,128]{1,0:T(8,128)(2,1)S(1)}, bf16[192,128]{1,0:T(8,128)(2,1)S(1)}, u32[]{:S(2)}, u32[]{:S(2)}) collective-permute-start(bf16[192,128]{1,0:T(8,128)(2,1)S(1)} %pad_maximum_fusion), channel_id=1, source_target_pairs={{0,24},{4,28},{8,16},{12,20},{16,8},{20,12},{24,0},{28,4},{1,25},{... | collective-permute-start | bytes 147464 | tf_op jit(solution)/shard_map/ppermute | solution.py:445
  34.1 5.5 %collective-permute-start.12 = (bf16[160,128]{1,0:T(8,128)(2,1)S(1)}, bf16[160,128]{1,0:T(8,128)(2,1)S(1)}, u32[]{:S(2)}, u32[]{:S(2)}) collective-permute-start(bf16[160,128]{1,0:T(8,128)(2,1)S(1)} %reduce-precision_convert_fusion.1), channel_id=1, source_target_pairs={{0,2},{1,3},{2,0},{3,1},{4,6},{5,7},{6,4},{7,5},{8,10},{9,11},{10,... | collective-permute-start | bytes 122888 | tf_op jit(solution)/shard_map/ppermute | solution.py:441
  34.9 5.8 %collective-permute-start.13 = (bf16[160,128]{1,0:T(8,128)(2,1)S(1)}, bf16[160,128]{1,0:T(8,128)(2,1)S(1)}, u32[]{:S(2)}, u32[]{:S(2)}) collective-permute-start(bf16[160,128]{1,0:T(8,128)(2,1)S(1)} %reduce-precision_convert_fusion.1), channel_id=1, source_target_pairs={{0,1},{1,2},{2,3},{3,0},{4,5},{5,6},{6,7},{7,4},{8,9},{9,10},{10,1... | collective-permute-start | bytes 122888 | tf_op jit(solution)/shard_map/ppermute | solution.py:441
  36.7 4.4 %collective-permute-start.14 = (bf16[160,128]{1,0:T(8,128)(2,1)S(1)}, bf16[160,128]{1,0:T(8,128)(2,1)S(1)}, u32[]{:S(2)}, u32[]{:S(2)}) collective-permute-start(bf16[160,128]{1,0:T(8,128)(2,1)S(1)} %reduce-precision_convert_fusion.1), channel_id=1, source_target_pairs={{0,3},{1,0},{2,1},{3,2},{4,7},{5,4},{6,5},{7,6},{8,11},{9,8},{10,9... | collective-permute-start | bytes 122888 | tf_op jit(solution)/shard_map/ppermute | solution.py:441
  41.2 1.3 %collective-permute-start.15 = (bf16[160,128]{1,0:T(8,128)(2,1)S(1)}, bf16[160,128]{1,0:T(8,128)(2,1)S(1)}, u32[]{:S(2)}, u32[]{:S(2)}) collective-permute-start(bf16[160,128]{1,0:T(8,128)(2,1)S(1)} %reduce-precision_convert_fusion.own_ref), channel_id=1, source_target_pairs={{0,4},{4,0},{8,12},{12,8},{16,20},{20,16},{24,28},{28,24},{1,5},{5... | collective-permute-start | bytes 122888 | tf_op jit(solution)/shard_map/ppermute | solution.py:445

commit v6 on v5

--- a/solution.py
+++ b/solution.py
@@ -73,18 +73,14 @@
     return lax.rem(odd, 2)
 
 
-def load_body(
-    x_hbm, k_hbm, caps_hbm, x_ref, one_ref, two_ref, taps_ref, caps_ref, sems
-):
+def load_body(x_hbm, caps_hbm, one_ref, two_ref, caps_ref, sems):
     rows = x_hbm.shape[1]
     odd = lax.rem(lax.axis_index("space"), 2)
     low, high = odd * (rows - SIDE), (1 - odd) * (rows - SIDE)
     copies = [
-        pltpu.make_async_copy(k_hbm, taps_ref, sems.at[0]),
-        pltpu.make_async_copy(x_hbm.at[:, pl.ds(high, SIDE)], one_ref, sems.at[1]),
-        pltpu.make_async_copy(x_hbm.at[:, pl.ds(low, SIDE)], two_ref, sems.at[2]),
-        pltpu.make_async_copy(x_hbm, x_ref, sems.at[3]),
-        pltpu.make_async_copy(caps_hbm, caps_ref, sems.at[4]),
+        pltpu.make_async_copy(x_hbm.at[:, pl.ds(high, SIDE)], one_ref, sems.at[0]),
+        pltpu.make_async_copy(x_hbm.at[:, pl.ds(low, SIDE)], two_ref, sems.at[1]),
+        pltpu.make_async_copy(caps_hbm, caps_ref, sems.at[2]),
     ]
     for copy in copies:
         copy.start()
@@ -117,26 +113,32 @@
     lax.fori_loop(0, channels // LANES, tile, 0)
 
 
-def first_conv_body(x_ref, taps_ref, caps_ref, w_hbm, part_ref, kw_ref, same_caps_ref, w_ref, sem):
-    cols, channels = x_ref.shape[2:]
-    copy = pltpu.make_async_copy(w_hbm, w_ref, sem)
-    copy.start()
+def first_conv_body(
+    x_hbm, taps_hbm, w_hbm, caps_ref, x_ref, part_ref, kw_ref, same_caps_ref, w_ref, taps_ref, sems
+):
+    cols, channels = x_hbm.shape[2:]
+    copies = [
+        pltpu.make_async_copy(taps_hbm, taps_ref, sems.at[0]),
+        pltpu.make_async_copy(x_hbm, x_ref, sems.at[1]),
+        pltpu.make_async_copy(w_hbm, w_ref, sems.at[2]),
+    ]
+    for copy in copies:
+        copy.start()
     same_caps_ref[...] = caps_ref[...]
     masks = column_masks(cols, channels)
+    copies[0].wait()
     for i in range(TAPS):
         taps = taps_ref[i].astype(F32)
         for j in range(TAPS):
             spread = jnp.broadcast_to(taps[j : j + 1], (cols, channels))
             kw_ref[i * TAPS + j] = jnp.where(masks[j], spread, 0.0)
+    copies[1].wait()
     conv_rows(x_ref, kw_ref, part_ref, 0)
-    copy.wait()
-
-
-def later_conv_body(image, x_ref, kw_ref, w_hbm, part_ref, w_ref, sem):
-    copy = pltpu.make_async_copy(w_hbm, w_ref, sem)
-    copy.start()
+    copies[2].wait()
+
+
+def later_conv_body(image, x_ref, kw_ref, part_ref):
     conv_rows(x_ref, kw_ref, part_ref, image)
-    copy.wait()
 
 
 def gelu_tanh(values):
@@ -238,7 +240,12 @@
         )
 
 
-def slope_body(hid_ref, x_ref, before_ref, after_ref, slope_ref, wide_ref):
+def slope_body(
+    hid_ref, x_ref, before_ref, after_ref, win_ref, wout_ref,
+    slope_ref, wide_ref, win_t_ref, wout_t_ref,
+):
+    win_t_ref[...] = win_ref[...].T
+    wout_t_ref[...] = wout_ref[...].T
     images, rows = x_ref.shape[:2]
     for b in range(images):
         for q in range(SIDE):
@@ -269,7 +276,8 @@
 
 
 def text_cast_body(bit, mine_ref, theirs_ref, cast_ref):
-    cast_ref[...] = unit_rows(joined(bit, mine_ref, theirs_ref))[0].astype(BF)
+    unit = unit_rows(joined(bit, mine_ref, theirs_ref))[0]
+    cast_ref[...] = unit.astype(BF).astype(F32)
 
 
 def kernel_sums(grad_ref, wide_ref, list_ref, tap_ref, half):
@@ -307,7 +315,7 @@
 
 
 def backward_body(
-    scene_pixels, text_ref, pos_ref, slope_ref, normed_ref, inv_ref, win_ref, wout_ref,
+    scene_pixels, text_ref, pos_ref, slope_ref, normed_ref, inv_ref, win_t_ref, wout_t_ref,
     wide_ref, *refs,
 ):
     *part_refs, grad_ref, pay_ref, list_ref, tap_ref, hg_ref, row_ref = refs
@@ -318,38 +326,27 @@
     image_unit, pooled_norm = unit_rows(pooled)
     image_cast = image_unit.astype(BF)
     text_cast = text_ref[...]
-    logits = (
-        LOGIT_SCALE
-        * lax.dot_general(
-            image_cast, text_cast, (((1,), (1,)), ((), ())), preferred_element_type=F32
-        )
-        + LOGIT_BIAS
-    )
-    row_at = lax.broadcasted_iota(jnp.int32, (images, count), 0)
-    positive = jnp.zeros((images, count), jnp.int32)
+    at = lax.broadcasted_iota(jnp.int32, (count, 1), 0)
+    sides, pair_grads, losses = [], [], []
     for b in range(images):
-        positive = jnp.where(row_at == b, pos_ref[b], positive)
-    labels = jnp.where(
-        positive == lax.broadcasted_iota(jnp.int32, (images, count), 1), 1.0, -1.0
-    ).astype(F32)
-    margin = -labels * logits
-    losses = jnp.maximum(margin, 0.0) + jnp.log(1.0 + jnp.exp(-jnp.abs(margin)))
-    loss_part = jnp.sum(jnp.sum(losses, axis=1, keepdims=True), axis=0, keepdims=True)
-    pair_grad = (-labels / (1.0 + jnp.exp(-margin))).astype(BF)
-    image_side = LOGIT_SCALE * jnp.dot(pair_grad, text_cast, preferred_element_type=F32)
+        unit = image_cast[b : b + 1].astype(F32)
+        logits = LOGIT_SCALE * jnp.sum(unit * text_cast, axis=1, keepdims=True) + LOGIT_BIAS
+        labels = jnp.where(at == pos_ref[b], 1.0, -1.0).astype(F32)
+        margin = -labels * logits
+        pair_grad = (-labels / (1.0 + jnp.exp(-margin))).astype(BF).astype(F32)
+        sides.append(LOGIT_SCALE * jnp.sum(pair_grad * text_cast, axis=0, keepdims=True))
+        pair_grads.append(pair_grad)
+        losses.append(jnp.maximum(margin, 0.0) + jnp.log(1.0 + jnp.exp(-jnp.abs(margin))))
+    image_side = jnp.concatenate(sides, axis=0)
     pooled_grad = (
         image_side - image_unit * jnp.sum(image_unit * image_side, axis=-1, keepdims=True)
     ) / pooled_norm
     slope = (pooled_grad / scene_pixels).astype(BF)
-    act_grad = lax.dot_general(
-        slope, wout_ref[...], (((1,), (1,)), ((), ())), preferred_element_type=F32
-    )
+    act_grad = jnp.dot(slope, wout_t_ref[...], preferred_element_type=F32)
     for b in range(images):
         some = pl.ds(b * pixels, pixels)
         hg_ref[some, :] = (act_grad[b : b + 1] * slope_ref[some, :]).astype(BF)
-    normed_grad = lax.dot_general(
-        hg_ref[...], win_ref[...], (((1,), (1,)), ((), ())), preferred_element_type=F32
-    )
+    normed_grad = jnp.dot(hg_ref[...], win_t_ref[...], preferred_element_type=F32)
     normed = normed_ref[...]
     grad_ref[...] = inv_ref[:, 0:1] * (
         normed_grad
@@ -363,21 +360,23 @@
 
     row_ref[...] = jnp.zeros_like(row_ref)
     chunks = channels // LANES
-    high, mid, low = three_terms(loss_part)
+    high, mid, low = three_terms(jnp.sum(sum(losses), axis=0, keepdims=True))
     lane = lax.broadcasted_iota(jnp.int32, (1, LANES), 1)
+    row_at = lax.broadcasted_iota(jnp.int32, (count, LANES), 0)
+    column = lax.broadcasted_iota(jnp.int32, (count, LANES), 1)
     for b in range(images):
         for c in range(chunks):
             row_ref[b * (chunks + 1) + c : b * (chunks + 1) + c + 1, :] = image_cast[
                 b : b + 1, c * LANES : (c + 1) * LANES
             ].astype(F32)
         at = b * (chunks + 1) + chunks
-        row_ref[at : at + 1, 0:count] = pair_grad[b : b + 1, :].astype(F32)
+        placed = jnp.where(column == row_at, pair_grads[b], 0.0)
+        known = jnp.sum(placed, axis=0, keepdims=True)
         if b == 0:
-            known = row_ref[at : at + 1, :]
             known = jnp.where(lane == LANES - 3, high, known)
             known = jnp.where(lane == LANES - 2, mid, known)
             known = jnp.where(lane == LANES - 1, low, known)
-            row_ref[at : at + 1, :] = known
+        row_ref[at : at + 1, :] = known
     pay_ref[listed:, :] = row_ref[...].astype(BF)
 
 
@@ -509,9 +508,9 @@
     return pair_sum(group_parts(mine, axis, stride, members))
 
 
-def rows_joined(body, mine, theirs, bit):
+def rows_joined(body, mine, theirs, bit, dtype=BF):
     shape = (2 * mine.shape[0], mine.shape[1])
-    (out,) = call(functools.partial(body, bit), [(shape, BF)], [mine, theirs])
+    (out,) = call(functools.partial(body, bit), [(shape, dtype)], [mine, theirs])
     return out
 
 
@@ -523,40 +522,34 @@
     scene_pixels = rows * space_count * cols
     edge = (images, SIDE, cols, channels)
 
-    x, one, two, taps, own_captions = call(
+    one, two, own_captions = call(
         load_body,
-        [
-            (scenes.shape, BF),
-            (edge, BF),
-            (edge, BF),
-            (kernel.shape, BF),
-            (captions.shape, BF),
-        ],
-        [scenes, kernel, captions],
-        scratch=[pltpu.SemaphoreType.DMA((5,))],
-        hbm=(0, 1, 2),
+        [(edge, BF), (edge, BF), (captions.shape, BF)],
+        [scenes, captions],
+        scratch=[pltpu.SemaphoreType.DMA((3,))],
+        hbm=(0, 1),
     )
     one = swap_edges(one, False)
     two = swap_edges(two, True)
     theirs = flip(own_captions, "dp", 1)
     part = (scenes.shape[1:], F32)
-    first, spread, gathered, win = call(
+    x, first, spread, gathered, wout = call(
         first_conv_body,
-        [part, ((TAPS * TAPS, cols, channels), F32), (captions.shape, BF), (weight_in.shape, BF)],
-        [x, taps, own_captions, weight_in],
-        scratch=[pltpu.SemaphoreType.DMA],
-        hbm=(3,),
+        [
+            (scenes.shape, BF),
+            part,
+            ((TAPS * TAPS, cols, channels), F32),
+            (captions.shape, BF),
+            (weight_out.shape, BF),
+        ],
+        [scenes, kernel, weight_out, own_captions],
+        scratch=[pltpu.VMEM(kernel.shape, BF), pltpu.SemaphoreType.DMA((3,))],
+        hbm=(0, 1, 2),
     )
     gathered = rows_joined(join_body, gathered, theirs, 1)
     dp_bits = bits("dp")
     theirs = flip(gathered, "dp", dp_bits[1] + 1)
-    second, wout = call(
-        functools.partial(later_conv_body, 1),
-        [part, (weight_out.shape, BF)],
-        [x, spread, weight_out],
-        scratch=[pltpu.SemaphoreType.DMA],
-        hbm=(2,),
-    )
+    (second,) = call(functools.partial(later_conv_body, 1), [part], [x, spread])
     sums, normed, inv, hidden, before, after, gathered = call(
         forward_body,
         [
@@ -568,7 +561,7 @@
             (edge, BF),
             (gathered.shape, BF),
         ],
-        [one, two, spread, x, win, wout, gathered, first, second],
+        [one, two, spread, x, weight_in, wout, gathered, first, second],
         scratch=[
             pltpu.VMEM((pixels, channels), F32),
             pltpu.VMEM((pixels, channels), BF),
@@ -578,15 +571,20 @@
     for bit in dp_bits[1:-1]:
         gathered = rows_joined(join_body, gathered, theirs, bit)
         theirs = flip(gathered, "dp", 2 * bit + 1)
-    text_cast = rows_joined(text_cast_body, gathered, theirs, dp_bits[-1])
+    text_cast = rows_joined(text_cast_body, gathered, theirs, dp_bits[-1], F32)
     space_groups = groups(space_count, 1)
     for stride, members in space_groups[:-1]:
         sums = pair_sum(flipped_parts(sums, "space", stride, members))
     parts = flipped_parts(sums, "space", *space_groups[-1])
-    slope, wide = call(
+    slope, wide, win_t, wout_t = call(
         slope_body,
-        [((pixels, hidden_units), F32), ((images, rows + 2 * SIDE, cols, channels), F32)],
-        [hidden, x, before, after],
+        [
+            ((pixels, hidden_units), F32),
+            ((images, rows + 2 * SIDE, cols, channels), F32),
+            (weight_out.shape, BF),
+            (weight_in.shape, BF),
+        ],
+        [hidden, x, before, after, weight_in, wout],
     )
 
     listed = channels // LANES // 2 * TAPS * TAPS
@@ -597,7 +595,7 @@
         functools.partial(backward_body, scene_pixels),
         [((pixels, channels), F32), ((listed + own_rows, LANES), BF)],
         [
-            text_cast, positives, slope, normed, inv, weight_in, weight_out, wide, *parts,
+            text_cast, positives, slope, normed, inv, win_t, wout_t, wide, *parts,
         ],
         scratch=[
             pltpu.VMEM((listed, LANES), F32),

time: 43.4 us -> 42.4 us (0.977)
  waiting for transfers between devices: 8.63 us -> 7.06 us
  Pallas kernels: 14 us -> 14.6 us
    ppermute x11, waiting for transfers between devices: 6.26 us -> 4.69 us  [flip(): lax.ppermute(array, axis, [(i, i ^ mask) for i in range(lax.axis_size(axi...]
    pallas_call x12, Pallas kernels: 14 us -> 14.6 us  [call(): pl.pallas_call(body, out_shape=[placed_out(shape, dtype) for shape, dtype...]
  transfers between devices with their start and end apart: 16 -> 16, of which waited for: 9 -> 8; matrix products, arithmetic and copies ran while one was open for 0% -> 0% of each run, Pallas kernels for 19% -> 23%
where the time goes in v6:
time: 42.4 us; the launch traced here: 42.2 us
  starting transfers between devices  19.5 us (46%)
  Pallas kernels  14.6 us (34%)
  waiting for transfers between devices  7.06 us (17%)
  between operations  0.88 us (2%)
    pallas_call x12, Pallas kernels, call(): pl.pallas_call(body, out_shape=[placed_out(shape, dtype) for shape, dtype...  14.6 us
    ppermute x11, starting transfers between devices, flip(): lax.ppermute(array, axis, [(i, i ^ mask) for i in range(lax.axis_size(axi...  11.8 us
    ppermute x11, waiting for transfers between devices, flip(): lax.ppermute(array, axis, [(i, i ^ mask) for i in range(lax.axis_size(axi...  4.69 us
    ppermute x3, starting transfers between devices, shifted(): return lax.ppermute(array, axis, pairs)  4.62 us
    ppermute x2, starting transfers between devices, swap_edges(): return lax.ppermute(array, ('dp', 'space'), pairs)  3.09 us
    ppermute x3, waiting for transfers between devices, shifted(): return lax.ppermute(array, axis, pairs)  2.36 us
  transfers between devices with their start and end apart: 16, of which 8 were waited for; matrix products, arithmetic and copies ran while one was open for 0% of the time, Pallas kernels for 23%

profile of v6, /device:TPU:0, one launch (start us, length us, event | category | flops | bytes accessed | tf_op | source)
XLA Modules:
  0.0 42.2 jit_solution(2652277652469492926)
XLA Ops:
  0.6 1.0 %shard_map.85 = (bf16[2,3,8,768]{3,2,1,0:T(8,128)(2,1)S(1)}, bf16[2,3,8,768]{3,2,1,0:T(8,128)(2,1)S(1)}, bf16[2,768]{1,0:T(2,128)(2,1)S(1)}) custom-call(bf16[2,14,8,768]{3,2,1,0:T(8,128)(2,1)} %x_hbm.3, bf16[2,768]{1,0:T(2,128)(2,1)} %caps_hbm.1), custom_call_target="tpu_custom_call" | custom-call | tf_op jit(solution)/shard_map/pallas_call | solution.py:46
  1.6 0.0 copy-start
  1.6 3.1 %collective-permute-start = (bf16[2,3,8,768]{3,2,1,0:T(8,128)(2,1)S(1)}, bf16[2,3,8,768]{3,2,1,0:T(8,128)(2,1)S(1)}, u32[]{:S(2)}, u32[]{:S(2)}) collective-permute-start(bf16[2,3,8,768]{3,2,1,0:T(8,128)(2,1)S(1)} %get-tuple-element.26), channel_id=1, source_target_pairs={{0,1},{1,0},{2,3},{3,2},{4,5},{5,4},{6,7},{7,6},{8,9},{9,8},{10,11... | collective-permute-start | bytes 221192 | tf_op jit(solution)/shard_map/ppermute | solution.py:497
  4.7 0.0 collective-permute-start.1
  4.7 0.5 %collective-permute-start.2 = (bf16[2,768]{1,0:T(2,128)(2,1)S(1)}, bf16[2,768]{1,0:T(2,128)(2,1)S(1)}, u32[]{:S(2)}, u32[]{:S(2)}) collective-permute-start(bf16[2,768]{1,0:T(2,128)(2,1)S(1)} %get-tuple-element.28.caps_ref), channel_id=1, source_target_pairs={{0,4},{4,0},{8,12},{12,8},{16,20},{20,16},{24,28},{28,24},{1,5},{5... | collective-permute-start | bytes 9224 | tf_op jit(solution)/shard_map/ppermute | solution.py:444
  5.2 2.1 %shard_map.86 = (bf16[2,14,8,768]{3,2,1,0:T(8,128)(2,1)S(1)}, f32[14,8,768]{2,1,0:T(8,128)S(1)}, f32[49,8,768]{2,1,0:T(8,128)S(1)}, bf16[2,768]{1,0:T(2,128)(2,1)S(1)}, bf16[1536,768]{1,0:T(8,128)(2,1)S(1)}) custom-call(bf16[2,14,8,768]{3,2,1,0:T(8,128)(2,1)} %x_hbm.3, bf16[7,7,768]{2,1,0:T(8,128)(2,1)} %taps_hbm.1, bf16[1536,768]{1,0:T(8,128)(2,1)} %w_hbm.1, ...), custom_call_target="tpu_custom_call" | custom-call | tf_op jit(solution)/shard_map/pallas_call | solution.py:46
  7.3 0.0 collective-permute-done.2.theirs_ref
  7.4 1.2 %collective-permute-start.3 = (bf16[4,768]{1,0:T(4,128)(2,1)S(1)}, bf16[4,768]{1,0:T(4,128)(2,1)S(1)}, u32[]{:S(2)}, u32[]{:S(2)}) collective-permute-start(bf16[4,768]{1,0:T(4,128)(2,1)S(1)} %shard_map.87.caps_ref), channel_id=1, source_target_pairs={{0,12},{4,8},{8,4},{12,0},{16,28},{20,24},{24,20},{28,16},{1,13},{... | collective-permute-start | bytes 18440 | tf_op jit(solution)/shard_map/ppermute | solution.py:444
  8.5 1.1 %shard_map.88.second_ref = f32[14,8,768]{2,1,0:T(8,128)S(1)} custom-call(bf16[2,14,8,768]{3,2,1,0:T(8,128)(2,1)S(1)} %get-tuple-element.30.x_ref, f32[49,8,768]{2,1,0:T(8,128)S(1)} %get-tuple-element.29.kw_ref), custom_call_target="tpu_custom_call" | custom-call | tf_op jit(solution)/shard_map/pallas_call | solution.py:46
  9.6 0.0 collective-permute-done.one_ref
  9.6 0.0 collective-permute-done.1.two_ref
  9.6 0.0 copy-done
  9.6 1.8 %shard_map.89 = (f32[2,768]{1,0:T(2,128)S(1)}, f32[224,768]{1,0:T(8,128)S(1)}, f32[224,128]{1,0:T(8,128)S(1)}, f32[224,1536]{1,0:T(8,128)S(1)}, bf16[2,3,8,768]{...) custom-call(bf16[2,3,8,768]{3,2,1,0:T(8,128)(2,1)S(1)} %collective-permute-done.one_ref, ...), custom_call_target="tpu_custom_call" | custom-call | tf_op jit(solution)/shard_map/pallas_call | solution.py:46
  11.5 0.0 collective-permute-done.3.theirs_ref
  11.5 1.7 %collective-permute-start.4 = (bf16[8,768]{1,0:T(8,128)(2,1)S(1)}, bf16[8,768]{1,0:T(8,128)(2,1)S(1)}, u32[]{:S(2)}, u32[]{:S(2)}) collective-permute-start(bf16[8,768]{1,0:T(8,128)(2,1)S(1)} %shard_map.90.mine_ref), channel_id=1, source_target_pairs={{0,20},{4,16},{8,28},{12,24},{16,4},{20,0},{24,12},{28,8},{1,21},{... | collective-permute-start | bytes 36872 | tf_op jit(solution)/shard_map/ppermute | solution.py:444
  13.2 2.6 %collective-permute-start.5 = (f32[2,768]{1,0:T(2,128)S(1)}, f32[2,768]{1,0:T(2,128)S(1)}, u32[]{:S(2)}, u32[]{:S(2)}) collective-permute-start(f32[2,768]{1,0:T(2,128)S(1)} %get-tuple-element.44.refs_0_), channel_id=1, source_target_pairs={{0,1},{1,0},{2,3},{3,2},{4,5},{5,4},{6,7},{7,6},{8,9},{9,8},{10,11... | collective-permute-start | bytes 18440 | tf_op jit(solution)/shard_map/ppermute | solution.py:444
  15.8 0.4 collective-permute-start.6
  16.2 2.0 %collective-permute-start.7 = (f32[2,768]{1,0:T(2,128)S(1)}, f32[2,768]{1,0:T(2,128)S(1)}, u32[]{:S(2)}, u32[]{:S(2)}) collective-permute-start(f32[2,768]{1,0:T(2,128)S(1)} %get-tuple-element.44.refs_0_), channel_id=1, source_target_pairs={{0,3},{1,2},{2,1},{3,0},{4,7},{5,6},{6,5},{7,4},{8,11},{9,10},{10,... | collective-permute-start | bytes 18440 | tf_op jit(solution)/shard_map/ppermute | solution.py:444
  18.2 0.0 copy-start.1
  18.2 2.4 %shard_map.92 = (f32[224,1536]{1,0:T(8,128)S(1)}, f32[2,20,8,768]{3,2,1,0:T(8,128)S(1)}, bf16[1536,768]{1,0:T(8,128)(2,1)S(1)}, bf16[768,1536]{1,0:T(8,128)(2,1)S(1)}) custom-call(f32[224,1536]{1,0:T(8,128)S(1)} %get-tuple-element.35.hid_ref, bf16[2,14,8,768]{3,2,1,0:T(8,128)(2,1)S(1)} %get-tuple-element.30.x_ref, ...), custom_call_target="tpu_custom_call" | custom-call | tf_op jit(solution)/shard_map/pallas_call | solution.py:46
  20.6 0.0 collective-permute-done.4.theirs_ref
  20.6 0.1 shard_map.91.text_ref
  20.8 0.0 collective-permute-done.5.refs_1_
  20.8 0.0 collective-permute-done.6.refs_2_
  20.8 0.9 %collective-permute-done.7.refs_3_ = f32[2,768]{1,0:T(2,128)S(1)} collective-permute-done((f32[2,768]{1,0:T(2,128)S(1)}, f32[2,768]{1,0:T(2,128)S(1)}, u32[]{:S(2)}, u32[]{:S(2)}) %collective-permute-start.7) | collective-permute-done | bytes 6176 | tf_op jit(solution)/shard_map/ppermute | solution.py:444
  21.7 0.0 copy-done.1
  21.7 3.3 %shard_map.93 = (f32[224,768]{1,0:T(8,128)S(1)}, bf16[176,128]{1,0:T(8,128)(2,1)S(1)}) custom-call(f32[16,768]{1,0:T(8,128)S(1)} %shard_map.91.text_ref, s32[2]{0:T(128)S(1)} %copy-done.1, f32[224,1536]{1,0:T(8,128)S(1)} %get-tuple-element.38.slope_ref, f32[224,768]{1,0:T(8,128)S(1)} %get-tuple-element.39.normed_ref, ...), custom_call_target="tpu_custom_call" | custom-call | tf_op jit(solution)/shard_map/pallas_call | solution.py:46
  25.0 0.1 collective-permute-start.8
  25.0 1.3 %shard_map.94 = f32[160,128]{1,0:T(8,128)S(1)} custom-call(f32[224,768]{1,0:T(8,128)S(1)} %get-tuple-element.45.grad_ref, f32[2,20,8,768]{3,2,1,0:T(8,128)S(1)} %get-tuple-element.43.wide_ref), custom_call_target="tpu_custom_call" | custom-call | tf_op jit(solution)/shard_map/pallas_call | solution.py:46
  26.3 0.0 collective-permute-done.8
  26.4 0.7 %collective-permute-start.10 = (bf16[192,128]{1,0:T(8,128)(2,1)S(1)}, bf16[192,128]{1,0:T(8,128)(2,1)S(1)}, u32[]{:S(2)}, u32[]{:S(2)}) collective-permute-start(bf16[192,128]{1,0:T(8,128)(2,1)S(1)} %pad_maximum_fusion), channel_id=1, source_target_pairs={{0,20},{4,16},{8,28},{12,24},{16,4},{20,0},{24,12},{28,8},{1,21},{... | collective-permute-start | bytes 147464 | tf_op jit(solution)/shard_map/ppermute | solution.py:444
  27.1 0.2 collective-permute-start.11
  27.2 2.4 %collective-permute-start.9 = (bf16[192,128]{1,0:T(8,128)(2,1)S(1)}, bf16[192,128]{1,0:T(8,128)(2,1)S(1)}, u32[]{:S(2)}, u32[]{:S(2)}) collective-permute-start(bf16[192,128]{1,0:T(8,128)(2,1)S(1)} %pad_maximum_fusion), channel_id=1, source_target_pairs={{0,24},{4,28},{8,16},{12,20},{16,8},{20,12},{24,0},{28,4},{1,25},{... | collective-permute-start | bytes 147464 | tf_op jit(solution)/shard_map/ppermute | solution.py:444
  29.7 0.3 collective-permute-done.10
  30.0 0.9 %collective-permute-done.11 = bf16[192,128]{1,0:T(8,128)(2,1)S(1)} collective-permute-done((bf16[192,128]{1,0:T(8,128)(2,1)S(1)}, bf16[192,128]{1,0:T(8,128)(2,1)S(1)}, u32[]{:S(2)}, u32[]{:S(2)}) %collective-permute-start.11) | collective-permute-done | bytes 49184 | tf_op jit(solution)/shard_map/ppermute | solution.py:444
  30.9 2.2 %collective-permute-done.9 = bf16[192,128]{1,0:T(8,128)(2,1)S(1)} collective-permute-done((bf16[192,128]{1,0:T(8,128)(2,1)S(1)}, bf16[192,128]{1,0:T(8,128)(2,1)S(1)}, u32[]{:S(2)}, u32[]{:S(2)}) %collective-permute-start.9) | collective-permute-done | bytes 49184 | tf_op jit(solution)/shard_map/ppermute | solution.py:444
  33.1 0.8 %collective-permute-start.12 = (bf16[160,128]{1,0:T(8,128)(2,1)S(1)}, bf16[160,128]{1,0:T(8,128)(2,1)S(1)}, u32[]{:S(2)}, u32[]{:S(2)}) collective-permute-start(bf16[160,128]{1,0:T(8,128)(2,1)S(1)} %reduce-precision_convert_fusion.1), channel_id=1, source_target_pairs={{0,2},{1,3},{2,0},{3,1},{4,6},{5,7},{6,4},{7,5},{8,10},{9,11},{10,... | collective-permute-start | bytes 122888 | tf_op jit(solution)/shard_map/ppermute | solution.py:440
  33.9 1.8 %collective-permute-start.13 = (bf16[160,128]{1,0:T(8,128)(2,1)S(1)}, bf16[160,128]{1,0:T(8,128)(2,1)S(1)}, u32[]{:S(2)}, u32[]{:S(2)}) collective-permute-start(bf16[160,128]{1,0:T(8,128)(2,1)S(1)} %reduce-precision_convert_fusion.1), channel_id=1, source_target_pairs={{0,1},{1,2},{2,3},{3,0},{4,5},{5,6},{6,7},{7,4},{8,9},{9,10},{10,1... | collective-permute-start | bytes 122888 | tf_op jit(solution)/shard_map/ppermute | solution.py:440
  35.7 2.0 %collective-permute-start.14 = (bf16[160,128]{1,0:T(8,128)(2,1)S(1)}, bf16[160,128]{1,0:T(8,128)(2,1)S(1)}, u32[]{:S(2)}, u32[]{:S(2)}) collective-permute-start(bf16[160,128]{1,0:T(8,128)(2,1)S(1)} %reduce-precision_convert_fusion.1), channel_id=1, source_target_pairs={{0,3},{1,0},{2,1},{3,2},{4,7},{5,4},{6,5},{7,6},{8,11},{9,8},{10,9... | collective-permute-start | bytes 122888 | tf_op jit(solution)/shard_map/ppermute | solution.py:440
  37.8 1.2 %collective-permute-done.12 = bf16[160,128]{1,0:T(8,128)(2,1)S(1)} collective-permute-done((bf16[160,128]{1,0:T(8,128)(2,1)S(1)}, bf16[160,128]{1,0:T(8,128)(2,1)S(1)}, u32[]{:S(2)}, u32[]{:S(2)}) %collective-permute-start.12) | collective-permute-done | bytes 40992 | tf_op jit(solution)/shard_map/ppermute | solution.py:440
  39.0 0.8 %collective-permute-done.13 = bf16[160,128]{1,0:T(8,128)(2,1)S(1)} collective-permute-done((bf16[160,128]{1,0:T(8,128)(2,1)S(1)}, bf16[160,128]{1,0:T(8,128)(2,1)S(1)}, u32[]{:S(2)}, u32[]{:S(2)}) %collective-permute-start.13) | collective-permute-done | bytes 40992 | tf_op jit(solution)/shard_map/ppermute | solution.py:440
  39.8 0.4 collective-permute-done.14
  40.2 0.1 collective-permute-start.15
  40.3 0.8 %shard_map.95 = (f32[2,768]{1,0:T(2,128)}, f32[1,1]{1,0:T(1,128)}) custom-call(bf16[128,128]{1,0:T(8,128)(2,1)S(1)} %maximum_select_fusion.rows_ref, bf16[2,768]{1,0:T(2,128)(2,1)S(1)} %get-tuple-element.28.caps_ref), custom_call_target="tpu_custom_call" | custom-call | tf_op jit(solution)/shard_map/pallas_call | solution.py:46
  41.1 0.4 collective-permute-done.15.other_ref
  41.5 0.7 %shard_map.96 = f32[7,7,768]{2,1,0:T(8,128)} custom-call(bf16[160,128]{1,0:T(8,128)(2,1)S(1)} %reduce-precision_convert_fusion.own_ref, bf16[160,128]{1,0:T(8,128)(2,1)S(1)} %collective-permute-done.15.other_ref), custom_call_target="tpu_custom_call" | custom-call | tf_op jit(solution)/shard_map/pallas_call | solution.py:46
  (15 shorter events, 0.2 us)
Async XLA Ops:
  1.6 8.0 %copy-start = (bf16[768,1536]{1,0:T(8,128)(2,1)S(1)}, bf16[768,1536]{1,0:T(8,128)(2,1)}, u32[]{:S(2)}) copy-start(bf16[768,1536]{1,0:T(8,128)(2,1)} %win_ref.3) | copy-start | bytes 7077892
  1.6 8.0 %collective-permute-start = (bf16[2,3,8,768]{3,2,1,0:T(8,128)(2,1)S(1)}, bf16[2,3,8,768]{3,2,1,0:T(8,128)(2,1)S(1)}, u32[]{:S(2)}, u32[]{:S(2)}) collective-permute-start(bf16[2,3,8,768]{3,2,1,0:T(8,128)(2,1)S(1)} %get-tuple-element.26), channel_id=1, source_target_pairs={{0,1},{1,0},{2,3},{3,2},{4,5},{5,4},{6,7},{7,6},{8,9},{9,8},{10,11... | collective-permute-start | bytes 221192 | tf_op jit(solution)/shard_map/ppermute | solution.py:497
  4.7 4.9 %collective-permute-start.1 = (bf16[2,3,8,768]{3,2,1,0:T(8,128)(2,1)S(1)}, bf16[2,3,8,768]{3,2,1,0:T(8,128)(2,1)S(1)}, u32[]{:S(2)}, u32[]{:S(2)}) collective-permute-start(bf16[2,3,8,768]{3,2,1,0:T(8,128)(2,1)S(1)} %get-tuple-element.27), channel_id=1, source_target_pairs={{0,4},{1,2},{2,1},{3,7},{4,0},{5,6},{6,5},{7,3},{8,12},{9,10},{10,... | collective-permute-start | bytes 221192 | tf_op jit(solution)/shard_map/ppermute | solution.py:497
  4.7 2.6 %collective-permute-start.2 = (bf16[2,768]{1,0:T(2,128)(2,1)S(1)}, bf16[2,768]{1,0:T(2,128)(2,1)S(1)}, u32[]{:S(2)}, u32[]{:S(2)}) collective-permute-start(bf16[2,768]{1,0:T(2,128)(2,1)S(1)} %get-tuple-element.28.caps_ref), channel_id=1, source_target_pairs={{0,4},{4,0},{8,12},{12,8},{16,20},{20,16},{24,28},{28,24},{1,5},{5... | collective-permute-start | bytes 9224 | tf_op jit(solution)/shard_map/ppermute | solution.py:444
  7.4 4.1 %collective-permute-start.3 = (bf16[4,768]{1,0:T(4,128)(2,1)S(1)}, bf16[4,768]{1,0:T(4,128)(2,1)S(1)}, u32[]{:S(2)}, u32[]{:S(2)}) collective-permute-start(bf16[4,768]{1,0:T(4,128)(2,1)S(1)} %shard_map.87.caps_ref), channel_id=1, source_target_pairs={{0,12},{4,8},{8,4},{12,0},{16,28},{20,24},{24,20},{28,16},{1,13},{... | collective-permute-start | bytes 18440 | tf_op jit(solution)/shard_map/ppermute | solution.py:444
  11.5 9.1 %collective-permute-start.4 = (bf16[8,768]{1,0:T(8,128)(2,1)S(1)}, bf16[8,768]{1,0:T(8,128)(2,1)S(1)}, u32[]{:S(2)}, u32[]{:S(2)}) collective-permute-start(bf16[8,768]{1,0:T(8,128)(2,1)S(1)} %shard_map.90.mine_ref), channel_id=1, source_target_pairs={{0,20},{4,16},{8,28},{12,24},{16,4},{20,0},{24,12},{28,8},{1,21},{... | collective-permute-start | bytes 36872 | tf_op jit(solution)/shard_map/ppermute | solution.py:444
  13.2 7.6 %collective-permute-start.5 = (f32[2,768]{1,0:T(2,128)S(1)}, f32[2,768]{1,0:T(2,128)S(1)}, u32[]{:S(2)}, u32[]{:S(2)}) collective-permute-start(f32[2,768]{1,0:T(2,128)S(1)} %get-tuple-element.44.refs_0_), channel_id=1, source_target_pairs={{0,1},{1,0},{2,3},{3,2},{4,5},{5,4},{6,7},{7,6},{8,9},{9,8},{10,11... | collective-permute-start | bytes 18440 | tf_op jit(solution)/shard_map/ppermute | solution.py:444
  15.8 4.9 %collective-permute-start.6 = (f32[2,768]{1,0:T(2,128)S(1)}, f32[2,768]{1,0:T(2,128)S(1)}, u32[]{:S(2)}, u32[]{:S(2)}) collective-permute-start(f32[2,768]{1,0:T(2,128)S(1)} %get-tuple-element.44.refs_0_), channel_id=1, source_target_pairs={{0,2},{1,3},{2,0},{3,1},{4,6},{5,7},{6,4},{7,5},{8,10},{9,11},{10,... | collective-permute-start | bytes 18440 | tf_op jit(solution)/shard_map/ppermute | solution.py:444
  16.2 5.4 %collective-permute-start.7 = (f32[2,768]{1,0:T(2,128)S(1)}, f32[2,768]{1,0:T(2,128)S(1)}, u32[]{:S(2)}, u32[]{:S(2)}) collective-permute-start(f32[2,768]{1,0:T(2,128)S(1)} %get-tuple-element.44.refs_0_), channel_id=1, source_target_pairs={{0,3},{1,2},{2,1},{3,0},{4,7},{5,6},{6,5},{7,4},{8,11},{9,10},{10,... | collective-permute-start | bytes 18440 | tf_op jit(solution)/shard_map/ppermute | solution.py:444
  18.2 3.5 %copy-start.1 = (s32[2]{0:T(128)S(1)}, s32[2]{0:T(128)}, u32[]{:S(2)}) copy-start(s32[2]{0:T(128)} %pos_ref.1) | copy-start | bytes 28
  25.0 1.4 %collective-permute-start.8 = (bf16[176,128]{1,0:T(8,128)(2,1)S(1)}, bf16[176,128]{1,0:T(8,128)(2,1)S(1)}, u32[]{:S(2)}, u32[]{:S(2)}) collective-permute-start(bf16[176,128]{1,0:T(8,128)(2,1)S(1)} %get-tuple-element.46), channel_id=1, source_target_pairs={{0,4},{4,0},{8,12},{12,8},{16,20},{20,16},{24,28},{28,24},{1,5},{5... | collective-permute-start | bytes 135176 | tf_op jit(solution)/shard_map/ppermute | solution.py:444
  26.4 3.6 %collective-permute-start.10 = (bf16[192,128]{1,0:T(8,128)(2,1)S(1)}, bf16[192,128]{1,0:T(8,128)(2,1)S(1)}, u32[]{:S(2)}, u32[]{:S(2)}) collective-permute-start(bf16[192,128]{1,0:T(8,128)(2,1)S(1)} %pad_maximum_fusion), channel_id=1, source_target_pairs={{0,20},{4,16},{8,28},{12,24},{16,4},{20,0},{24,12},{28,8},{1,21},{... | collective-permute-start | bytes 147464 | tf_op jit(solution)/shard_map/ppermute | solution.py:444
  27.1 3.8 %collective-permute-start.11 = (bf16[192,128]{1,0:T(8,128)(2,1)S(1)}, bf16[192,128]{1,0:T(8,128)(2,1)S(1)}, u32[]{:S(2)}, u32[]{:S(2)}) collective-permute-start(bf16[192,128]{1,0:T(8,128)(2,1)S(1)} %pad_maximum_fusion), channel_id=1, source_target_pairs={{0,12},{4,8},{8,4},{12,0},{16,28},{20,24},{24,20},{28,16},{1,13},{... | collective-permute-start | bytes 147464 | tf_op jit(solution)/shard_map/ppermute | solution.py:444
  27.2 5.9 %collective-permute-start.9 = (bf16[192,128]{1,0:T(8,128)(2,1)S(1)}, bf16[192,128]{1,0:T(8,128)(2,1)S(1)}, u32[]{:S(2)}, u32[]{:S(2)}) collective-permute-start(bf16[192,128]{1,0:T(8,128)(2,1)S(1)} %pad_maximum_fusion), channel_id=1, source_target_pairs={{0,24},{4,28},{8,16},{12,20},{16,8},{20,12},{24,0},{28,4},{1,25},{... | collective-permute-start | bytes 147464 | tf_op jit(solution)/shard_map/ppermute | solution.py:444
  33.1 5.8 %collective-permute-start.12 = (bf16[160,128]{1,0:T(8,128)(2,1)S(1)}, bf16[160,128]{1,0:T(8,128)(2,1)S(1)}, u32[]{:S(2)}, u32[]{:S(2)}) collective-permute-start(bf16[160,128]{1,0:T(8,128)(2,1)S(1)} %reduce-precision_convert_fusion.1), channel_id=1, source_target_pairs={{0,2},{1,3},{2,0},{3,1},{4,6},{5,7},{6,4},{7,5},{8,10},{9,11},{10,... | collective-permute-start | bytes 122888 | tf_op jit(solution)/shard_map/ppermute | solution.py:440
  33.9 5.8 %collective-permute-start.13 = (bf16[160,128]{1,0:T(8,128)(2,1)S(1)}, bf16[160,128]{1,0:T(8,128)(2,1)S(1)}, u32[]{:S(2)}, u32[]{:S(2)}) collective-permute-start(bf16[160,128]{1,0:T(8,128)(2,1)S(1)} %reduce-precision_convert_fusion.1), channel_id=1, source_target_pairs={{0,1},{1,2},{2,3},{3,0},{4,5},{5,6},{6,7},{7,4},{8,9},{9,10},{10,1... | collective-permute-start | bytes 122888 | tf_op jit(solution)/shard_map/ppermute | solution.py:440
  35.7 4.4 %collective-permute-start.14 = (bf16[160,128]{1,0:T(8,128)(2,1)S(1)}, bf16[160,128]{1,0:T(8,128)(2,1)S(1)}, u32[]{:S(2)}, u32[]{:S(2)}) collective-permute-start(bf16[160,128]{1,0:T(8,128)(2,1)S(1)} %reduce-precision_convert_fusion.1), channel_id=1, source_target_pairs={{0,3},{1,0},{2,1},{3,2},{4,7},{5,4},{6,5},{7,6},{8,11},{9,8},{10,9... | collective-permute-start | bytes 122888 | tf_op jit(solution)/shard_map/ppermute | solution.py:440
  40.2 1.3 %collective-permute-start.15 = (bf16[160,128]{1,0:T(8,128)(2,1)S(1)}, bf16[160,128]{1,0:T(8,128)(2,1)S(1)}, u32[]{:S(2)}, u32[]{:S(2)}) collective-permute-start(bf16[160,128]{1,0:T(8,128)(2,1)S(1)} %reduce-precision_convert_fusion.own_ref), channel_id=1, source_target_pairs={{0,4},{4,0},{8,12},{12,8},{16,20},{20,16},{24,28},{28,24},{1,5},{5... | collective-permute-start | bytes 122888 | tf_op jit(solution)/shard_map/ppermute | solution.py:444

commit v7 on v6

--- a/solution.py
+++ b/solution.py
@@ -14,6 +14,10 @@
 TAPS = 7
 SIDE = 3
 LANES = 128
+SUMS_ORDER = (3, 2, 1, 0)
+CHIPS_ORDER = (0, 1, 3, 2)
+SPACE_ORDER = (1, 0, 2, 3)
+TURNS = (0, 2, 1, 3)
 BF = jnp.bfloat16
 F32 = jnp.float32
 
@@ -114,13 +118,15 @@
 
 
 def first_conv_body(
-    x_hbm, taps_hbm, w_hbm, caps_ref, x_ref, part_ref, kw_ref, same_caps_ref, w_ref, taps_ref, sems
+    x_hbm, taps_hbm, w_hbm, pos_hbm, caps_ref,
+    x_ref, part_ref, kw_ref, same_caps_ref, w_ref, labels_ref, taps_ref, pos_ref, sems,
 ):
     cols, channels = x_hbm.shape[2:]
     copies = [
         pltpu.make_async_copy(taps_hbm, taps_ref, sems.at[0]),
         pltpu.make_async_copy(x_hbm, x_ref, sems.at[1]),
         pltpu.make_async_copy(w_hbm, w_ref, sems.at[2]),
+        pltpu.make_async_copy(pos_hbm, pos_ref, sems.at[3]),
     ]
     for copy in copies:
         copy.start()
@@ -134,11 +140,22 @@
             kw_ref[i * TAPS + j] = jnp.where(masks[j], spread, 0.0)
     copies[1].wait()
     conv_rows(x_ref, kw_ref, part_ref, 0)
+    copies[3].wait()
+    images, count, lanes = labels_ref.shape
+    caption = lax.broadcasted_iota(jnp.int32, (count, lanes), 0)
+    for b in range(images):
+        labels_ref[b] = jnp.where(caption == pos_ref[b], 1.0, -1.0).astype(F32)
     copies[2].wait()
 
 
-def later_conv_body(image, x_ref, kw_ref, part_ref):
+def later_conv_body(image, x_ref, kw_ref, part_ref, own_ref):
     conv_rows(x_ref, kw_ref, part_ref, image)
+    images, rows = x_ref.shape[:2]
+    for b in range(images):
+        own = x_ref[b, 0].astype(F32)
+        for r in range(1, rows):
+            own = own + x_ref[b, r].astype(F32)
+        own_ref[b : b + 1, :] = jnp.sum(own, axis=0, keepdims=True)
 
 
 def gelu_tanh(values):
@@ -160,11 +177,12 @@
 
 
 def forward_body(
-    one_ref, two_ref, kw_ref, x_ref, win_ref, wout_ref, caps_ref, first_ref, second_ref,
+    one_ref, two_ref, kw_ref, own_ref, win_ref, wout_ref, caps_ref, first_ref, second_ref,
     sums_ref, normed_ref, inv_ref, hid_ref, before_ref, after_ref, same_caps_ref,
     conv_ref, cast_ref, act_ref,
 ):
-    images, rows, cols, channels = x_ref.shape
+    images = own_ref.shape[0]
+    rows, cols, channels = first_ref.shape
     hidden_units = win_ref.shape[1]
     pixels = rows * cols
     place = lax.axis_index("space")
@@ -232,27 +250,27 @@
         act_ref[:, some] = jnp.concatenate(listed, axis=0)
     mixed = jnp.dot(act_ref[...].astype(BF), wout_ref[...], preferred_element_type=F32)
     for b in range(images):
-        own = x_ref[b, 0].astype(F32)
-        for r in range(1, rows):
-            own = own + x_ref[b, r].astype(F32)
-        sums_ref[b : b + 1, :] = jnp.sum(own, axis=0, keepdims=True) + jnp.sum(
+        sums_ref[b : b + 1, :] = own_ref[b : b + 1, :] + jnp.sum(
             mixed[3 * b : 3 * b + 3], axis=0, keepdims=True
         )
 
 
 def slope_body(
     hid_ref, x_ref, before_ref, after_ref, win_ref, wout_ref,
-    slope_ref, wide_ref, win_t_ref, wout_t_ref,
+    slope_ref, odd_ref, even_gap_ref, odd_gap_ref, win_t_ref, wout_t_ref,
 ):
     win_t_ref[...] = win_ref[...].T
     wout_t_ref[...] = wout_ref[...].T
     images, rows = x_ref.shape[:2]
     for b in range(images):
-        for q in range(SIDE):
-            wide_ref[b, q] = before_ref[b, q].astype(F32)
-            wide_ref[b, rows + SIDE + q] = after_ref[b, q].astype(F32)
-        for r in range(rows):
-            wide_ref[b, SIDE + r] = x_ref[b, r].astype(F32)
+        padded = [before_ref[b, q].astype(F32) for q in range(SIDE)]
+        padded += [x_ref[b, r].astype(F32) for r in range(rows)]
+        padded += [after_ref[b, q].astype(F32) for q in range(SIDE)]
+        for n in range(len(padded) // 2):
+            odd_ref[b, n] = padded[2 * n + 1]
+            even_gap_ref[b, n] = padded[2 * n] - padded[2 * n + 1]
+            if n > 0:
+                odd_gap_ref[b, n - 1] = padded[2 * n] - padded[2 * n - 1]
     for start in range(0, hid_ref.shape[1], 256):
         some = pl.ds(start, 256)
         slope_ref[:, some] = gelu_slope(hid_ref[:, some])
@@ -280,30 +298,47 @@
     cast_ref[...] = unit.astype(BF).astype(F32)
 
 
-def kernel_sums(grad_ref, wide_ref, list_ref, tap_ref, half):
-    images, padded_rows, cols, channels = wide_ref.shape
-    rows = padded_rows - 2 * SIDE
+def kernel_sums(
+    grad_ref, pair_ref, odd_ref, even_gap_ref, odd_gap_ref, list_ref, tap_ref, half
+):
+    images, pairs, cols, channels = odd_ref.shape
+    pairs -= SIDE
     masks = column_masks(cols)
     tiles = channels // LANES // 2
     taps = TAPS * TAPS
+    evens, odds = (TAPS + 1) // 2, TAPS // 2
 
     def tile(t, carry):
         at = tile_at(half * tiles + t)
+
+        def rolled(ref, row, j):
+            value = ref[pl.ds(row * cols, cols), at]
+            return value if j == SIDE else pltpu.roll(value, (j - SIDE) % cols, 0)
+
         for j in range(TAPS):
-            sums = [None] * TAPS
+            shared, even, odd = [None] * evens, [None] * evens, [None] * odds
+
+            def add(sums, rows_ref, grads, b, n):
+                here = rows_ref[b, n, :, at]
+                for l in range(len(sums)):
+                    if 0 <= n - l < pairs:
+                        term = here * grads[n - l]
+                        sums[l] = term if sums[l] is None else sums[l] + term
+
             for b in range(images):
-                grads = []
-                for r in range(rows):
-                    grad = grad_ref[pl.ds((b * rows + r) * cols, cols), at]
-                    grads.append(grad if j == SIDE else pltpu.roll(grad, (j - SIDE) % cols, 0))
-                for q in range(padded_rows):
-                    here = wide_ref[b, q, :, at]
-                    for i in range(TAPS):
-                        if 0 <= q - i < rows:
-                            term = here * grads[q - i]
-                            sums[i] = term if sums[i] is None else sums[i] + term
+                first = b * pairs
+                both = [rolled(pair_ref, first + m, j) for m in range(pairs)]
+                for n in range(pairs + SIDE):
+                    add(shared, odd_ref, both, b, n)
+                low = [rolled(grad_ref, 2 * (first + m), j) for m in range(pairs)]
+                for n in range(pairs + SIDE):
+                    add(even, even_gap_ref, low, b, n)
+                high = [rolled(grad_ref, 2 * (first + m) + 1, j) for m in range(pairs)]
+                for n in range(pairs + SIDE - 1):
+                    add(odd, odd_gap_ref, high, b, n)
             for i in range(TAPS):
-                tap_ref[pl.ds((i * TAPS + j) * cols, cols), :] = jnp.where(masks[j], sums[i], 0.0)
+                total = shared[i // 2] + (odd if i % 2 else even)[i // 2]
+                tap_ref[pl.ds((i * TAPS + j) * cols, cols), :] = jnp.where(masks[j], total, 0.0)
         total = tap_ref[pl.ds(0, taps, stride=cols), :]
         for w in range(1, cols):
             total = total + tap_ref[pl.ds(w, taps, stride=cols), :]
@@ -315,23 +350,22 @@
 
 
 def backward_body(
-    scene_pixels, text_ref, pos_ref, slope_ref, normed_ref, inv_ref, win_t_ref, wout_t_ref,
-    wide_ref, *refs,
+    scene_pixels, patterns, text_ref, labels_ref, slope_ref, normed_ref, inv_ref, win_t_ref, wout_t_ref,
+    odd_ref, even_gap_ref, odd_gap_ref, *refs,
 ):
-    *part_refs, grad_ref, pay_ref, list_ref, tap_ref, hg_ref, row_ref = refs
-    images, padded_rows, cols, channels = wide_ref.shape
-    pixels = (padded_rows - 2 * SIDE) * cols
+    *part_refs, grad_ref, pair_ref, pay_ref, list_ref, tap_ref, hg_ref, row_ref = refs
+    images, padded_pairs, cols, channels = odd_ref.shape
+    pixels = 2 * (padded_pairs - SIDE) * cols
     count = text_ref.shape[0]
-    pooled = pair_sum([ref[...] for ref in part_refs]) / scene_pixels
+    pooled = pair_sum(patterns, [ref[...] for ref in part_refs]) / scene_pixels
     image_unit, pooled_norm = unit_rows(pooled)
     image_cast = image_unit.astype(BF)
     text_cast = text_ref[...]
-    at = lax.broadcasted_iota(jnp.int32, (count, 1), 0)
     sides, pair_grads, losses = [], [], []
     for b in range(images):
         unit = image_cast[b : b + 1].astype(F32)
         logits = LOGIT_SCALE * jnp.sum(unit * text_cast, axis=1, keepdims=True) + LOGIT_BIAS
-        labels = jnp.where(at == pos_ref[b], 1.0, -1.0).astype(F32)
+        labels = labels_ref[b, :, 0:1]
         margin = -labels * logits
         pair_grad = (-labels / (1.0 + jnp.exp(-margin))).astype(BF).astype(F32)
         sides.append(LOGIT_SCALE * jnp.sum(pair_grad * text_cast, axis=0, keepdims=True))
@@ -353,8 +387,15 @@
         - jnp.mean(normed_grad, axis=-1, keepdims=True)
         - normed * jnp.mean(normed_grad * normed, axis=-1, keepdims=True)
     )
+    for m in range(images * (padded_pairs - SIDE)):
+        start = 2 * m * cols
+        pair_ref[pl.ds(m * cols, cols), :] = (
+            grad_ref[pl.ds(start, cols), :] + grad_ref[pl.ds(start + cols, cols), :]
+        )
     half = 1 - own_half()
-    kernel_sums(grad_ref, wide_ref, list_ref, tap_ref, half)
+    kernel_sums(
+        grad_ref, pair_ref, odd_ref, even_gap_ref, odd_gap_ref, list_ref, tap_ref, half
+    )
     listed = list_ref.shape[0]
     pay_ref[0:listed, :] = list_ref[...].astype(BF)
 
@@ -380,9 +421,43 @@
     pay_ref[listed:, :] = row_ref[...].astype(BF)
 
 
-def own_half_body(grad_ref, wide_ref, list_ref, tap_ref):
-    half = own_half()
-    kernel_sums(grad_ref, wide_ref, list_ref, tap_ref, half)
+def own_half_body(grad_ref, pair_ref, odd_ref, even_gap_ref, odd_gap_ref, list_ref, tap_ref):
+    kernel_sums(
+        grad_ref, pair_ref, odd_ref, even_gap_ref, odd_gap_ref, list_ref, tap_ref, own_half()
+    )
+
+
+def place_units(out_ref, start, blocks):
+    for place, rows in blocks:
+        count = rows.shape[0]
+        out_ref[pl.ds(pl.multiple_of(start + place * count, 16), count), :] = rows
+
+
+def cores_body(own_ref, pay_ref, other_ref, both_ref):
+    listed = own_ref.shape[0]
+    both_ref[0:listed, :] = (own_ref[...] + other_ref[0:listed, :].astype(F32)).astype(BF)
+    core = lax.rem(lax.axis_index("dp"), 2)
+    place_units(
+        both_ref, listed, [(core, pay_ref[listed:, :]), (1 - core, other_ref[listed:, :])]
+    )
+
+
+def chips_body(stride, listed, patterns, *refs):
+    *part_refs, total_ref, units_ref = refs
+    members = len(part_refs)
+    total_ref[...] = pair_sum(patterns, [ref[0:listed, :] for ref in part_refs]).astype(BF)
+    place = lax.rem(lax.axis_index("dp") // stride, members)
+    low, high = lax.rem(place, 2), place // 2
+    blocks = []
+    for pattern, ref in zip(patterns, part_refs):
+        there = low + pattern % 2 * (1 - 2 * low) + 2 * (high + pattern // 2 * (1 - 2 * high))
+        blocks.append((there, ref[listed:, :]))
+    place_units(units_ref, 0, blocks)
+
+
+def sum_body(patterns, *refs):
+    *part_refs, total_ref = refs
+    total_ref[...] = pair_sum(patterns, [ref[...] for ref in part_refs]).astype(BF)
 
 
 def text_body(rows_ref, caps_ref, text_ref, loss_ref, wide_ref):
@@ -432,7 +507,7 @@
                 out_ref[i, :, at] = wide_ref[pl.ds((t * TAPS + i) * TAPS, TAPS), :]
 
 
-def shifted(array, axis, stride, step, size=4):
+def shifted(array, axis, stride, step, size):
     pairs = []
     for i in range(lax.axis_size(axis)):
         place = i // stride % size
@@ -458,28 +533,17 @@
     return [1 << k for k in range(size.bit_length() - 1)]
 
 
-def join(mine, theirs, axis, bit):
-    upper = lax.rem(lax.axis_index(axis) // bit, 2) == 1
-    return jnp.where(
-        upper,
-        jnp.concatenate([theirs, mine], axis=0),
-        jnp.concatenate([mine, theirs], axis=0),
-    )
-
-
-def rounded(values):
-    return lax.reduce_precision(values, 8, 7).astype(BF)
-
-
-def group_parts(mine, axis, stride, members):
-    if members == 2:
-        return [mine, flip(mine, axis, stride)]
-    one, two, three = [shifted(mine, axis, stride, k) for k in (1, 2, 3)]
-    return [mine, two, one, three]
-
-
-def flipped_parts(mine, axis, stride, members):
-    return [mine] + [flip(mine, axis, k * stride) for k in range(1, members)]
+def pair_sum(patterns, parts):
+    by_pattern = {p: part.astype(F32) for p, part in zip(patterns, parts)}
+    parts = [by_pattern[p] for p in sorted(patterns)]
+    while len(parts) > 1:
+        parts = [parts[k] + parts[k + 1] for k in range(0, len(parts), 2)]
+    return parts[0]
+
+
+def group_parts(send, mine, members, order):
+    patterns = [p for p in order if p < members]
+    return tuple(patterns), [send(p) if p else mine for p in patterns]
 
 
 def swap_edges(array, second):
@@ -497,17 +561,6 @@
     return lax.ppermute(array, ("dp", "space"), pairs)
 
 
-def pair_sum(parts):
-    parts = [part.astype(F32) for part in parts]
-    while len(parts) > 1:
-        parts = [parts[k] + parts[k + 1] for k in range(0, len(parts), 2)]
-    return parts[0]
-
-
-def group_sum(mine, axis, stride, members):
-    return pair_sum(group_parts(mine, axis, stride, members))
-
-
 def rows_joined(body, mine, theirs, bit, dtype=BF):
     shape = (2 * mine.shape[0], mine.shape[1])
     (out,) = call(functools.partial(body, bit), [(shape, dtype)], [mine, theirs])
@@ -533,7 +586,7 @@
     two = swap_edges(two, True)
     theirs = flip(own_captions, "dp", 1)
     part = (scenes.shape[1:], F32)
-    x, first, spread, gathered, wout = call(
+    x, first, spread, gathered, wout, labels = call(
         first_conv_body,
         [
             (scenes.shape, BF),
@@ -541,15 +594,22 @@
             ((TAPS * TAPS, cols, channels), F32),
             (captions.shape, BF),
             (weight_out.shape, BF),
+            ((images, images * lax.axis_size("dp"), LANES), F32),
         ],
-        [scenes, kernel, weight_out, own_captions],
-        scratch=[pltpu.VMEM(kernel.shape, BF), pltpu.SemaphoreType.DMA((3,))],
-        hbm=(0, 1, 2),
+        [scenes, kernel, weight_out, positives, own_captions],
+        scratch=[
+            pltpu.VMEM(kernel.shape, BF),
+            pltpu.SMEM(positives.shape, jnp.int32),
+            pltpu.SemaphoreType.DMA((4,)),
+        ],
+        hbm=(0, 1, 2, 3),
     )
     gathered = rows_joined(join_body, gathered, theirs, 1)
     dp_bits = bits("dp")
     theirs = flip(gathered, "dp", dp_bits[1] + 1)
-    (second,) = call(functools.partial(later_conv_body, 1), [part], [x, spread])
+    second, own_sums = call(
+        functools.partial(later_conv_body, 1), [part, ((images, channels), F32)], [x, spread]
+    )
     sums, normed, inv, hidden, before, after, gathered = call(
         forward_body,
         [
@@ -561,7 +621,7 @@
             (edge, BF),
             (gathered.shape, BF),
         ],
-        [one, two, spread, x, weight_in, wout, gathered, first, second],
+        [one, two, spread, own_sums, weight_in, wout, gathered, first, second],
         scratch=[
             pltpu.VMEM((pixels, channels), F32),
             pltpu.VMEM((pixels, channels), BF),
@@ -573,14 +633,20 @@
         theirs = flip(gathered, "dp", 2 * bit + 1)
     text_cast = rows_joined(text_cast_body, gathered, theirs, dp_bits[-1], F32)
     space_groups = groups(space_count, 1)
-    for stride, members in space_groups[:-1]:
-        sums = pair_sum(flipped_parts(sums, "space", stride, members))
-    parts = flipped_parts(sums, "space", *space_groups[-1])
-    slope, wide, win_t, wout_t = call(
+    for stride, members in space_groups:
+        patterns, parts = group_parts(
+            lambda p: flip(sums, "space", p * stride), sums, members, SUMS_ORDER
+        )
+        if stride != space_groups[-1][0]:
+            sums = pair_sum(patterns, parts)
+    padded_pairs = rows // 2 + SIDE
+    slope, odd, even_gap, odd_gap, win_t, wout_t = call(
         slope_body,
         [
             ((pixels, hidden_units), F32),
-            ((images, rows + 2 * SIDE, cols, channels), F32),
+            ((images, padded_pairs, cols, channels), F32),
+            ((images, padded_pairs, cols, channels), F32),
+            ((images, padded_pairs - 1, cols, channels), F32),
             (weight_out.shape, BF),
             (weight_in.shape, BF),
         ],
@@ -591,11 +657,16 @@
     listed += -listed % 16
     own_rows = images * (channels // LANES + 1)
     own_rows += -own_rows % 16
-    grad, pay = call(
-        functools.partial(backward_body, scene_pixels),
-        [((pixels, channels), F32), ((listed + own_rows, LANES), BF)],
+    grad, pair, pay = call(
+        functools.partial(backward_body, scene_pixels, patterns),
         [
-            text_cast, positives, slope, normed, inv, win_t, wout_t, wide, *parts,
+            ((pixels, channels), F32),
+            ((pixels // 2, channels), F32),
+            ((listed + own_rows, LANES), BF),
+        ],
+        [
+            text_cast, labels, slope, normed, inv, win_t, wout_t,
+            odd, even_gap, odd_gap, *parts,
         ],
         scratch=[
             pltpu.VMEM((listed, LANES), F32),
@@ -603,31 +674,29 @@
             pltpu.VMEM((pixels, hidden_units), BF),
             pltpu.VMEM((own_rows, LANES), F32),
         ],
-        smem=(1,),
     )
     other = flip(pay, "dp", 1)
     (own,) = call(
         own_half_body,
         [((listed, LANES), F32)],
-        [grad, wide],
+        [grad, pair, odd, even_gap, odd_gap],
         scratch=[pltpu.VMEM((TAPS * TAPS * cols, LANES), F32)],
     )
-    total = own + other[:listed].astype(F32)
-    units = join(pay[listed:], other[listed:], "dp", 1)
-    for stride, members in groups(lax.axis_size("dp"), 2):
-        mine = rounded(total)
-        both = jnp.concatenate([mine, units], axis=0)
-        near = flip(both, "dp", stride + 1)
-        total = mine.astype(F32) + near[:listed].astype(F32)
-        joined = join(units, near[listed:], "dp", stride)
-        if members == 4:
-            far = flip(both, "dp", 2 * stride + 1)
-            cross = flip(both, "dp", 3 * stride)
-            total = total + (far[:listed].astype(F32) + cross[:listed].astype(F32))
-            joined = join(
-                joined, join(far[listed:], cross[listed:], "dp", stride), "dp", 2 * stride
-            )
-        units = joined
+    units_rows = 2 * own_rows
+    (both,) = call(cores_body, [((listed + units_rows, LANES), BF)], [own, pay, other])
+    chip_groups = groups(lax.axis_size("dp"), 2)
+    for stride, members in chip_groups:
+        patterns, parts = group_parts(
+            lambda p: flip(both, "dp", p * stride + (p != 3)), both, members, CHIPS_ORDER
+        )
+        units_rows *= members
+        total, units = call(
+            functools.partial(chips_body, stride, listed, patterns),
+            [((listed, LANES), BF), ((units_rows, LANES), BF)],
+            parts,
+        )
+        if stride != chip_groups[-1][0]:
+            both = jnp.concatenate([total, units], axis=0)
     text_grad, loss = call(
         text_body,
         [((images, channels), F32), ((1, 1), F32)],
@@ -635,14 +704,18 @@
         scratch=[pltpu.VMEM(units.shape, F32)],
         placed_out=jax.ShapeDtypeStruct,
     )
-    for stride, members in groups(space_count, 1):
-        total = group_sum(rounded(total), "space", stride, members)
-    mine = rounded(total)
-    other = flip(mine, "dp", 1)
+    for stride, members in space_groups:
+        patterns, parts = group_parts(
+            lambda p: shifted(total, "space", stride, TURNS[p] if members == 4 else p, members), total, members, SPACE_ORDER
+        )
+        (total,) = call(
+            functools.partial(sum_body, patterns), [((listed, LANES), BF)], parts
+        )
+    other = flip(total, "dp", 1)
     (kernel_grad,) = call(
         merge_body,
         [((TAPS, TAPS, channels), F32)],
-        [mine, other],
+        [total, other],
         scratch=[pltpu.VMEM((listed, LANES), F32)],
         placed_out=jax.ShapeDtypeStruct,
     )

time: 42.4 us -> 40.1 us (0.946)
  waiting for transfers between devices: 7.06 us -> 5.44 us
    ppermute x11, waiting for transfers between devices: 4.69 us -> 3.35 us  [flip(): lax.ppermute(array, axis, [(i, i ^ mask) for i in range(lax.axis_size(axi...]
    ppermute x11, starting transfers between devices: 11.8 us -> 11.1 us  [flip(): lax.ppermute(array, axis, [(i, i ^ mask) for i in range(lax.axis_size(axi...]
    ppermute x3, starting transfers between devices: 4.62 us -> 5.18 us  [shifted(): return lax.ppermute(array, axis, pairs)]
    pallas_call x12 -> x15, Pallas kernels: 14.6 us -> 14.3 us  [call(): pl.pallas_call(body, out_shape=[placed_out(shape, dtype) for shape, dtype...]
  transfers between devices with their start and end apart: 16 -> 16, of which waited for: 8 -> 6; matrix products, arithmetic and copies ran while one was open for 0% -> 0% of each run, Pallas kernels for 23% -> 24%
where the time goes in v7:
time: 40.1 us; the launch traced here: 39.9 us
  starting transfers between devices  19.4 us (48%)
  Pallas kernels  14.3 us (36%)
  waiting for transfers between devices  5.44 us (14%)
  between operations  0.81 us (2%)
    pallas_call x15, Pallas kernels, call(): pl.pallas_call(body, out_shape=[placed_out(shape, dtype) for shape, dtype...  14.3 us
    ppermute x11, starting transfers between devices, flip(): lax.ppermute(array, axis, [(i, i ^ mask) for i in range(lax.axis_size(axi...  11.1 us
    ppermute x3, starting transfers between devices, shifted(): return lax.ppermute(array, axis, pairs)  5.18 us
    ppermute x11, waiting for transfers between devices, flip(): lax.ppermute(array, axis, [(i, i ^ mask) for i in range(lax.axis_size(axi...  3.35 us
    ppermute x2, starting transfers between devices, swap_edges(): return lax.ppermute(array, ('dp', 'space'), pairs)  3.09 us
    ppermute x3, waiting for transfers between devices, shifted(): return lax.ppermute(array, axis, pairs)  2.08 us
  transfers between devices with their start and end apart: 16, of which 6 were waited for; matrix products, arithmetic and copies ran while one was open for 0% of the time, Pallas kernels for 24%

profile of v7, /device:TPU:0, one launch (start us, length us, event | category | flops | bytes accessed | tf_op | source)
XLA Modules:
  0.0 39.9 jit_solution(8983498675376406922)
XLA Ops:
  0.6 0.0 copy-start
  0.6 1.1 %shard_map.85 = (bf16[2,3,8,768]{3,2,1,0:T(8,128)(2,1)S(1)}, bf16[2,3,8,768]{3,2,1,0:T(8,128)(2,1)S(1)}, bf16[2,768]{1,0:T(2,128)(2,1)S(1)}) custom-call(bf16[2,14,8,768]{3,2,1,0:T(8,128)(2,1)} %x_hbm.3, bf16[2,768]{1,0:T(2,128)(2,1)} %caps_hbm.1), custom_call_target="tpu_custom_call" | custom-call | tf_op jit(solution)/shard_map/pallas_call | solution.py:50
  1.8 3.1 %collective-permute-start = (bf16[2,3,8,768]{3,2,1,0:T(8,128)(2,1)S(1)}, bf16[2,3,8,768]{3,2,1,0:T(8,128)(2,1)S(1)}, u32[]{:S(2)}, u32[]{:S(2)}) collective-permute-start(bf16[2,3,8,768]{3,2,1,0:T(8,128)(2,1)S(1)} %get-tuple-element.34), channel_id=1, source_target_pairs={{0,1},{1,0},{2,3},{3,2},{4,5},{5,4},{6,7},{7,6},{8,9},{9,8},{10,11... | collective-permute-start | bytes 221192 | tf_op jit(solution)/shard_map/ppermute | solution.py:561
  4.8 0.0 collective-permute-start.1
  4.8 0.5 %collective-permute-start.2 = (bf16[2,768]{1,0:T(2,128)(2,1)S(1)}, bf16[2,768]{1,0:T(2,128)(2,1)S(1)}, u32[]{:S(2)}, u32[]{:S(2)}) collective-permute-start(bf16[2,768]{1,0:T(2,128)(2,1)S(1)} %get-tuple-element.36.caps_ref), channel_id=1, source_target_pairs={{0,4},{4,0},{8,12},{12,8},{16,20},{20,16},{24,28},{28,24},{1,5},{5... | collective-permute-start | bytes 9224 | tf_op jit(solution)/shard_map/ppermute | solution.py:519
  5.4 2.1 %shard_map.86 = (bf16[2,14,8,768]{3,2,1,0:T(8,128)(2,1)S(1)}, f32[14,8,768]{2,1,0:T(8,128)S(1)}, f32[49,8,768]{2,1,0:T(8,128)S(1)}, bf16[2,768]{1,0:T(2,128)(2,1...) custom-call(bf16[2,14,8,768]{3,2,1,0:T(8,128)(2,1)} %x_hbm.3, bf16[7,7,768]{2,1,0:T(8,128)(2,1)} %taps_hbm.1, ...), custom_call_target="tpu_custom_call" | custom-call | tf_op jit(solution)/shard_map/pallas_call | solution.py:50
  7.5 0.0 collective-permute-done.2.theirs_ref
  7.5 1.2 %collective-permute-start.3 = (bf16[4,768]{1,0:T(4,128)(2,1)S(1)}, bf16[4,768]{1,0:T(4,128)(2,1)S(1)}, u32[]{:S(2)}, u32[]{:S(2)}) collective-permute-start(bf16[4,768]{1,0:T(4,128)(2,1)S(1)} %shard_map.88.caps_ref), channel_id=1, source_target_pairs={{0,12},{4,8},{8,4},{12,0},{16,28},{20,24},{24,20},{28,16},{1,13},{... | collective-permute-start | bytes 18440 | tf_op jit(solution)/shard_map/ppermute | solution.py:519
  8.7 1.1 %shard_map.87 = (f32[14,8,768]{2,1,0:T(8,128)S(1)}, f32[2,768]{1,0:T(2,128)S(1)}) custom-call(bf16[2,14,8,768]{3,2,1,0:T(8,128)(2,1)S(1)} %get-tuple-element.38.x_ref, f32[49,8,768]{2,1,0:T(8,128)S(1)} %get-tuple-element.37.kw_ref), custom_call_target="tpu_custom_call" | custom-call | tf_op jit(solution)/shard_map/pallas_call | solution.py:50
  9.8 0.0 collective-permute-done.one_ref
  9.9 0.0 collective-permute-done.1.two_ref
  9.9 0.0 copy-done
  9.9 1.8 %shard_map.89 = (f32[2,768]{1,0:T(2,128)S(1)}, f32[224,768]{1,0:T(8,128)S(1)}, f32[224,128]{1,0:T(8,128)S(1)}, f32[224,1536]{1,0:T(8,128)S(1)}, bf16[2,3,8,768]{...) custom-call(bf16[2,3,8,768]{3,2,1,0:T(8,128)(2,1)S(1)} %collective-permute-done.one_ref, ...), custom_call_target="tpu_custom_call" | custom-call | tf_op jit(solution)/shard_map/pallas_call | solution.py:50
  11.7 0.0 collective-permute-done.3.theirs_ref
  11.7 1.7 %collective-permute-start.4 = (bf16[8,768]{1,0:T(8,128)(2,1)S(1)}, bf16[8,768]{1,0:T(8,128)(2,1)S(1)}, u32[]{:S(2)}, u32[]{:S(2)}) collective-permute-start(bf16[8,768]{1,0:T(8,128)(2,1)S(1)} %shard_map.90.mine_ref), channel_id=1, source_target_pairs={{0,20},{4,16},{8,28},{12,24},{16,4},{20,0},{24,12},{28,8},{1,21},{... | collective-permute-start | bytes 36872 | tf_op jit(solution)/shard_map/ppermute | solution.py:519
  13.4 2.5 %collective-permute-start.5 = (f32[2,768]{1,0:T(2,128)S(1)}, f32[2,768]{1,0:T(2,128)S(1)}, u32[]{:S(2)}, u32[]{:S(2)}) collective-permute-start(f32[2,768]{1,0:T(2,128)S(1)} %get-tuple-element.57.refs_3_), channel_id=1, source_target_pairs={{0,3},{1,2},{2,1},{3,0},{4,7},{5,6},{6,5},{7,4},{8,11},{9,10},{10,... | collective-permute-start | bytes 18440 | tf_op jit(solution)/shard_map/ppermute | solution.py:519
  15.9 1.6 %collective-permute-start.6 = (f32[2,768]{1,0:T(2,128)S(1)}, f32[2,768]{1,0:T(2,128)S(1)}, u32[]{:S(2)}, u32[]{:S(2)}) collective-permute-start(f32[2,768]{1,0:T(2,128)S(1)} %get-tuple-element.57.refs_3_), channel_id=1, source_target_pairs={{0,2},{1,3},{2,0},{3,1},{4,6},{5,7},{6,4},{7,5},{8,10},{9,11},{10,... | collective-permute-start | bytes 18440 | tf_op jit(solution)/shard_map/ppermute | solution.py:519
  17.5 0.3 collective-permute-start.7
  17.8 2.5 %shard_map.92 = (f32[224,1536]{1,0:T(8,128)S(1)}, f32[2,10,8,768]{3,2,1,0:T(8,128)S(1)}, f32[2,10,8,768]{3,2,1,0:T(8,128)S(1)}, f32[2,9,8,768]{3,2,1,0:T(8,128)S...) custom-call(f32[224,1536]{1,0:T(8,128)S(1)} %get-tuple-element.46.hid_ref, ...), custom_call_target="tpu_custom_call" | custom-call | tf_op jit(solution)/shard_map/pallas_call | solution.py:50
  20.3 0.0 collective-permute-done.4.theirs_ref
  20.3 0.1 shard_map.91.text_ref
  20.4 0.0 collective-permute-done.5.refs_0_
  20.5 0.0 collective-permute-done.6.refs_1_
  20.5 0.7 %collective-permute-done.7.refs_2_ = f32[2,768]{1,0:T(2,128)S(1)} collective-permute-done((f32[2,768]{1,0:T(2,128)S(1)}, f32[2,768]{1,0:T(2,128)S(1)}, u32[]{:S(2)}, u32[]{:S(2)}) %collective-permute-start.7) | collective-permute-done | bytes 6176 | tf_op jit(solution)/shard_map/ppermute | solution.py:519
  21.2 2.7 %shard_map.93 = (f32[224,768]{1,0:T(8,128)S(1)}, f32[112,768]{1,0:T(8,128)S(1)}, bf16[176,128]{1,0:T(8,128)(2,1)S(1)}) custom-call(f32[16,768]{1,0:T(8,128)S(1)} %shard_map.91.text_ref, f32[2,16,128]{2,1,0:T(8,128)S(1)} %get-tuple-element.45.labels_ref, f32[224,1536]{1,0:T(8,128)S(1)} %get-tuple-element.49.slope_ref, ...), custom_call_target="tpu_custom_call" | custom-call | tf_op jit(solution)/shard_map/pallas_call | solution.py:50
  23.9 0.0 collective-permute-start.8
  23.9 1.1 %shard_map.94.own_ref = f32[160,128]{1,0:T(8,128)S(1)} custom-call(f32[224,768]{1,0:T(8,128)S(1)} %get-tuple-element.58.grad_ref, f32[112,768]{1,0:T(8,128)S(1)} %get-tuple-element.59.pair_ref, f32[2,10,8,768]{3,2,1,0:T(8,128)S(1)} %get-tuple-element.54.odd_ref, f32[2,10,8,768]{3,2,1,0:T(8,128)S(1)} %get-tuple-element.55.even_gap_ref, ...), custom_call_target="tpu_custom_call" | custom-call | tf_op jit(solution)/shard_map/pallas_call | solution.py:50
  25.0 0.1 collective-permute-done.8.other_ref
  25.2 0.6 %collective-permute-start.10 = (bf16[192,128]{1,0:T(8,128)(2,1)S(1)}, bf16[192,128]{1,0:T(8,128)(2,1)S(1)}, u32[]{:S(2)}, u32[]{:S(2)}) collective-permute-start(bf16[192,128]{1,0:T(8,128)(2,1)S(1)} %shard_map.95.refs_0_), channel_id=1, source_target_pairs={{0,24},{4,28},{8,16},{12,20},{16,8},{20,12},{24,0},{28,4},{1,25},{... | collective-permute-start | bytes 147464 | tf_op jit(solution)/shard_map/ppermute | solution.py:519
  25.7 1.2 %collective-permute-start.11 = (bf16[192,128]{1,0:T(8,128)(2,1)S(1)}, bf16[192,128]{1,0:T(8,128)(2,1)S(1)}, u32[]{:S(2)}, u32[]{:S(2)}) collective-permute-start(bf16[192,128]{1,0:T(8,128)(2,1)S(1)} %shard_map.95.refs_0_), channel_id=1, source_target_pairs={{0,20},{4,16},{8,28},{12,24},{16,4},{20,0},{24,12},{28,8},{1,21},{... | collective-permute-start | bytes 147464 | tf_op jit(solution)/shard_map/ppermute | solution.py:519
  26.9 1.5 %collective-permute-start.9 = (bf16[192,128]{1,0:T(8,128)(2,1)S(1)}, bf16[192,128]{1,0:T(8,128)(2,1)S(1)}, u32[]{:S(2)}, u32[]{:S(2)}) collective-permute-start(bf16[192,128]{1,0:T(8,128)(2,1)S(1)} %shard_map.95.refs_0_), channel_id=1, source_target_pairs={{0,12},{4,8},{8,4},{12,0},{16,28},{20,24},{24,20},{28,16},{1,13},{... | collective-permute-start | bytes 147464 | tf_op jit(solution)/shard_map/ppermute | solution.py:519
  28.5 2.1 %collective-permute-done.10.refs_2_ = bf16[192,128]{1,0:T(8,128)(2,1)S(1)} collective-permute-done((bf16[192,128]{1,0:T(8,128)(2,1)S(1)}, bf16[192,128]{1,0:T(8,128)(2,1)S(1)}, u32[]{:S(2)}, u32[]{:S(2)}) %collective-permute-start.10) | collective-permute-done | bytes 49184 | tf_op jit(solution)/shard_map/ppermute | solution.py:519
  30.6 0.0 collective-permute-done.11.refs_3_
  30.6 0.0 collective-permute-done.9.refs_1_
  30.7 1.4 %collective-permute-start.12 = (bf16[160,128]{1,0:T(8,128)(2,1)S(1)}, bf16[160,128]{1,0:T(8,128)(2,1)S(1)}, u32[]{:S(2)}, u32[]{:S(2)}) collective-permute-start(bf16[160,128]{1,0:T(8,128)(2,1)S(1)} %get-tuple-element.64.refs_1_), channel_id=1, source_target_pairs={{0,2},{1,3},{2,0},{3,1},{4,6},{5,7},{6,4},{7,5},{8,10},{9,11},{10,... | collective-permute-start | bytes 122888 | tf_op jit(solution)/shard_map/ppermute | solution.py:515
  32.0 1.1 %collective-permute-start.13 = (bf16[160,128]{1,0:T(8,128)(2,1)S(1)}, bf16[160,128]{1,0:T(8,128)(2,1)S(1)}, u32[]{:S(2)}, u32[]{:S(2)}) collective-permute-start(bf16[160,128]{1,0:T(8,128)(2,1)S(1)} %get-tuple-element.64.refs_1_), channel_id=1, source_target_pairs={{0,1},{1,2},{2,3},{3,0},{4,5},{5,6},{6,7},{7,4},{8,9},{9,10},{10,1... | collective-permute-start | bytes 122888 | tf_op jit(solution)/shard_map/ppermute | solution.py:515
  33.1 2.8 %collective-permute-start.14 = (bf16[160,128]{1,0:T(8,128)(2,1)S(1)}, bf16[160,128]{1,0:T(8,128)(2,1)S(1)}, u32[]{:S(2)}, u32[]{:S(2)}) collective-permute-start(bf16[160,128]{1,0:T(8,128)(2,1)S(1)} %get-tuple-element.64.refs_1_), channel_id=1, source_target_pairs={{0,3},{1,0},{2,1},{3,2},{4,7},{5,4},{6,5},{7,6},{8,11},{9,8},{10,9... | collective-permute-start | bytes 122888 | tf_op jit(solution)/shard_map/ppermute | solution.py:515
  35.8 1.1 %collective-permute-done.12.refs_0_ = bf16[160,128]{1,0:T(8,128)(2,1)S(1)} collective-permute-done((bf16[160,128]{1,0:T(8,128)(2,1)S(1)}, bf16[160,128]{1,0:T(8,128)(2,1)S(1)}, u32[]{:S(2)}, u32[]{:S(2)}) %collective-permute-start.12) | collective-permute-done | bytes 40992 | tf_op jit(solution)/shard_map/ppermute | solution.py:515
  36.9 1.0 %collective-permute-done.13.refs_2_ = bf16[160,128]{1,0:T(8,128)(2,1)S(1)} collective-permute-done((bf16[160,128]{1,0:T(8,128)(2,1)S(1)}, bf16[160,128]{1,0:T(8,128)(2,1)S(1)}, u32[]{:S(2)}, u32[]{:S(2)}) %collective-permute-start.13) | collective-permute-done | bytes 40992 | tf_op jit(solution)/shard_map/ppermute | solution.py:515
  37.9 0.0 collective-permute-done.14.refs_3_
  37.9 0.1 collective-permute-start.15
  38.0 0.8 %shard_map.97 = (f32[2,768]{1,0:T(2,128)}, f32[1,1]{1,0:T(1,128)}) custom-call(bf16[128,128]{1,0:T(8,128)(2,1)S(1)} %get-tuple-element.61.rows_ref, bf16[2,768]{1,0:T(2,128)(2,1)S(1)} %get-tuple-element.36.caps_ref), custom_call_target="tpu_custom_call" | custom-call | tf_op jit(solution)/shard_map/pallas_call | solution.py:50
  38.8 0.4 collective-permute-done.15.other_ref
  39.2 0.7 %shard_map.99 = f32[7,7,768]{2,1,0:T(8,128)} custom-call(bf16[160,128]{1,0:T(8,128)(2,1)S(1)} %shard_map.98.own_ref, bf16[160,128]{1,0:T(8,128)(2,1)S(1)} %collective-permute-done.15.other_ref), custom_call_target="tpu_custom_call" | custom-call | tf_op jit(solution)/shard_map/pallas_call | solution.py:50
  (5 shorter events, 0.1 us)
Async XLA Ops:
  0.6 9.2 %copy-start = (bf16[768,1536]{1,0:T(8,128)(2,1)S(1)}, bf16[768,1536]{1,0:T(8,128)(2,1)}, u32[]{:S(2)}) copy-start(bf16[768,1536]{1,0:T(8,128)(2,1)} %win_ref.3) | copy-start | bytes 7077892
  1.8 8.1 %collective-permute-start = (bf16[2,3,8,768]{3,2,1,0:T(8,128)(2,1)S(1)}, bf16[2,3,8,768]{3,2,1,0:T(8,128)(2,1)S(1)}, u32[]{:S(2)}, u32[]{:S(2)}) collective-permute-start(bf16[2,3,8,768]{3,2,1,0:T(8,128)(2,1)S(1)} %get-tuple-element.34), channel_id=1, source_target_pairs={{0,1},{1,0},{2,3},{3,2},{4,5},{5,4},{6,7},{7,6},{8,9},{9,8},{10,11... | collective-permute-start | bytes 221192 | tf_op jit(solution)/shard_map/ppermute | solution.py:561
  4.8 5.0 %collective-permute-start.1 = (bf16[2,3,8,768]{3,2,1,0:T(8,128)(2,1)S(1)}, bf16[2,3,8,768]{3,2,1,0:T(8,128)(2,1)S(1)}, u32[]{:S(2)}, u32[]{:S(2)}) collective-permute-start(bf16[2,3,8,768]{3,2,1,0:T(8,128)(2,1)S(1)} %get-tuple-element.35), channel_id=1, source_target_pairs={{0,4},{1,2},{2,1},{3,7},{4,0},{5,6},{6,5},{7,3},{8,12},{9,10},{10,... | collective-permute-start | bytes 221192 | tf_op jit(solution)/shard_map/ppermute | solution.py:561
  4.8 2.7 %collective-permute-start.2 = (bf16[2,768]{1,0:T(2,128)(2,1)S(1)}, bf16[2,768]{1,0:T(2,128)(2,1)S(1)}, u32[]{:S(2)}, u32[]{:S(2)}) collective-permute-start(bf16[2,768]{1,0:T(2,128)(2,1)S(1)} %get-tuple-element.36.caps_ref), channel_id=1, source_target_pairs={{0,4},{4,0},{8,12},{12,8},{16,20},{20,16},{24,28},{28,24},{1,5},{5... | collective-permute-start | bytes 9224 | tf_op jit(solution)/shard_map/ppermute | solution.py:519
  7.5 4.1 %collective-permute-start.3 = (bf16[4,768]{1,0:T(4,128)(2,1)S(1)}, bf16[4,768]{1,0:T(4,128)(2,1)S(1)}, u32[]{:S(2)}, u32[]{:S(2)}) collective-permute-start(bf16[4,768]{1,0:T(4,128)(2,1)S(1)} %shard_map.88.caps_ref), channel_id=1, source_target_pairs={{0,12},{4,8},{8,4},{12,0},{16,28},{20,24},{24,20},{28,16},{1,13},{... | collective-permute-start | bytes 18440 | tf_op jit(solution)/shard_map/ppermute | solution.py:519
  11.7 8.6 %collective-permute-start.4 = (bf16[8,768]{1,0:T(8,128)(2,1)S(1)}, bf16[8,768]{1,0:T(8,128)(2,1)S(1)}, u32[]{:S(2)}, u32[]{:S(2)}) collective-permute-start(bf16[8,768]{1,0:T(8,128)(2,1)S(1)} %shard_map.90.mine_ref), channel_id=1, source_target_pairs={{0,20},{4,16},{8,28},{12,24},{16,4},{20,0},{24,12},{28,8},{1,21},{... | collective-permute-start | bytes 36872 | tf_op jit(solution)/shard_map/ppermute | solution.py:519
  13.4 7.0 %collective-permute-start.5 = (f32[2,768]{1,0:T(2,128)S(1)}, f32[2,768]{1,0:T(2,128)S(1)}, u32[]{:S(2)}, u32[]{:S(2)}) collective-permute-start(f32[2,768]{1,0:T(2,128)S(1)} %get-tuple-element.57.refs_3_), channel_id=1, source_target_pairs={{0,3},{1,2},{2,1},{3,0},{4,7},{5,6},{6,5},{7,4},{8,11},{9,10},{10,... | collective-permute-start | bytes 18440 | tf_op jit(solution)/shard_map/ppermute | solution.py:519
  15.9 4.6 %collective-permute-start.6 = (f32[2,768]{1,0:T(2,128)S(1)}, f32[2,768]{1,0:T(2,128)S(1)}, u32[]{:S(2)}, u32[]{:S(2)}) collective-permute-start(f32[2,768]{1,0:T(2,128)S(1)} %get-tuple-element.57.refs_3_), channel_id=1, source_target_pairs={{0,2},{1,3},{2,0},{3,1},{4,6},{5,7},{6,4},{7,5},{8,10},{9,11},{10,... | collective-permute-start | bytes 18440 | tf_op jit(solution)/shard_map/ppermute | solution.py:519
  17.5 3.6 %collective-permute-start.7 = (f32[2,768]{1,0:T(2,128)S(1)}, f32[2,768]{1,0:T(2,128)S(1)}, u32[]{:S(2)}, u32[]{:S(2)}) collective-permute-start(f32[2,768]{1,0:T(2,128)S(1)} %get-tuple-element.57.refs_3_), channel_id=1, source_target_pairs={{0,1},{1,0},{2,3},{3,2},{4,5},{5,4},{6,7},{7,6},{8,9},{9,8},{10,11... | collective-permute-start | bytes 18440 | tf_op jit(solution)/shard_map/ppermute | solution.py:519
  23.9 1.2 %collective-permute-start.8 = (bf16[176,128]{1,0:T(8,128)(2,1)S(1)}, bf16[176,128]{1,0:T(8,128)(2,1)S(1)}, u32[]{:S(2)}, u32[]{:S(2)}) collective-permute-start(bf16[176,128]{1,0:T(8,128)(2,1)S(1)} %get-tuple-element.60.pay_ref), channel_id=1, source_target_pairs={{0,4},{4,0},{8,12},{12,8},{16,20},{20,16},{24,28},{28,24},{1,5},{5... | collective-permute-start | bytes 135176 | tf_op jit(solution)/shard_map/ppermute | solution.py:519
  25.2 5.5 %collective-permute-start.10 = (bf16[192,128]{1,0:T(8,128)(2,1)S(1)}, bf16[192,128]{1,0:T(8,128)(2,1)S(1)}, u32[]{:S(2)}, u32[]{:S(2)}) collective-permute-start(bf16[192,128]{1,0:T(8,128)(2,1)S(1)} %shard_map.95.refs_0_), channel_id=1, source_target_pairs={{0,24},{4,28},{8,16},{12,20},{16,8},{20,12},{24,0},{28,4},{1,25},{... | collective-permute-start | bytes 147464 | tf_op jit(solution)/shard_map/ppermute | solution.py:519
  25.7 4.9 %collective-permute-start.11 = (bf16[192,128]{1,0:T(8,128)(2,1)S(1)}, bf16[192,128]{1,0:T(8,128)(2,1)S(1)}, u32[]{:S(2)}, u32[]{:S(2)}) collective-permute-start(bf16[192,128]{1,0:T(8,128)(2,1)S(1)} %shard_map.95.refs_0_), channel_id=1, source_target_pairs={{0,20},{4,16},{8,28},{12,24},{16,4},{20,0},{24,12},{28,8},{1,21},{... | collective-permute-start | bytes 147464 | tf_op jit(solution)/shard_map/ppermute | solution.py:519
  26.9 3.7 %collective-permute-start.9 = (bf16[192,128]{1,0:T(8,128)(2,1)S(1)}, bf16[192,128]{1,0:T(8,128)(2,1)S(1)}, u32[]{:S(2)}, u32[]{:S(2)}) collective-permute-start(bf16[192,128]{1,0:T(8,128)(2,1)S(1)} %shard_map.95.refs_0_), channel_id=1, source_target_pairs={{0,12},{4,8},{8,4},{12,0},{16,28},{20,24},{24,20},{28,16},{1,13},{... | collective-permute-start | bytes 147464 | tf_op jit(solution)/shard_map/ppermute | solution.py:519
  30.7 6.3 %collective-permute-start.12 = (bf16[160,128]{1,0:T(8,128)(2,1)S(1)}, bf16[160,128]{1,0:T(8,128)(2,1)S(1)}, u32[]{:S(2)}, u32[]{:S(2)}) collective-permute-start(bf16[160,128]{1,0:T(8,128)(2,1)S(1)} %get-tuple-element.64.refs_1_), channel_id=1, source_target_pairs={{0,2},{1,3},{2,0},{3,1},{4,6},{5,7},{6,4},{7,5},{8,10},{9,11},{10,... | collective-permute-start | bytes 122888 | tf_op jit(solution)/shard_map/ppermute | solution.py:515
  32.0 5.9 %collective-permute-start.13 = (bf16[160,128]{1,0:T(8,128)(2,1)S(1)}, bf16[160,128]{1,0:T(8,128)(2,1)S(1)}, u32[]{:S(2)}, u32[]{:S(2)}) collective-permute-start(bf16[160,128]{1,0:T(8,128)(2,1)S(1)} %get-tuple-element.64.refs_1_), channel_id=1, source_target_pairs={{0,1},{1,2},{2,3},{3,0},{4,5},{5,6},{6,7},{7,4},{8,9},{9,10},{10,1... | collective-permute-start | bytes 122888 | tf_op jit(solution)/shard_map/ppermute | solution.py:515
  33.1 4.8 %collective-permute-start.14 = (bf16[160,128]{1,0:T(8,128)(2,1)S(1)}, bf16[160,128]{1,0:T(8,128)(2,1)S(1)}, u32[]{:S(2)}, u32[]{:S(2)}) collective-permute-start(bf16[160,128]{1,0:T(8,128)(2,1)S(1)} %get-tuple-element.64.refs_1_), channel_id=1, source_target_pairs={{0,3},{1,0},{2,1},{3,2},{4,7},{5,4},{6,5},{7,6},{8,11},{9,8},{10,9... | collective-permute-start | bytes 122888 | tf_op jit(solution)/shard_map/ppermute | solution.py:515
  37.9 1.3 %collective-permute-start.15 = (bf16[160,128]{1,0:T(8,128)(2,1)S(1)}, bf16[160,128]{1,0:T(8,128)(2,1)S(1)}, u32[]{:S(2)}, u32[]{:S(2)}) collective-permute-start(bf16[160,128]{1,0:T(8,128)(2,1)S(1)} %shard_map.98.own_ref), channel_id=1, source_target_pairs={{0,4},{4,0},{8,12},{12,8},{16,20},{20,16},{24,28},{28,24},{1,5},{5... | collective-permute-start | bytes 122888 | tf_op jit(solution)/shard_map/ppermute | solution.py:519

commit v8 on v7

--- a/solution.py
+++ b/solution.py
@@ -77,7 +77,9 @@
     return lax.rem(odd, 2)
 
 
-def load_body(x_hbm, caps_hbm, one_ref, two_ref, caps_ref, sems):
+def load_body(
+    x_hbm, k_hbm, caps_hbm, one_ref, two_ref, caps_ref, taps_ref, x_ref, sems
+):
     rows = x_hbm.shape[1]
     odd = lax.rem(lax.axis_index("space"), 2)
     low, high = odd * (rows - SIDE), (1 - odd) * (rows - SIDE)
@@ -85,6 +87,8 @@
         pltpu.make_async_copy(x_hbm.at[:, pl.ds(high, SIDE)], one_ref, sems.at[0]),
         pltpu.make_async_copy(x_hbm.at[:, pl.ds(low, SIDE)], two_ref, sems.at[1]),
         pltpu.make_async_copy(caps_hbm, caps_ref, sems.at[2]),
+        pltpu.make_async_copy(k_hbm, taps_ref, sems.at[3]),
+        pltpu.make_async_copy(x_hbm, x_ref, sems.at[4]),
     ]
     for copy in copies:
         copy.start()
@@ -118,34 +122,30 @@
 
 
 def first_conv_body(
-    x_hbm, taps_hbm, w_hbm, pos_hbm, caps_ref,
-    x_ref, part_ref, kw_ref, same_caps_ref, w_ref, labels_ref, taps_ref, pos_ref, sems,
+    x_ref, taps_ref, w_hbm, pos_hbm, caps_ref,
+    part_ref, kw_ref, same_caps_ref, w_ref, labels_ref, pos_ref, sems,
 ):
-    cols, channels = x_hbm.shape[2:]
+    cols, channels = x_ref.shape[2:]
     copies = [
-        pltpu.make_async_copy(taps_hbm, taps_ref, sems.at[0]),
-        pltpu.make_async_copy(x_hbm, x_ref, sems.at[1]),
-        pltpu.make_async_copy(w_hbm, w_ref, sems.at[2]),
-        pltpu.make_async_copy(pos_hbm, pos_ref, sems.at[3]),
+        pltpu.make_async_copy(w_hbm, w_ref, sems.at[0]),
+        pltpu.make_async_copy(pos_hbm, pos_ref, sems.at[1]),
     ]
     for copy in copies:
         copy.start()
     same_caps_ref[...] = caps_ref[...]
     masks = column_masks(cols, channels)
-    copies[0].wait()
     for i in range(TAPS):
         taps = taps_ref[i].astype(F32)
         for j in range(TAPS):
             spread = jnp.broadcast_to(taps[j : j + 1], (cols, channels))
             kw_ref[i * TAPS + j] = jnp.where(masks[j], spread, 0.0)
+    conv_rows(x_ref, kw_ref, part_ref, 0)
     copies[1].wait()
-    conv_rows(x_ref, kw_ref, part_ref, 0)
-    copies[3].wait()
     images, count, lanes = labels_ref.shape
     caption = lax.broadcasted_iota(jnp.int32, (count, lanes), 0)
     for b in range(images):
         labels_ref[b] = jnp.where(caption == pos_ref[b], 1.0, -1.0).astype(F32)
-    copies[2].wait()
+    copies[0].wait()
 
 
 def later_conv_body(image, x_ref, kw_ref, part_ref, own_ref):
@@ -177,7 +177,7 @@
 
 
 def forward_body(
-    one_ref, two_ref, kw_ref, own_ref, win_ref, wout_ref, caps_ref, first_ref, second_ref,
+    two_ref, one_ref, kw_ref, own_ref, win_ref, wout_ref, caps_ref, first_ref, second_ref,
     sums_ref, normed_ref, inv_ref, hid_ref, before_ref, after_ref, same_caps_ref,
     conv_ref, cast_ref, act_ref,
 ):
@@ -575,34 +575,32 @@
     scene_pixels = rows * space_count * cols
     edge = (images, SIDE, cols, channels)
 
-    one, two, own_captions = call(
+    one, two, own_captions, taps, x = call(
         load_body,
-        [(edge, BF), (edge, BF), (captions.shape, BF)],
-        [scenes, captions],
-        scratch=[pltpu.SemaphoreType.DMA((3,))],
-        hbm=(0, 1),
-    )
+        [(edge, BF), (edge, BF), (captions.shape, BF), (kernel.shape, BF), (scenes.shape, BF)],
+        [scenes, kernel, captions],
+        scratch=[pltpu.SemaphoreType.DMA((5,))],
+        hbm=(0, 1, 2),
+    )
+    two = swap_edges(two, True)
     one = swap_edges(one, False)
-    two = swap_edges(two, True)
     theirs = flip(own_captions, "dp", 1)
     part = (scenes.shape[1:], F32)
-    x, first, spread, gathered, wout, labels = call(
+    first, spread, gathered, wout, labels = call(
         first_conv_body,
         [
-            (scenes.shape, BF),
             part,
             ((TAPS * TAPS, cols, channels), F32),
             (captions.shape, BF),
             (weight_out.shape, BF),
             ((images, images * lax.axis_size("dp"), LANES), F32),
         ],
-        [scenes, kernel, weight_out, positives, own_captions],
+        [x, taps, weight_out, positives, own_captions],
         scratch=[
-            pltpu.VMEM(kernel.shape, BF),
             pltpu.SMEM(positives.shape, jnp.int32),
-            pltpu.SemaphoreType.DMA((4,)),
+            pltpu.SemaphoreType.DMA((2,)),
         ],
-        hbm=(0, 1, 2, 3),
+        hbm=(2, 3),
     )
     gathered = rows_joined(join_body, gathered, theirs, 1)
     dp_bits = bits("dp")
@@ -621,7 +619,7 @@
             (edge, BF),
             (gathered.shape, BF),
         ],
-        [one, two, spread, own_sums, weight_in, wout, gathered, first, second],
+        [two, one, spread, own_sums, weight_in, wout, gathered, first, second],
         scratch=[
             pltpu.VMEM((pixels, channels), F32),
             pltpu.VMEM((pixels, channels), BF),

time: 40.1 us -> 39.9 us (level)
  starting transfers between devices: 19.4 us -> 20.1 us
  waiting for transfers between devices: 5.44 us -> 4.74 us
    ppermute x2, starting transfers between devices: 3.09 us -> 4.67 us  [swap_edges(): return lax.ppermute(array, ('dp', 'space'), pairs)]
    ppermute x11, waiting for transfers between devices: 3.35 us -> 2.66 us  [flip(): lax.ppermute(array, axis, [(i, i ^ mask) for i in range(lax.axis_size(axi...]
    ppermute x11, starting transfers between devices: 11.1 us -> 10.6 us  [flip(): lax.ppermute(array, axis, [(i, i ^ mask) for i in range(lax.axis_size(axi...]
  transfers between devices with their start and end apart: 16 -> 16, of which waited for: 6 -> 5; matrix products, arithmetic and copies ran while one was open for 0% -> 0% of each run, Pallas kernels for 24% -> 23%
where the time goes in v8:
time: 39.9 us; the launch traced here: 39.7 us
  starting transfers between devices  20.1 us (50%)
  Pallas kernels  14 us (35%)
  waiting for transfers between devices  4.74 us (12%)
  between operations  0.82 us (2%)
    pallas_call x15, Pallas kernels, call(): pl.pallas_call(body, out_shape=[placed_out(shape, dtype) for shape, dtype...  14 us
    ppermute x11, starting transfers between devices, flip(): lax.ppermute(array, axis, [(i, i ^ mask) for i in range(lax.axis_size(axi...  10.6 us
    ppermute x3, starting transfers between devices, shifted(): return lax.ppermute(array, axis, pairs)  4.84 us
    ppermute x2, starting transfers between devices, swap_edges(): return lax.ppermute(array, ('dp', 'space'), pairs)  4.67 us
    ppermute x11, waiting for transfers between devices, flip(): lax.ppermute(array, axis, [(i, i ^ mask) for i in range(lax.axis_size(axi...  2.66 us
    ppermute x3, waiting for transfers between devices, shifted(): return lax.ppermute(array, axis, pairs)  2.08 us
  transfers between devices with their start and end apart: 16, of which 5 were waited for; matrix products, arithmetic and copies ran while one was open for 0% of the time, Pallas kernels for 23%

profile of v8, /device:TPU:0, one launch (start us, length us, event | category | flops | bytes accessed | tf_op | source)
XLA Modules:
  0.0 39.7 jit_solution(11985571054387460972)
XLA Ops:
  0.6 0.0 copy-start
  0.6 1.3 %shard_map.85 = (bf16[2,3,8,768]{3,2,1,0:T(8,128)(2,1)S(1)}, bf16[2,3,8,768]{3,2,1,0:T(8,128)(2,1)S(1)}, bf16[2,768]{1,0:T(2,128)(2,1)S(1)}, bf16[7,7,768]{2,1,0:T(8,128)(2,1)S(1)}, bf16[2,14,8,768]{3,2,1,0:T(8,128)(2,1)S(1)}) custom-call(bf16[2,14,8,768]{3,2,1,0:T(8,128)(2,1)} %x_hbm.1, bf16[7,7,768]{2,1,0:T(8,128)(2,1)} %k_hbm.1, bf16[2,768]{1,0:T(2,128)(2,1)} %caps_hbm.1), custom_call_target="tpu_custom_call" | custom-call | tf_op jit(solution)/shard_map/pallas_call | solution.py:50
  2.0 0.5 %collective-permute-start = (bf16[2,3,8,768]{3,2,1,0:T(8,128)(2,1)S(1)}, bf16[2,3,8,768]{3,2,1,0:T(8,128)(2,1)S(1)}, u32[]{:S(2)}, u32[]{:S(2)}) collective-permute-start(bf16[2,3,8,768]{3,2,1,0:T(8,128)(2,1)S(1)} %get-tuple-element.35), channel_id=1, source_target_pairs={{0,4},{1,2},{2,1},{3,7},{4,0},{5,6},{6,5},{7,3},{8,12},{9,10},{10,... | collective-permute-start | bytes 221192 | tf_op jit(solution)/shard_map/ppermute | solution.py:561
  2.5 4.1 %collective-permute-start.1 = (bf16[2,3,8,768]{3,2,1,0:T(8,128)(2,1)S(1)}, bf16[2,3,8,768]{3,2,1,0:T(8,128)(2,1)S(1)}, u32[]{:S(2)}, u32[]{:S(2)}) collective-permute-start(bf16[2,3,8,768]{3,2,1,0:T(8,128)(2,1)S(1)} %get-tuple-element.36), channel_id=1, source_target_pairs={{0,1},{1,0},{2,3},{3,2},{4,5},{5,4},{6,7},{7,6},{8,9},{9,8},{10,11... | collective-permute-start | bytes 221192 | tf_op jit(solution)/shard_map/ppermute | solution.py:561
  6.6 0.0 collective-permute-start.2
  6.6 1.7 %shard_map.86 = (f32[14,8,768]{2,1,0:T(8,128)S(1)}, f32[49,8,768]{2,1,0:T(8,128)S(1)}, bf16[2,768]{1,0:T(2,128)(2,1)S(1)}, bf16[1536,768]{1,0:T(8,128)(2,1)S(1)}, f32[2,16,128]{2,1,0:T(8,128)S(1)}) custom-call(bf16[2,14,8,768]{3,2,1,0:T(8,128)(2,1)S(1)} %get-tuple-element.37.x_ref, bf16[7,7,768]{2,1,0:T(8,128)(2,1)S(1)} %get-tuple-element.38.taps_ref, ...), custom_call_target="tpu_custom_call" | custom-call | tf_op jit(solution)/shard_map/pallas_call | solution.py:50
  8.3 0.0 collective-permute-done.2.theirs_ref
  8.4 1.7 %collective-permute-start.3 = (bf16[4,768]{1,0:T(4,128)(2,1)S(1)}, bf16[4,768]{1,0:T(4,128)(2,1)S(1)}, u32[]{:S(2)}, u32[]{:S(2)}) collective-permute-start(bf16[4,768]{1,0:T(4,128)(2,1)S(1)} %shard_map.88.caps_ref), channel_id=1, source_target_pairs={{0,12},{4,8},{8,4},{12,0},{16,28},{20,24},{24,20},{28,16},{1,13},{... | collective-permute-start | bytes 18440 | tf_op jit(solution)/shard_map/ppermute | solution.py:519
  10.0 1.1 %shard_map.87 = (f32[14,8,768]{2,1,0:T(8,128)S(1)}, f32[2,768]{1,0:T(2,128)S(1)}) custom-call(bf16[2,14,8,768]{3,2,1,0:T(8,128)(2,1)S(1)} %get-tuple-element.37.x_ref, f32[49,8,768]{2,1,0:T(8,128)S(1)} %get-tuple-element.40.kw_ref), custom_call_target="tpu_custom_call" | custom-call | tf_op jit(solution)/shard_map/pallas_call | solution.py:50
  11.2 0.0 collective-permute-done.two_ref
  11.2 0.0 collective-permute-done.1.one_ref
  11.2 0.0 copy-done
  11.2 1.8 %shard_map.89 = (f32[2,768]{1,0:T(2,128)S(1)}, f32[224,768]{1,0:T(8,128)S(1)}, f32[224,128]{1,0:T(8,128)S(1)}, f32[224,1536]{1,0:T(8,128)S(1)}, bf16[2,3,8,768]{...) custom-call(bf16[2,3,8,768]{3,2,1,0:T(8,128)(2,1)S(1)} %collective-permute-done.two_ref, ...), custom_call_target="tpu_custom_call" | custom-call | tf_op jit(solution)/shard_map/pallas_call | solution.py:50
  13.0 0.0 collective-permute-done.3.theirs_ref
  13.0 1.2 %collective-permute-start.4 = (bf16[8,768]{1,0:T(8,128)(2,1)S(1)}, bf16[8,768]{1,0:T(8,128)(2,1)S(1)}, u32[]{:S(2)}, u32[]{:S(2)}) collective-permute-start(bf16[8,768]{1,0:T(8,128)(2,1)S(1)} %shard_map.90.mine_ref), channel_id=1, source_target_pairs={{0,20},{4,16},{8,28},{12,24},{16,4},{20,0},{24,12},{28,8},{1,21},{... | collective-permute-start | bytes 36872 | tf_op jit(solution)/shard_map/ppermute | solution.py:519
  14.2 1.3 %collective-permute-start.5 = (f32[2,768]{1,0:T(2,128)S(1)}, f32[2,768]{1,0:T(2,128)S(1)}, u32[]{:S(2)}, u32[]{:S(2)}) collective-permute-start(f32[2,768]{1,0:T(2,128)S(1)} %get-tuple-element.59.refs_3_), channel_id=1, source_target_pairs={{0,3},{1,2},{2,1},{3,0},{4,7},{5,6},{6,5},{7,4},{8,11},{9,10},{10,... | collective-permute-start | bytes 18440 | tf_op jit(solution)/shard_map/ppermute | solution.py:519
  15.6 0.1 collective-permute-start.6
  15.7 2.9 %collective-permute-start.7 = (f32[2,768]{1,0:T(2,128)S(1)}, f32[2,768]{1,0:T(2,128)S(1)}, u32[]{:S(2)}, u32[]{:S(2)}) collective-permute-start(f32[2,768]{1,0:T(2,128)S(1)} %get-tuple-element.59.refs_3_), channel_id=1, source_target_pairs={{0,1},{1,0},{2,3},{3,2},{4,5},{5,4},{6,7},{7,6},{8,9},{9,8},{10,11... | collective-permute-start | bytes 18440 | tf_op jit(solution)/shard_map/ppermute | solution.py:519
  18.6 2.5 %shard_map.92 = (f32[224,1536]{1,0:T(8,128)S(1)}, f32[2,10,8,768]{3,2,1,0:T(8,128)S(1)}, f32[2,10,8,768]{3,2,1,0:T(8,128)S(1)}, f32[2,9,8,768]{3,2,1,0:T(8,128)S...) custom-call(f32[224,1536]{1,0:T(8,128)S(1)} %get-tuple-element.48.hid_ref, ...), custom_call_target="tpu_custom_call" | custom-call | tf_op jit(solution)/shard_map/pallas_call | solution.py:50
  21.1 0.0 collective-permute-done.4.theirs_ref
  21.1 0.1 shard_map.91.text_ref
  21.3 0.0 collective-permute-done.5.refs_0_
  21.3 0.0 collective-permute-done.6.refs_1_
  21.3 0.0 collective-permute-done.7.refs_2_
  21.3 2.7 %shard_map.93 = (f32[224,768]{1,0:T(8,128)S(1)}, f32[112,768]{1,0:T(8,128)S(1)}, bf16[176,128]{1,0:T(8,128)(2,1)S(1)}) custom-call(f32[16,768]{1,0:T(8,128)S(1)} %shard_map.91.text_ref, f32[2,16,128]{2,1,0:T(8,128)S(1)} %get-tuple-element.47.labels_ref, f32[224,1536]{1,0:T(8,128)S(1)} %get-tuple-element.51.slope_ref, ...), custom_call_target="tpu_custom_call" | custom-call | tf_op jit(solution)/shard_map/pallas_call | solution.py:50
  24.0 0.0 collective-permute-start.8
  24.1 1.1 %shard_map.94.own_ref = f32[160,128]{1,0:T(8,128)S(1)} custom-call(f32[224,768]{1,0:T(8,128)S(1)} %get-tuple-element.60.grad_ref, f32[112,768]{1,0:T(8,128)S(1)} %get-tuple-element.61.pair_ref, f32[2,10,8,768]{3,2,1,0:T(8,128)S(1)} %get-tuple-element.56.odd_ref, f32[2,10,8,768]{3,2,1,0:T(8,128)S(1)} %get-tuple-element.57.even_gap_ref, ...), custom_call_target="tpu_custom_call" | custom-call | tf_op jit(solution)/shard_map/pallas_call | solution.py:50
  25.2 0.1 collective-permute-done.8.other_ref
  25.3 0.6 %collective-permute-start.10 = (bf16[192,128]{1,0:T(8,128)(2,1)S(1)}, bf16[192,128]{1,0:T(8,128)(2,1)S(1)}, u32[]{:S(2)}, u32[]{:S(2)}) collective-permute-start(bf16[192,128]{1,0:T(8,128)(2,1)S(1)} %shard_map.95.refs_0_), channel_id=1, source_target_pairs={{0,24},{4,28},{8,16},{12,20},{16,8},{20,12},{24,0},{28,4},{1,25},{... | collective-permute-start | bytes 147464 | tf_op jit(solution)/shard_map/ppermute | solution.py:519
  25.9 1.2 %collective-permute-start.11 = (bf16[192,128]{1,0:T(8,128)(2,1)S(1)}, bf16[192,128]{1,0:T(8,128)(2,1)S(1)}, u32[]{:S(2)}, u32[]{:S(2)}) collective-permute-start(bf16[192,128]{1,0:T(8,128)(2,1)S(1)} %shard_map.95.refs_0_), channel_id=1, source_target_pairs={{0,20},{4,16},{8,28},{12,24},{16,4},{20,0},{24,12},{28,8},{1,21},{... | collective-permute-start | bytes 147464 | tf_op jit(solution)/shard_map/ppermute | solution.py:519
  27.1 1.5 %collective-permute-start.9 = (bf16[192,128]{1,0:T(8,128)(2,1)S(1)}, bf16[192,128]{1,0:T(8,128)(2,1)S(1)}, u32[]{:S(2)}, u32[]{:S(2)}) collective-permute-start(bf16[192,128]{1,0:T(8,128)(2,1)S(1)} %shard_map.95.refs_0_), channel_id=1, source_target_pairs={{0,12},{4,8},{8,4},{12,0},{16,28},{20,24},{24,20},{28,16},{1,13},{... | collective-permute-start | bytes 147464 | tf_op jit(solution)/shard_map/ppermute | solution.py:519
  28.6 2.1 %collective-permute-done.10.refs_2_ = bf16[192,128]{1,0:T(8,128)(2,1)S(1)} collective-permute-done((bf16[192,128]{1,0:T(8,128)(2,1)S(1)}, bf16[192,128]{1,0:T(8,128)(2,1)S(1)}, u32[]{:S(2)}, u32[]{:S(2)}) %collective-permute-start.10) | collective-permute-done | bytes 49184 | tf_op jit(solution)/shard_map/ppermute | solution.py:519
  30.7 0.0 collective-permute-done.11.refs_3_
  30.8 0.0 collective-permute-done.9.refs_1_
  30.8 1.0 %collective-permute-start.12 = (bf16[160,128]{1,0:T(8,128)(2,1)S(1)}, bf16[160,128]{1,0:T(8,128)(2,1)S(1)}, u32[]{:S(2)}, u32[]{:S(2)}) collective-permute-start(bf16[160,128]{1,0:T(8,128)(2,1)S(1)} %get-tuple-element.66.refs_1_), channel_id=1, source_target_pairs={{0,2},{1,3},{2,0},{3,1},{4,6},{5,7},{6,4},{7,5},{8,10},{9,11},{10,... | collective-permute-start | bytes 122888 | tf_op jit(solution)/shard_map/ppermute | solution.py:515
  31.8 1.1 %collective-permute-start.13 = (bf16[160,128]{1,0:T(8,128)(2,1)S(1)}, bf16[160,128]{1,0:T(8,128)(2,1)S(1)}, u32[]{:S(2)}, u32[]{:S(2)}) collective-permute-start(bf16[160,128]{1,0:T(8,128)(2,1)S(1)} %get-tuple-element.66.refs_1_), channel_id=1, source_target_pairs={{0,1},{1,2},{2,3},{3,0},{4,5},{5,6},{6,7},{7,4},{8,9},{9,10},{10,1... | collective-permute-start | bytes 122888 | tf_op jit(solution)/shard_map/ppermute | solution.py:515
  32.9 2.8 %collective-permute-start.14 = (bf16[160,128]{1,0:T(8,128)(2,1)S(1)}, bf16[160,128]{1,0:T(8,128)(2,1)S(1)}, u32[]{:S(2)}, u32[]{:S(2)}) collective-permute-start(bf16[160,128]{1,0:T(8,128)(2,1)S(1)} %get-tuple-element.66.refs_1_), channel_id=1, source_target_pairs={{0,3},{1,0},{2,1},{3,2},{4,7},{5,4},{6,5},{7,6},{8,11},{9,8},{10,9... | collective-permute-start | bytes 122888 | tf_op jit(solution)/shard_map/ppermute | solution.py:515
  35.6 1.4 %collective-permute-done.12.refs_0_ = bf16[160,128]{1,0:T(8,128)(2,1)S(1)} collective-permute-done((bf16[160,128]{1,0:T(8,128)(2,1)S(1)}, bf16[160,128]{1,0:T(8,128)(2,1)S(1)}, u32[]{:S(2)}, u32[]{:S(2)}) %collective-permute-start.12) | collective-permute-done | bytes 40992 | tf_op jit(solution)/shard_map/ppermute | solution.py:515
  37.0 0.7 %collective-permute-done.13.refs_2_ = bf16[160,128]{1,0:T(8,128)(2,1)S(1)} collective-permute-done((bf16[160,128]{1,0:T(8,128)(2,1)S(1)}, bf16[160,128]{1,0:T(8,128)(2,1)S(1)}, u32[]{:S(2)}, u32[]{:S(2)}) %collective-permute-start.13) | collective-permute-done | bytes 40992 | tf_op jit(solution)/shard_map/ppermute | solution.py:515
  37.7 0.0 collective-permute-done.14.refs_3_
  37.7 0.1 collective-permute-start.15
  37.8 0.8 %shard_map.97 = (f32[2,768]{1,0:T(2,128)}, f32[1,1]{1,0:T(1,128)}) custom-call(bf16[128,128]{1,0:T(8,128)(2,1)S(1)} %get-tuple-element.63.rows_ref, bf16[2,768]{1,0:T(2,128)(2,1)S(1)} %get-tuple-element.39.caps_ref), custom_call_target="tpu_custom_call" | custom-call | tf_op jit(solution)/shard_map/pallas_call | solution.py:50
  38.6 0.4 collective-permute-done.15.other_ref
  39.0 0.7 %shard_map.99 = f32[7,7,768]{2,1,0:T(8,128)} custom-call(bf16[160,128]{1,0:T(8,128)(2,1)S(1)} %shard_map.98.own_ref, bf16[160,128]{1,0:T(8,128)(2,1)S(1)} %collective-permute-done.15.other_ref), custom_call_target="tpu_custom_call" | custom-call | tf_op jit(solution)/shard_map/pallas_call | solution.py:50
  (5 shorter events, 0.1 us)
Async XLA Ops:
  0.6 10.6 %copy-start = (bf16[768,1536]{1,0:T(8,128)(2,1)S(1)}, bf16[768,1536]{1,0:T(8,128)(2,1)}, u32[]{:S(2)}) copy-start(bf16[768,1536]{1,0:T(8,128)(2,1)} %win_ref.3) | copy-start | bytes 7077892
  2.0 9.2 %collective-permute-start = (bf16[2,3,8,768]{3,2,1,0:T(8,128)(2,1)S(1)}, bf16[2,3,8,768]{3,2,1,0:T(8,128)(2,1)S(1)}, u32[]{:S(2)}, u32[]{:S(2)}) collective-permute-start(bf16[2,3,8,768]{3,2,1,0:T(8,128)(2,1)S(1)} %get-tuple-element.35), channel_id=1, source_target_pairs={{0,4},{1,2},{2,1},{3,7},{4,0},{5,6},{6,5},{7,3},{8,12},{9,10},{10,... | collective-permute-start | bytes 221192 | tf_op jit(solution)/shard_map/ppermute | solution.py:561
  2.5 8.7 %collective-permute-start.1 = (bf16[2,3,8,768]{3,2,1,0:T(8,128)(2,1)S(1)}, bf16[2,3,8,768]{3,2,1,0:T(8,128)(2,1)S(1)}, u32[]{:S(2)}, u32[]{:S(2)}) collective-permute-start(bf16[2,3,8,768]{3,2,1,0:T(8,128)(2,1)S(1)} %get-tuple-element.36), channel_id=1, source_target_pairs={{0,1},{1,0},{2,3},{3,2},{4,5},{5,4},{6,7},{7,6},{8,9},{9,8},{10,11... | collective-permute-start | bytes 221192 | tf_op jit(solution)/shard_map/ppermute | solution.py:561
  6.6 1.7 %collective-permute-start.2 = (bf16[2,768]{1,0:T(2,128)(2,1)S(1)}, bf16[2,768]{1,0:T(2,128)(2,1)S(1)}, u32[]{:S(2)}, u32[]{:S(2)}) collective-permute-start(bf16[2,768]{1,0:T(2,128)(2,1)S(1)} %get-tuple-element.39.caps_ref), channel_id=1, source_target_pairs={{0,4},{4,0},{8,12},{12,8},{16,20},{20,16},{24,28},{28,24},{1,5},{5... | collective-permute-start | bytes 9224 | tf_op jit(solution)/shard_map/ppermute | solution.py:519
  8.4 4.6 %collective-permute-start.3 = (bf16[4,768]{1,0:T(4,128)(2,1)S(1)}, bf16[4,768]{1,0:T(4,128)(2,1)S(1)}, u32[]{:S(2)}, u32[]{:S(2)}) collective-permute-start(bf16[4,768]{1,0:T(4,128)(2,1)S(1)} %shard_map.88.caps_ref), channel_id=1, source_target_pairs={{0,12},{4,8},{8,4},{12,0},{16,28},{20,24},{24,20},{28,16},{1,13},{... | collective-permute-start | bytes 18440 | tf_op jit(solution)/shard_map/ppermute | solution.py:519
  13.0 8.1 %collective-permute-start.4 = (bf16[8,768]{1,0:T(8,128)(2,1)S(1)}, bf16[8,768]{1,0:T(8,128)(2,1)S(1)}, u32[]{:S(2)}, u32[]{:S(2)}) collective-permute-start(bf16[8,768]{1,0:T(8,128)(2,1)S(1)} %shard_map.90.mine_ref), channel_id=1, source_target_pairs={{0,20},{4,16},{8,28},{12,24},{16,4},{20,0},{24,12},{28,8},{1,21},{... | collective-permute-start | bytes 36872 | tf_op jit(solution)/shard_map/ppermute | solution.py:519
  14.2 7.0 %collective-permute-start.5 = (f32[2,768]{1,0:T(2,128)S(1)}, f32[2,768]{1,0:T(2,128)S(1)}, u32[]{:S(2)}, u32[]{:S(2)}) collective-permute-start(f32[2,768]{1,0:T(2,128)S(1)} %get-tuple-element.59.refs_3_), channel_id=1, source_target_pairs={{0,3},{1,2},{2,1},{3,0},{4,7},{5,6},{6,5},{7,4},{8,11},{9,10},{10,... | collective-permute-start | bytes 18440 | tf_op jit(solution)/shard_map/ppermute | solution.py:519
  15.6 5.7 %collective-permute-start.6 = (f32[2,768]{1,0:T(2,128)S(1)}, f32[2,768]{1,0:T(2,128)S(1)}, u32[]{:S(2)}, u32[]{:S(2)}) collective-permute-start(f32[2,768]{1,0:T(2,128)S(1)} %get-tuple-element.59.refs_3_), channel_id=1, source_target_pairs={{0,2},{1,3},{2,0},{3,1},{4,6},{5,7},{6,4},{7,5},{8,10},{9,11},{10,... | collective-permute-start | bytes 18440 | tf_op jit(solution)/shard_map/ppermute | solution.py:519
  15.7 5.6 %collective-permute-start.7 = (f32[2,768]{1,0:T(2,128)S(1)}, f32[2,768]{1,0:T(2,128)S(1)}, u32[]{:S(2)}, u32[]{:S(2)}) collective-permute-start(f32[2,768]{1,0:T(2,128)S(1)} %get-tuple-element.59.refs_3_), channel_id=1, source_target_pairs={{0,1},{1,0},{2,3},{3,2},{4,5},{5,4},{6,7},{7,6},{8,9},{9,8},{10,11... | collective-permute-start | bytes 18440 | tf_op jit(solution)/shard_map/ppermute | solution.py:519
  24.0 1.2 %collective-permute-start.8 = (bf16[176,128]{1,0:T(8,128)(2,1)S(1)}, bf16[176,128]{1,0:T(8,128)(2,1)S(1)}, u32[]{:S(2)}, u32[]{:S(2)}) collective-permute-start(bf16[176,128]{1,0:T(8,128)(2,1)S(1)} %get-tuple-element.62.pay_ref), channel_id=1, source_target_pairs={{0,4},{4,0},{8,12},{12,8},{16,20},{20,16},{24,28},{28,24},{1,5},{5... | collective-permute-start | bytes 135176 | tf_op jit(solution)/shard_map/ppermute | solution.py:519
  25.3 5.5 %collective-permute-start.10 = (bf16[192,128]{1,0:T(8,128)(2,1)S(1)}, bf16[192,128]{1,0:T(8,128)(2,1)S(1)}, u32[]{:S(2)}, u32[]{:S(2)}) collective-permute-start(bf16[192,128]{1,0:T(8,128)(2,1)S(1)} %shard_map.95.refs_0_), channel_id=1, source_target_pairs={{0,24},{4,28},{8,16},{12,20},{16,8},{20,12},{24,0},{28,4},{1,25},{... | collective-permute-start | bytes 147464 | tf_op jit(solution)/shard_map/ppermute | solution.py:519
  25.9 4.9 %collective-permute-start.11 = (bf16[192,128]{1,0:T(8,128)(2,1)S(1)}, bf16[192,128]{1,0:T(8,128)(2,1)S(1)}, u32[]{:S(2)}, u32[]{:S(2)}) collective-permute-start(bf16[192,128]{1,0:T(8,128)(2,1)S(1)} %shard_map.95.refs_0_), channel_id=1, source_target_pairs={{0,20},{4,16},{8,28},{12,24},{16,4},{20,0},{24,12},{28,8},{1,21},{... | collective-permute-start | bytes 147464 | tf_op jit(solution)/shard_map/ppermute | solution.py:519
  27.1 3.7 %collective-permute-start.9 = (bf16[192,128]{1,0:T(8,128)(2,1)S(1)}, bf16[192,128]{1,0:T(8,128)(2,1)S(1)}, u32[]{:S(2)}, u32[]{:S(2)}) collective-permute-start(bf16[192,128]{1,0:T(8,128)(2,1)S(1)} %shard_map.95.refs_0_), channel_id=1, source_target_pairs={{0,12},{4,8},{8,4},{12,0},{16,28},{20,24},{24,20},{28,16},{1,13},{... | collective-permute-start | bytes 147464 | tf_op jit(solution)/shard_map/ppermute | solution.py:519
  30.8 6.2 %collective-permute-start.12 = (bf16[160,128]{1,0:T(8,128)(2,1)S(1)}, bf16[160,128]{1,0:T(8,128)(2,1)S(1)}, u32[]{:S(2)}, u32[]{:S(2)}) collective-permute-start(bf16[160,128]{1,0:T(8,128)(2,1)S(1)} %get-tuple-element.66.refs_1_), channel_id=1, source_target_pairs={{0,2},{1,3},{2,0},{3,1},{4,6},{5,7},{6,4},{7,5},{8,10},{9,11},{10,... | collective-permute-start | bytes 122888 | tf_op jit(solution)/shard_map/ppermute | solution.py:515
  31.8 5.9 %collective-permute-start.13 = (bf16[160,128]{1,0:T(8,128)(2,1)S(1)}, bf16[160,128]{1,0:T(8,128)(2,1)S(1)}, u32[]{:S(2)}, u32[]{:S(2)}) collective-permute-start(bf16[160,128]{1,0:T(8,128)(2,1)S(1)} %get-tuple-element.66.refs_1_), channel_id=1, source_target_pairs={{0,1},{1,2},{2,3},{3,0},{4,5},{5,6},{6,7},{7,4},{8,9},{9,10},{10,1... | collective-permute-start | bytes 122888 | tf_op jit(solution)/shard_map/ppermute | solution.py:515
  32.9 4.8 %collective-permute-start.14 = (bf16[160,128]{1,0:T(8,128)(2,1)S(1)}, bf16[160,128]{1,0:T(8,128)(2,1)S(1)}, u32[]{:S(2)}, u32[]{:S(2)}) collective-permute-start(bf16[160,128]{1,0:T(8,128)(2,1)S(1)} %get-tuple-element.66.refs_1_), channel_id=1, source_target_pairs={{0,3},{1,0},{2,1},{3,2},{4,7},{5,4},{6,5},{7,6},{8,11},{9,8},{10,9... | collective-permute-start | bytes 122888 | tf_op jit(solution)/shard_map/ppermute | solution.py:515
  37.7 1.3 %collective-permute-start.15 = (bf16[160,128]{1,0:T(8,128)(2,1)S(1)}, bf16[160,128]{1,0:T(8,128)(2,1)S(1)}, u32[]{:S(2)}, u32[]{:S(2)}) collective-permute-start(bf16[160,128]{1,0:T(8,128)(2,1)S(1)} %shard_map.98.own_ref), channel_id=1, source_target_pairs={{0,4},{4,0},{8,12},{12,8},{16,20},{20,16},{24,28},{28,24},{1,5},{5... | collective-permute-start | bytes 122888 | tf_op jit(solution)/shard_map/ppermute | solution.py:519
